TPU v7x, 32 devices: a whole 2x2x4 slice. The times are simulated.
32 devices in a mesh: section: 2 (over y), seq: 16 (over z, x, core).
Axes of the slice: x: 2, y: 2, z: 4, core: 2. Of those that a mesh axis runs over, the one named last changes fastest.
Arguments:
- resident_microbatches: bfloat16 [2, 2048, 1024], P('section', 'seq'), may hold values from -64 to 64
- arriving_microbatch: bfloat16 [2048, 1024], P('seq'), may hold values from -64 to 64
- prenormal_scaling: float32 [2, 1024], P('section'), may hold values from 0.1 to 1.9
- attention_triple_matrix: bfloat16 [2, 1024, 3072], P('section', 'seq'), may hold values from -0.1875 to 0.1875
- exit_projection_matrix: bfloat16 [2, 1024, 1024], P('section'), may hold values from -0.1875 to 0.1875
- mirrored_lookup_tile: int32 [16, 4], replicated, may hold values from 0 to 1
Outputs:
- tick_out: bfloat16 [2, 2, 2048, 1024], P(None, 'section', 'seq')
All inputs are finite; a program needn't handle non-finite values.
Results may differ from a plain program's by a relative error of at most 0.004.
Values may be sent and summed in bfloat16 or wider, within the bound.
No kernel may reach another device: no remote copies, remote signals or barrier semaphores. Data moves between devices by JAX's collectives and lax.ppermute only.
A program may use at most 64 MiB of HBM per device.

v0:
```python
import jax
import jax.numpy as jnp
from jax import lax
from jax.sharding import PartitionSpec as P

HEADS = 8
HEAD = 128
BLOCK = 64
LEVELS = 4


epsilon = 1e-06


def swapped(x, axis, stride):
    return lax.ppermute(x, axis, [(i, i ^ 1 << stride) for i in range(lax.axis_size(axis))])


def from_behind(block, axis, distance):
    devices = range(lax.axis_size(axis))
    route = [(i - distance, i) for i in devices if i - distance in devices]
    return lax.ppermute(block, axis, route)


def head_norm(projected, row_count):
    shaped = projected.reshape(row_count, HEADS, HEAD)
    mean_square = jnp.mean(shaped * shaped, axis=-1, keepdims=True)
    return (shaped * lax.rsqrt(mean_square + epsilon)).astype(jnp.bfloat16)


def transform_through_tier(
    hidden_in, gain_row, weights, out_weights, mirrored_lookup_tile, compute_unit
):
    row_count = hidden_in.shape[0]
    blocks = row_count // BLOCK
    inner_width = HEADS * HEAD
    widened = hidden_in.astype(jnp.float32)
    mean_square = jnp.mean(widened * widened, axis=-1, keepdims=True)
    normed = (widened * lax.rsqrt(mean_square + epsilon) * gain_row).astype(jnp.bfloat16)
    projected = jnp.dot(normed, weights, preferred_element_type=jnp.float32)
    queries = head_norm(projected[:, :inner_width], row_count)
    key_rows = head_norm(projected[:, inner_width : 2 * inner_width], row_count).reshape(
        row_count, inner_width
    )
    values = projected[:, 2 * inner_width :].astype(jnp.bfloat16)
    key_value = jnp.stack([key_rows, values])
    remote = []
    for bit_level in range(LEVELS):
        partner = jnp.bitwise_xor(compute_unit, jnp.int32(1 << bit_level))
        requested = mirrored_lookup_tile[partner, bit_level]
        chosen_block = lax.dynamic_slice_in_dim(key_value, requested * BLOCK, BLOCK, 1)
        remote.append(swapped(chosen_block, "seq", bit_level))
    remote = jnp.concatenate(remote, axis=1)
    far_keys = jnp.broadcast_to(
        remote[0].reshape(1, LEVELS * BLOCK, HEADS, HEAD), (blocks, LEVELS * BLOCK, HEADS, HEAD)
    )
    far_values = jnp.broadcast_to(
        remote[1].reshape(1, LEVELS * BLOCK, HEADS, HEAD), (blocks, LEVELS * BLOCK, HEADS, HEAD)
    )
    query_blocks = queries.reshape(blocks, BLOCK, HEADS, HEAD)
    all_keys = jnp.concatenate([key_rows.reshape(blocks, BLOCK, HEADS, HEAD), far_keys], axis=1)
    all_values = jnp.concatenate([values.reshape(blocks, BLOCK, HEADS, HEAD), far_values], axis=1)
    score_scale = HEAD ** (-0.5)
    scores = (
        jnp.einsum("cqhd,ckhd->chqk", query_blocks, all_keys, preferred_element_type=jnp.float32)
        * score_scale
    )
    exps = jnp.exp(scores)
    weights_soft = (exps / jnp.sum(exps, axis=-1, keepdims=True)).astype(jnp.bfloat16)
    mixed_heads = jnp.einsum(
        "chqk,ckhd->cqhd", weights_soft, all_values, preferred_element_type=jnp.float32
    )
    attended = mixed_heads.astype(jnp.bfloat16).reshape(row_count, inner_width)
    return (widened + jnp.dot(attended, out_weights, preferred_element_type=jnp.float32)).astype(
        jnp.bfloat16
    )


def per_device(
    resident_microbatches,
    arriving_microbatch,
    prenormal_scaling,
    attention_triple_matrix,
    exit_projection_matrix,
    mirrored_lookup_tile,
):
    layer_parameters = lax.all_gather(attention_triple_matrix[0], "seq", axis=0, tiled=True)
    compute_unit = lax.axis_index("seq")
    section_index = lax.axis_index("section")
    starting_result = transform_through_tier(
        resident_microbatches[0],
        prenormal_scaling[0],
        layer_parameters,
        exit_projection_matrix[0],
        mirrored_lookup_tile,
        compute_unit,
    )
    moved = from_behind(starting_result, "section", 1)
    second_in = jnp.where(section_index == 0, arriving_microbatch, moved)
    second_out = transform_through_tier(
        second_in,
        prenormal_scaling[0],
        layer_parameters,
        exit_projection_matrix[0],
        mirrored_lookup_tile,
        compute_unit,
    )
    return jnp.stack([starting_result, second_out])[:, None]


def solution(mesh):
    placed = (
        P("section", "seq", None),
        P("seq", None),
        P("section", None),
        P("section", "seq", None),
        P("section", None, None),
        P(),
    )
    return jax.shard_map(
        per_device,
        mesh=mesh,
        in_specs=placed,
        out_specs=P(None, "section", "seq", None),
        check_vma=False,
    )
```

profile of v0, /device:TPU:0, one launch (start us, length us, event | category | flops | bytes accessed | tf_op | source)
XLA Modules:
  0.0 165.5 jit_solution(7764508550182320470)
XLA Ops:
  7.3 1.5 constant_dynamic-slice_fusion.1
  11.4 1.1 fusion.54
  12.5 61.7 %all-gather.3.cloned.1.call-done = bf16[1,1024,3072]{2,1,0:T(8,128)(2,1)} async-done(((bf16[1,64,3072]{2,1,0:T(8,128)(2,1)}), bf16[1,1024,3072]{2,1,0:T(8,128)(2,1)}) %all-gather.3.cloned.1.call-update) | async-done | bytes 6291472 | tf_op jit(solution)/shard_map/all_gather | solution.py:87
  74.2 3.9 %fusion.2 = f32[128,3072]{1,0:T(8,128)S(1)} fusion(bf16[1,1024,3072]{2,1,0:T(8,128)(2,1)} %all-gather.3.cloned.1.call-done, bf16[1,128,1024]{2,1,0:T(8,128)(2,1)} %param.6, f32[1024]{0:T(1024)} %bitcast.157, f32[128]{0:T(128)S(1)} %add_rsqrt_fusion.5), kind=kOutput, calls=%fused_computation.2 | convolution fusion | flops 805830656 | bytes 8131072 | tf_op jit(solution)/shard_map/dot_general | solution.py:40
  78.2 1.2 copy-done.2
  80.0 1.1 fusion.88
  81.3 1.4 multiply_bitcast_fusion.2
  82.8 1.0 fusion.73
  84.6 1.5 collective-permute-start.2
  88.4 1.1 collective-permute-start.3
  89.5 1.0 constant_dynamic-update-slice_fusion.3
  90.5 2.3 %collective-permute-done.1 = bf16[2,64,1024]{2,1,0:T(8,128)(2,1)} collective-permute-done((bf16[2,64,1024]{2,1,0:T(8,128)(2,1)}, bf16[2,64,1024]{2,1,0:T(8,128)(2,1)}, u32[]{:S(2)}, u32[]{:S(2)}) %collective-permute-start.1) | collective-permute-done | bytes 262176 | tf_op jit(solution)/shard_map/ppermute | solution.py:16
  93.8 2.1 %collective-permute-done.2 = bf16[2,64,1024]{2,1,0:T(8,128)(2,1)} collective-permute-done((bf16[2,64,1024]{2,1,0:T(8,128)(2,1)}, bf16[2,64,1024]{2,1,0:T(8,128)(2,1)}, u32[]{:S(2)}, u32[]{:S(2)}) %collective-permute-start.2) | collective-permute-done | bytes 262176 | tf_op jit(solution)/shard_map/ppermute | solution.py:16
  96.9 6.0 %collective-permute-done.3 = bf16[2,64,1024]{2,1,0:T(8,128)(2,1)S(1)} collective-permute-done((bf16[2,64,1024]{2,1,0:T(8,128)(2,1)S(1)}, bf16[2,64,1024]{2,1,0:T(8,128)(2,1)S(1)}, u32[]{:S(2)}, u32[]{:S(2)}) %collective-permute-start.3) | collective-permute-done | bytes 262176 | tf_op jit(solution)/shard_map/ppermute | solution.py:16
  104.2 1.8 %multiply_exponential_fusion.1 = f32[2,8,64,320]{3,2,1,0:T(8,128)} fusion(bf16[2,256,8,128]{3,1,2,0:T(8,128)(2,1)S(1)} %broadcast_in_dim.42, bf16[2,64,8,128]{3,1,2,0:T(8,128)(2,1)S(1)} %copy-done.5, f32[2,64,8,128]{3,2,1,0:T(8,128)S(1)} %bitcast.148, f32[2,64,8]{1,2,0:T(8,128)S(1)} %copy.63), kind=kOutput, calls=%fused_computation.11 | convolution fusion | flops 87097344 | bytes 3149824 | tf_op jit(solution)/shard_map/cqhd,ckhd->chqk/dot_general | solution.py:65
  106.3 3.3 %fusion.43 = bf16[2,64,8,128]{3,1,2,0:T(8,128)(2,1)} fusion(bf16[2,256,8,128]{3,1,2,0:T(8,128)(2,1)S(1)} %broadcast_in_dim.19, bf16[2,64,8,128]{3,1,2,0:T(8,128)(2,1)} %copy.61, f32[2,8,64,320]{3,2,1,0:T(8,128)} %multiply_exponential_fusion.1), kind=kOutput, calls=%fused_computation.33 | convolution fusion | flops 87295296 | bytes 2883584 | tf_op jit(solution)/shard_map/chqk,ckhd->cqhd/dot_general | solution.py:70
  109.5 1.1 copy.68
  111.1 3.4 %collective-permute-start.4 = (bf16[128,1024]{1,0:T(8,128)(2,1)S(1)}, bf16[128,1024]{1,0:T(8,128)(2,1)S(1)}, u32[]{:S(2)}, u32[]{:S(2)}) collective-permute-start(bf16[128,1024]{1,0:T(8,128)(2,1)S(1)} %fusion.37), channel_id=1, source_target_pairs={{0,16},{1,17},{2,18},{3,19},{4,20},{5,21},{6,22},{7,23},{8,24},{9,... | collective-permute-start | bytes 786440 | tf_op jit(solution)/shard_map/ppermute | solution.py:22
  114.6 4.5 %collective-permute-done.4 = bf16[128,1024]{1,0:T(8,128)(2,1)S(1)} collective-permute-done((bf16[128,1024]{1,0:T(8,128)(2,1)S(1)}, bf16[128,1024]{1,0:T(8,128)(2,1)S(1)}, u32[]{:S(2)}, u32[]{:S(2)}) %collective-permute-start.4) | collective-permute-done | bytes 262176 | tf_op jit(solution)/shard_map/ppermute | solution.py:22
  119.3 3.8 %fusion = f32[128,3072]{1,0:T(8,128)S(1)} fusion(bf16[1,1024,3072]{2,1,0:T(8,128)(2,1)} %all-gather.3.cloned.1.call-done, bf16[128,1024]{1,0:T(8,128)(2,1)S(1)} %get-tuple-element.6, f32[128]{0:T(128)S(1)} %add_rsqrt_fusion.4, f32[1024]{0:T(1024)S(1)} %bitcast.158), kind=kOutput, calls=%fused_computation | convolution fusion | flops 805830656 | bytes 8131072 | tf_op jit(solution)/shard_map/dot_general | solution.py:40
  123.1 1.1 copy-done.1
  124.9 1.8 %fusion.90 = (bf16[16,8,8,128]{3,1,2,0:T(8,128)(2,1)}, bf16[1,128,1024]{2,1,0:T(8,128)(2,1)S(1)}) fusion(f32[128,3072]{1,0:T(8,128)} %copy-done.1), kind=kLoop, calls=%fused_computation.114 | loop fusion | bytes 786432
  126.9 1.4 multiply_bitcast_fusion
  128.4 1.0 fusion.69
  129.4 1.5 collective-permute-start.6
  132.2 1.0 copy.96
  134.2 2.5 %collective-permute-start.8 = (bf16[2,64,1024]{2,1,0:T(8,128)(2,1)S(1)}, bf16[2,64,1024]{2,1,0:T(8,128)(2,1)S(1)}, u32[]{:S(2)}, u32[]{:S(2)}) collective-permute-start(bf16[2,64,1024]{2,1,0:T(8,128)(2,1)S(1)} %copy-done.9), channel_id=1, source_target_pairs={{0,8},{1,9},{2,10},{3,11},{4,12},{5,13},{6,14},{7,15},{8,0},{9,1},... | collective-permute-start | bytes 786440 | tf_op jit(solution)/shard_map/ppermute | solution.py:16
  139.4 2.0 %collective-permute-done.7 = bf16[2,64,1024]{2,1,0:T(8,128)(2,1)} collective-permute-done((bf16[2,64,1024]{2,1,0:T(8,128)(2,1)}, bf16[2,64,1024]{2,1,0:T(8,128)(2,1)}, u32[]{:S(2)}, u32[]{:S(2)}) %collective-permute-start.7) | collective-permute-done | bytes 262176 | tf_op jit(solution)/shard_map/ppermute | solution.py:16
  142.4 6.8 %collective-permute-done.8 = bf16[2,64,1024]{2,1,0:T(8,128)(2,1)S(1)} collective-permute-done((bf16[2,64,1024]{2,1,0:T(8,128)(2,1)S(1)}, bf16[2,64,1024]{2,1,0:T(8,128)(2,1)S(1)}, u32[]{:S(2)}, u32[]{:S(2)}) %collective-permute-start.8) | collective-permute-done | bytes 262176 | tf_op jit(solution)/shard_map/ppermute | solution.py:16
  150.6 1.8 %multiply_exponential_fusion = f32[2,8,64,320]{3,2,1,0:T(8,128)} fusion(bf16[2,256,8,128]{3,1,2,0:T(8,128)(2,1)S(1)} %broadcast_in_dim.46, bf16[2,64,8,128]{3,1,2,0:T(8,128)(2,1)S(1)} %copy-done.4, f32[2,64,8,128]{3,2,1,0:T(8,128)S(1)} %bitcast.149, f32[2,64,8]{1,2,0:T(8,128)S(1)} %copy.74), kind=kOutput, calls=%fused_computation.9 | convolution fusion | flops 87097344 | bytes 3149824 | tf_op jit(solution)/shard_map/cqhd,ckhd->chqk/dot_general | solution.py:65
  152.5 3.2 %fusion.46 = bf16[2,64,8,128]{3,1,2,0:T(8,128)(2,1)} fusion(bf16[2,256,8,128]{3,1,2,0:T(8,128)(2,1)S(1)} %broadcast_in_dim.44, bf16[2,64,8,128]{3,1,2,0:T(8,128)(2,1)} %copy.72, f32[2,8,64,320]{3,2,1,0:T(8,128)} %multiply_exponential_fusion), kind=kOutput, calls=%fused_computation.34 | convolution fusion | flops 87295296 | bytes 2883584 | tf_op jit(solution)/shard_map/chqk,ckhd->cqhd/dot_general | solution.py:70
  155.8 1.1 copy.79
  (97 shorter events, 18.8 us)
Async XLA Ops:
  6.5 104.1 %copy-start = (bf16[1,1024,1024]{2,1,0:T(8,128)(2,1)S(1)}, bf16[1,1024,1024]{2,1,0:T(8,128)(2,1)}, u32[]{:S(2)}) copy-start(bf16[1,1024,1024]{2,1,0:T(8,128)(2,1)} %param.10) | copy-start | bytes 6291460
  6.5 67.7 %all-gather.3.cloned.1.call-start = ((), (), s32[]{:S(2)}) async-start(), calls=%async_computation | async-start | bytes 6684672 | tf_op jit(solution)/shard_map/all_gather | solution.py:87
  78.2 1.2 copy-start.2
  83.8 5.7 %collective-permute-start = (bf16[2,64,1024]{2,1,0:T(8,128)(2,1)}, bf16[2,64,1024]{2,1,0:T(8,128)(2,1)}, u32[]{:S(2)}, u32[]{:S(2)}) collective-permute-start(bf16[2,64,1024]{2,1,0:T(8,128)(2,1)} %get-tuple-element.28), channel_id=1, source_target_pairs={{0,1},{1,0},{2,3},{3,2},{4,5},{5,4},{6,7},{7,6},{8,9},{9,8},{10,11... | collective-permute-start | bytes 786440 | tf_op jit(solution)/shard_map/ppermute | solution.py:16
  84.1 8.8 %collective-permute-start.1 = (bf16[2,64,1024]{2,1,0:T(8,128)(2,1)}, bf16[2,64,1024]{2,1,0:T(8,128)(2,1)}, u32[]{:S(2)}, u32[]{:S(2)}) collective-permute-start(bf16[2,64,1024]{2,1,0:T(8,128)(2,1)} %get-tuple-element.29), channel_id=1, source_target_pairs={{0,2},{1,3},{2,0},{3,1},{4,6},{5,7},{6,4},{7,5},{8,10},{9,11},{10,... | collective-permute-start | bytes 786440 | tf_op jit(solution)/shard_map/ppermute | solution.py:16
  84.6 11.3 %collective-permute-start.2 = (bf16[2,64,1024]{2,1,0:T(8,128)(2,1)}, bf16[2,64,1024]{2,1,0:T(8,128)(2,1)}, u32[]{:S(2)}, u32[]{:S(2)}) collective-permute-start(bf16[2,64,1024]{2,1,0:T(8,128)(2,1)} %get-tuple-element.30), channel_id=1, source_target_pairs={{0,4},{1,5},{2,6},{3,7},{4,0},{5,1},{6,2},{7,3},{8,12},{9,13},{10,... | collective-permute-start | bytes 786440 | tf_op jit(solution)/shard_map/ppermute | solution.py:16
  87.3 1.1 copy-start.10
  88.4 14.5 %collective-permute-start.3 = (bf16[2,64,1024]{2,1,0:T(8,128)(2,1)S(1)}, bf16[2,64,1024]{2,1,0:T(8,128)(2,1)S(1)}, u32[]{:S(2)}, u32[]{:S(2)}) collective-permute-start(bf16[2,64,1024]{2,1,0:T(8,128)(2,1)S(1)} %copy-done.10), channel_id=1, source_target_pairs={{0,8},{1,9},{2,10},{3,11},{4,12},{5,13},{6,14},{7,15},{8,0},{9,1},... | collective-permute-start | bytes 786440 | tf_op jit(solution)/shard_map/ppermute | solution.py:16
  103.3 1.0 copy-start.5
  106.2 4.4 %copy-start.3 = (bf16[1,128,1024]{2,1,0:T(8,128)(2,1)S(1)}, bf16[1,128,1024]{2,1,0:T(8,128)(2,1)}, u32[]{:S(2)}) copy-start(bf16[1,128,1024]{2,1,0:T(8,128)(2,1)} %param.6) | copy-start | bytes 786436
  110.6 8.4 %copy-start.8 = (bf16[128,1024]{1,0:T(8,128)(2,1)S(1)}, bf16[128,1024]{1,0:T(8,128)(2,1)}, u32[]{:S(2)}) copy-start(bf16[128,1024]{1,0:T(8,128)(2,1)} %param.7) | copy-start | bytes 786436
  110.7 8.6 %copy-start.11 = (f32[1,1024]{1,0:T(1,128)S(1)}, f32[1,1024]{1,0:T(1,128)}, u32[]{:S(2)}) copy-start(f32[1,1024]{1,0:T(1,128)} %param.8) | copy-start | bytes 12292
  111.1 12.0 %copy-start.6 = (bf16[128,1024]{1,0:T(8,128)(2,1)}, bf16[128,1024]{1,0:T(8,128)(2,1)S(1)}, u32[]{:S(2)}) copy-start(bf16[128,1024]{1,0:T(8,128)(2,1)S(1)} %fusion.37) | copy-start | bytes 786436
  111.1 7.9 %collective-permute-start.4 = (bf16[128,1024]{1,0:T(8,128)(2,1)S(1)}, bf16[128,1024]{1,0:T(8,128)(2,1)S(1)}, u32[]{:S(2)}, u32[]{:S(2)}) collective-permute-start(bf16[128,1024]{1,0:T(8,128)(2,1)S(1)} %fusion.37), channel_id=1, source_target_pairs={{0,16},{1,17},{2,18},{3,19},{4,20},{5,21},{6,22},{7,23},{8,24},{9,... | collective-permute-start | bytes 786440 | tf_op jit(solution)/shard_map/ppermute | solution.py:22
  123.1 1.2 copy-start.1
  129.4 7.3 %collective-permute-start.5 = (bf16[2,64,1024]{2,1,0:T(8,128)(2,1)}, bf16[2,64,1024]{2,1,0:T(8,128)(2,1)}, u32[]{:S(2)}, u32[]{:S(2)}) collective-permute-start(bf16[2,64,1024]{2,1,0:T(8,128)(2,1)} %get-tuple-element.24), channel_id=1, source_target_pairs={{0,1},{1,0},{2,3},{3,2},{4,5},{5,4},{6,7},{7,6},{8,9},{9,8},{10,11... | collective-permute-start | bytes 786440 | tf_op jit(solution)/shard_map/ppermute | solution.py:16
  129.4 9.0 %collective-permute-start.6 = (bf16[2,64,1024]{2,1,0:T(8,128)(2,1)}, bf16[2,64,1024]{2,1,0:T(8,128)(2,1)}, u32[]{:S(2)}, u32[]{:S(2)}) collective-permute-start(bf16[2,64,1024]{2,1,0:T(8,128)(2,1)} %get-tuple-element.25), channel_id=1, source_target_pairs={{0,2},{1,3},{2,0},{3,1},{4,6},{5,7},{6,4},{7,5},{8,10},{9,11},{10,... | collective-permute-start | bytes 786440 | tf_op jit(solution)/shard_map/ppermute | solution.py:16
  130.9 10.6 %collective-permute-start.7 = (bf16[2,64,1024]{2,1,0:T(8,128)(2,1)}, bf16[2,64,1024]{2,1,0:T(8,128)(2,1)}, u32[]{:S(2)}, u32[]{:S(2)}) collective-permute-start(bf16[2,64,1024]{2,1,0:T(8,128)(2,1)} %get-tuple-element.26), channel_id=1, source_target_pairs={{0,4},{1,5},{2,6},{3,7},{4,0},{5,1},{6,2},{7,3},{8,12},{9,13},{10,... | collective-permute-start | bytes 786440 | tf_op jit(solution)/shard_map/ppermute | solution.py:16
  132.1 2.0 %copy-start.9 = (bf16[2,64,1024]{2,1,0:T(8,128)(2,1)S(1)}, bf16[2,64,1024]{2,1,0:T(8,128)(2,1)}, u32[]{:S(2)}) copy-start(bf16[2,64,1024]{2,1,0:T(8,128)(2,1)} %get-tuple-element.23) | copy-start | bytes 786436
  134.2 15.1 %collective-permute-start.8 = (bf16[2,64,1024]{2,1,0:T(8,128)(2,1)S(1)}, bf16[2,64,1024]{2,1,0:T(8,128)(2,1)S(1)}, u32[]{:S(2)}, u32[]{:S(2)}) collective-permute-start(bf16[2,64,1024]{2,1,0:T(8,128)(2,1)S(1)} %copy-done.9), channel_id=1, source_target_pairs={{0,8},{1,9},{2,10},{3,11},{4,12},{5,13},{6,14},{7,15},{8,0},{9,1},... | collective-permute-start | bytes 786440 | tf_op jit(solution)/shard_map/ppermute | solution.py:16
  149.6 1.0 copy-start.4
  156.9 1.0 copy-start.7
Sparse Core Ops, SparseCore 0:
  9.6 64.5 all-gather.2
where the time goes:
time: 166 us
  waiting for transfers between devices  87 us (52%)
  local copies, waits for them, and re-layouts  22.8 us (14%)
  matrix products  18.7 us (11%)
  between operations  16.5 us (10%)
  starting transfers between devices  10.8 us (7%)
  other arithmetic  9.64 us (6%)
    all_gather x1, waiting for transfers between devices, per_device(): lax.all_gather(attention_triple_matrix[0], 'seq', axis=0, tiled=True)  61.7 us
    ppermute x8, waiting for transfers between devices, swapped(): lax.ppermute(x, axis, [(i, i ^ 1 << stride) for i in range(lax.axis_size(...  20.1 us
    unnamed x48, local copies, waits for them, and re-layouts  15.3 us
    dot_general x2, matrix products, transform_through_tier(): projected = jnp.dot(normed, weights, preferred_element_type=jnp.float32)  7.77 us
    ppermute x8, starting transfers between devices, swapped(): lax.ppermute(x, axis, [(i, i ^ 1 << stride) for i in range(lax.axis_size(...  7.43 us
    dot_general x2, matrix products, transform_through_tier(): jnp.einsum('chqk,ckhd->cqhd', weights_soft, all_values, preferred_element...  6.46 us
    ppermute x1, waiting for transfers between devices, from_behind(): return lax.ppermute(block, axis, route)  4.52 us
    dot_general x2, matrix products, transform_through_tier(): jnp.einsum('cqhd,ckhd->chqk', query_blocks, all_keys, preferred_element_t...  3.58 us
  transfers between devices with their start and end apart: 10, of which 8 were waited for; matrix products, arithmetic and copies ran while one was open for 8% of the time, Pallas kernels for 0%

commit v1 on v0

v1 whole, which is shorter than its diff:
```python
import functools

import jax
import jax.numpy as jnp
from jax import lax
from jax.experimental import pallas as pl
from jax.experimental.pallas import tpu as pltpu
from jax.sharding import PartitionSpec as P

HEADS = 8
HEAD = 128
BLOCK = 64
LEVELS = 4
WIDE = 256

epsilon = 1e-06


def swapped(x, axis, mask):
    return lax.ppermute(x, axis, [(i, i ^ mask) for i in range(lax.axis_size(axis))])


def from_behind(block, axis, distance):
    devices = range(lax.axis_size(axis))
    route = [(i - distance, i) for i in devices if i - distance in devices]
    return lax.ppermute(block, axis, route)


def row_norm(rows, gain):
    widened = rows.astype(jnp.float32)
    mean_square = jnp.mean(widened * widened, axis=-1, keepdims=True)
    return (widened * lax.rsqrt(mean_square + epsilon) * gain).astype(jnp.bfloat16)


def head_norm(one_head):
    mean_square = jnp.mean(one_head * one_head, axis=-1, keepdims=True)
    return (one_head * lax.rsqrt(mean_square + epsilon)).astype(jnp.bfloat16)


def layer_kernel(pieces, offsets, own_ref, far_ref, gain_ref, exit_ref, *rest):
    shards = rest[:pieces]
    out_ref, triple, leave, normed, queries, keys, values, attended, load_sem, exit_sem = rest[pieces:]
    inner = HEADS * HEAD
    rows = own_ref.shape[0]
    far_rows = far_ref.shape[0]
    piece_rows = shards[0].shape[0]
    exit_copy = pltpu.make_async_copy(exit_ref, leave, exit_sem)
    for third in range(3):
        for i, shard in enumerate(shards):
            spot = pl.multiple_of(offsets[i], piece_rows)
            pltpu.make_async_copy(
                shard.at[:, pl.ds(third * inner, inner)],
                triple.at[third, pl.ds(spot, piece_rows), :],
                load_sem.at[third],
            ).start()
    exit_copy.start()

    def loaded(third):
        pltpu.make_async_copy(triple.at[third], triple.at[third], load_sem.at[third]).wait()

    gain = gain_ref[...]
    normed[:rows] = row_norm(own_ref[...], gain)
    normed[rows:] = row_norm(far_ref[...], gain)
    loaded(0)
    for start in range(0, inner, WIDE):
        projected = jnp.dot(
            normed[:rows], triple[0, :, start : start + WIDE], preferred_element_type=jnp.float32
        )
        for head in range(0, WIDE, HEAD):
            queries[:, start + head : start + head + HEAD] = head_norm(projected[:, head : head + HEAD])
    loaded(1)
    for start in range(0, inner, WIDE):
        projected = jnp.dot(
            normed[...], triple[1, :, start : start + WIDE], preferred_element_type=jnp.float32
        )
        for head in range(0, WIDE, HEAD):
            keys[:, start + head : start + head + HEAD] = head_norm(projected[:, head : head + HEAD])
    loaded(2)
    for start in range(0, inner, WIDE):
        values[:, start : start + WIDE] = jnp.dot(
            normed[...], triple[2, :, start : start + WIDE], preferred_element_type=jnp.float32
        ).astype(jnp.bfloat16)
    reader = lax.broadcasted_iota(jnp.int32, (rows, rows + far_rows), 0) // BLOCK
    column = lax.broadcasted_iota(jnp.int32, (rows, rows + far_rows), 1)
    read = jnp.logical_or(column >= rows, column // BLOCK == reader)
    score_scale = HEAD ** (-0.5)
    for start in range(0, inner, HEAD):
        span = slice(start, start + HEAD)
        scores = (
            lax.dot_general(
                queries[:, span],
                keys[:, span],
                (((1,), (1,)), ((), ())),
                preferred_element_type=jnp.float32,
            )
            * score_scale
        )
        exps = jnp.where(read, jnp.exp(scores), 0.0)
        weights = (exps / jnp.sum(exps, axis=-1, keepdims=True)).astype(jnp.bfloat16)
        attended[:, span] = jnp.dot(
            weights, values[:, span], preferred_element_type=jnp.float32
        ).astype(jnp.bfloat16)
    exit_copy.wait()
    for start in range(0, own_ref.shape[1], WIDE):
        span = slice(start, start + WIDE)
        out_ref[:, span] = (
            own_ref[:, span].astype(jnp.float32)
            + jnp.dot(attended[...], leave[:, span], preferred_element_type=jnp.float32)
        ).astype(jnp.bfloat16)


def layer(own, far, gain, exit_matrix, offsets, shards):
    rows, width = own.shape
    far_rows = far.shape[0]
    inner = HEADS * HEAD
    in_vmem = pl.BlockSpec(memory_space=pltpu.VMEM)
    anywhere = pl.BlockSpec(memory_space=pl.ANY)
    return pl.pallas_call(
        functools.partial(layer_kernel, len(shards)),
        out_shape=jax.ShapeDtypeStruct((rows, width), jnp.bfloat16),
        in_specs=[pl.BlockSpec(memory_space=pltpu.SMEM), in_vmem, in_vmem, in_vmem, anywhere]
        + [anywhere] * len(shards),
        out_specs=in_vmem,
        scratch_shapes=[
            pltpu.VMEM((3, width, inner), jnp.bfloat16),
            pltpu.VMEM((inner, width), jnp.bfloat16),
            pltpu.VMEM((rows + far_rows, width), jnp.bfloat16),
            pltpu.VMEM((rows, inner), jnp.bfloat16),
            pltpu.VMEM((rows + far_rows, inner), jnp.bfloat16),
            pltpu.VMEM((rows + far_rows, inner), jnp.bfloat16),
            pltpu.VMEM((rows, inner), jnp.bfloat16),
            pltpu.SemaphoreType.DMA((3,)),
            pltpu.SemaphoreType.DMA,
        ],
        compiler_params=pltpu.CompilerParams(vmem_limit_bytes=40 * 1024 * 1024),
        cost_estimate=pl.CostEstimate(flops=2_400_000_000, bytes_accessed=9_000_000, transcendentals=400_000),
    )(offsets, own, far, gain, exit_matrix, *shards)


def gathered(shard):
    devices = lax.axis_size("seq")
    me = lax.axis_index("seq")
    rows = shard.shape[0]
    if devices != 16:
        whole = lax.all_gather(shard, "seq", axis=0, tiled=True)
        return [whole], jnp.zeros((1,), jnp.int32)
    held = {0: shard}
    for mask in (4, 8, 12):
        held[mask] = swapped(shard, "seq", mask)
    for mask in (0, 4, 8, 12):
        held[mask | 2] = swapped(held[mask], "seq", 2)
    for mask in (0, 4, 2, 8, 6, 12, 10, 14):
        held[mask | 1] = swapped(held[mask], "seq", 1)
    order = sorted(held)
    offsets = jnp.stack([jnp.bitwise_xor(me, mask) * rows for mask in order]).astype(jnp.int32)
    return [held[mask] for mask in order], offsets


def partner_rows(own, lookup):
    me = lax.axis_index("seq")
    remote = []
    for level in range(LEVELS):
        partner = jnp.bitwise_xor(me, jnp.int32(1 << level))
        requested = lookup[partner, level]
        chosen = lax.dynamic_slice_in_dim(own, requested * BLOCK, BLOCK, 0)
        remote.append(swapped(chosen, "seq", 1 << level))
    return jnp.concatenate(remote, axis=0)


def per_device(resident, arriving, gain, triple, exit_matrix, lookup):
    section = lax.axis_index("section")
    shards, offsets = gathered(triple[0])
    first_in = resident[0]
    first_out = layer(first_in, partner_rows(first_in, lookup), gain, exit_matrix[0], offsets, shards)
    moved = from_behind(first_out, "section", 1)
    second_in = jnp.where(section == 0, arriving, moved)
    second_out = layer(second_in, partner_rows(second_in, lookup), gain, exit_matrix[0], offsets, shards)
    return jnp.stack([first_out, second_out])[:, None]


def solution(mesh):
    placed = (
        P("section", "seq", None),
        P("seq", None),
        P("section", None),
        P("section", "seq", None),
        P("section", None, None),
        P(),
    )
    return jax.shard_map(
        per_device,
        mesh=mesh,
        in_specs=placed,
        out_specs=P(None, "section", "seq", None),
        check_vma=False,
    )
```

time: 166 us -> 115 us (0.69)
  waiting for transfers between devices: 87 us -> 58.9 us
  matrix products: 18.7 us -> 0 us
  Pallas kernels: 0 us -> 14.5 us
  between operations: 16.5 us -> 2.7 us
  starting transfers between devices: 10.8 us -> 24.5 us
  local copies, waits for them, and re-layouts: 22.8 us -> 10.7 us
  other arithmetic: 9.64 us -> 2.9 us
    all_gather x1 -> x0, waiting for transfers between devices: 61.7 us -> none  [per_device(): lax.all_gather(attention_triple_matrix[0], 'seq', axis=0, tiled=True)]
    ppermute x8 -> x23, waiting for transfers between devices: 20.1 us -> 53.8 us  [swapped(): lax.ppermute(x, axis, [(i, i ^ mask) for i in range(lax.axis_size(axis))])]
    dot_general x8 -> x0, matrix products: 18.7 us -> none  [the longest x2 7.77 us: transform_through_tier(): projected = jnp.dot(normed, weights, preferred_element_type=jnp.float32)]
    pallas_call x0 -> x2, Pallas kernels: none -> 14.5 us  [layer(): pl.pallas_call(functools.partial(layer_kernel, len(shards)), out_shape=ja...]
    ppermute x8 -> x23, starting transfers between devices: 7.43 us -> 20.2 us  [swapped(): lax.ppermute(x, axis, [(i, i ^ mask) for i in range(lax.axis_size(axis))])]
    unnamed x48 -> x34, local copies, waits for them, and re-layouts: 15.3 us -> 7.84 us
    unnamed x4 -> x0, other arithmetic: 2.87 us -> none
    convert_element_type x2 -> x0, local copies, waits for them, and re-layouts: 2.25 us -> none  [transform_through_tier(): attended = mixed_heads.astype(jnp.bfloat16).reshape(row_count, inner_width)]
  transfers between devices with their start and end apart: 10 -> 24, of which waited for: 8 -> 9; matrix products, arithmetic and copies ran while one was open for 8% -> 1% of each run, Pallas kernels for 0% -> 0%
where the time goes in v1:
time: 115 us; the launch traced here: 114 us
  waiting for transfers between devices  58.9 us (51%)
  starting transfers between devices  24.5 us (21%)
  Pallas kernels  14.5 us (13%)
  local copies, waits for them, and re-layouts  10.7 us (9%)
  other arithmetic  2.9 us (3%)
  between operations  2.7 us (2%)
    ppermute x23, waiting for transfers between devices, swapped(): lax.ppermute(x, axis, [(i, i ^ mask) for i in range(lax.axis_size(axis))])  53.8 us
    ppermute x23, starting transfers between devices, swapped(): lax.ppermute(x, axis, [(i, i ^ mask) for i in range(lax.axis_size(axis))])  20.2 us
    pallas_call x2, Pallas kernels, layer(): pl.pallas_call(functools.partial(layer_kernel, len(shards)), out_shape=ja...  14.5 us
    unnamed x34, local copies, waits for them, and re-layouts  7.84 us
    ppermute x1, waiting for transfers between devices, from_behind(): return lax.ppermute(block, axis, route)  5.13 us
    ppermute x1, starting transfers between devices, from_behind(): return lax.ppermute(block, axis, route)  4.26 us
  transfers between devices with their start and end apart: 24, of which 9 were waited for; matrix products, arithmetic and copies ran while one was open for 1% of the time, Pallas kernels for 0%

profile of v1, /device:TPU:0, one launch (start us, length us, event | category | flops | bytes accessed | tf_op | source)
XLA Modules:
  0.0 114.2 jit_solution(16157422376778301530)
XLA Ops:
  0.0 1.5 %constant_dynamic-slice_fusion.4 = (s32[1,1]{0,1:T(1,128)}, s32[1,1]{0,1:T(1,128)}, s32[1,1]{0,1:T(1,128)}, s32[1,1]{0,1:T(1,128)}) fusion(s32[16,4]{0,1:T(4,128)} %param.11, s32[]{:T(128)S(6)} %select_n.40, s32[]{:T(128)S(6)} %select_n.42, s32[]{:T(128)S(6)} %select_n.46, s32[]{:T(128)S(6)} %select_n.44), kind=kLoop, calls=%fused_computation.12 | loop fusion | bytes 48 | tf_op jit(solution)/shard_map/dynamic_slice | solution.py:164
  4.1 1.1 %dynamic-slice_bitcast_fusion.3 = (bf16[64,1024]{1,0:T(8,128)(2,1)S(1)}, bf16[64,1024]{1,0:T(8,128)(2,1)S(1)}, bf16[64,1024]{1,0:T(8,128)(2,1)S(1)}, bf16[64,1024]{1,0:T(8,128)(2,1)S(1)}) fusion(bf16[1,128,1024]{2,1,0:T(8,128)(2,1)} %param.6, s32[]{:T(128)S(6)} %select_n.41, s32[]{:T(128)S(6)} %select_n.43, s32[]{:T(128)S(6)} %select_n.47, s32[]{:T(128)S(6)} %select_n.45), kind=kLoop, calls=%fused_computation.7 | loop fusion | bytes 1048592 | tf_op jit(solution)/shard_map/dynamic_slice | solution.py:165
  5.7 2.6 %collective-permute-start.1 = (bf16[64,1024]{1,0:T(8,128)(2,1)S(1)}, bf16[64,1024]{1,0:T(8,128)(2,1)S(1)}, u32[]{:S(2)}, u32[]{:S(2)}) collective-permute-start(bf16[64,1024]{1,0:T(8,128)(2,1)S(1)} %get-tuple-element.10), channel_id=1, source_target_pairs={{0,2},{1,3},{2,0},{3,1},{4,6},{5,7},{6,4},{7,5},{8,10},{9,11},{10,... | collective-permute-start | bytes 393224 | tf_op jit(solution)/shard_map/ppermute | solution.py:20
  8.3 2.6 %collective-permute-start.3 = (bf16[64,1024]{1,0:T(8,128)(2,1)S(1)}, bf16[64,1024]{1,0:T(8,128)(2,1)S(1)}, u32[]{:S(2)}, u32[]{:S(2)}) collective-permute-start(bf16[64,1024]{1,0:T(8,128)(2,1)S(1)} %get-tuple-element.11), channel_id=1, source_target_pairs={{0,8},{1,9},{2,10},{3,11},{4,12},{5,13},{6,14},{7,15},{8,0},{9,1},... | collective-permute-start | bytes 393224 | tf_op jit(solution)/shard_map/ppermute | solution.py:20
  10.9 1.6 %collective-permute-start.2 = (bf16[64,1024]{1,0:T(8,128)(2,1)S(1)}, bf16[64,1024]{1,0:T(8,128)(2,1)}, u32[]{:S(2)}, u32[]{:S(2)}) collective-permute-start(bf16[64,1024]{1,0:T(8,128)(2,1)S(1)} %get-tuple-element.12), channel_id=1, source_target_pairs={{0,4},{1,5},{2,6},{3,7},{4,0},{5,1},{6,2},{7,3},{8,12},{9,13},{10,... | collective-permute-start | bytes 393224 | tf_op jit(solution)/shard_map/ppermute | solution.py:20
  12.7 1.7 %collective-permute-start.11 = (bf16[64,3072]{1,0:T(8,128)(2,1)}, bf16[64,3072]{1,0:T(8,128)(2,1)S(1)}, u32[]{:S(2)}, u32[]{:S(2)}) collective-permute-start(bf16[64,3072]{1,0:T(8,128)(2,1)} %bitcast.41), channel_id=1, source_target_pairs={{0,8},{1,9},{2,10},{3,11},{4,12},{5,13},{6,14},{7,15},{8,0},{9,1},... | collective-permute-start | bytes 1179656 | tf_op jit(solution)/shard_map/ppermute | solution.py:20
  14.4 2.5 %collective-permute-start.7 = (bf16[64,3072]{1,0:T(8,128)(2,1)}, bf16[64,3072]{1,0:T(8,128)(2,1)S(1)}, u32[]{:S(2)}, u32[]{:S(2)}) collective-permute-start(bf16[64,3072]{1,0:T(8,128)(2,1)} %bitcast.42), channel_id=1, source_target_pairs={{0,4},{1,5},{2,6},{3,7},{4,0},{5,1},{6,2},{7,3},{8,12},{9,13},{10,... | collective-permute-start | bytes 1179656 | tf_op jit(solution)/shard_map/ppermute | solution.py:20
  16.9 2.0 %collective-permute-done.3 = bf16[64,1024]{1,0:T(8,128)(2,1)S(1)} collective-permute-done((bf16[64,1024]{1,0:T(8,128)(2,1)S(1)}, bf16[64,1024]{1,0:T(8,128)(2,1)S(1)}, u32[]{:S(2)}, u32[]{:S(2)}) %collective-permute-start.3) | collective-permute-done | bytes 131104 | tf_op jit(solution)/shard_map/ppermute | solution.py:20
  19.5 8.4 %collective-permute-done.15.rest_12_ = bf16[64,3072]{1,0:T(8,128)(2,1)S(1)} collective-permute-done((bf16[64,3072]{1,0:T(8,128)(2,1)}, bf16[64,3072]{1,0:T(8,128)(2,1)S(1)}, u32[]{:S(2)}, u32[]{:S(2)}) %collective-permute-start.15) | collective-permute-done | bytes 393248 | tf_op jit(solution)/shard_map/ppermute | solution.py:20
  28.5 22.8 %collective-permute-done.11.rest_8_ = bf16[64,3072]{1,0:T(8,128)(2,1)S(1)} collective-permute-done((bf16[64,3072]{1,0:T(8,128)(2,1)}, bf16[64,3072]{1,0:T(8,128)(2,1)S(1)}, u32[]{:S(2)}, u32[]{:S(2)}) %collective-permute-start.11) | collective-permute-done | bytes 393248 | tf_op jit(solution)/shard_map/ppermute | solution.py:20
  52.0 0.7 copy-done.6
  52.7 1.5 %collective-permute-start.9 = (bf16[64,3072]{1,0:T(8,128)(2,1)S(1)}, bf16[64,3072]{1,0:T(8,128)(2,1)}, u32[]{:S(2)}, u32[]{:S(2)}) collective-permute-start(bf16[64,3072]{1,0:T(8,128)(2,1)S(1)} %collective-permute-done.7.rest_4_), channel_id=1, source_target_pairs={{0,2},{1,3},{2,0},{3,1},{4,6},{5,7},{6,4},{7,5},{8,10},{9,11},{10,... | collective-permute-start | bytes 1179656 | tf_op jit(solution)/shard_map/ppermute | solution.py:20
  54.4 0.7 copy-done.9
  55.6 7.8 %collective-permute-done.13.rest_10_ = bf16[64,3072]{1,0:T(8,128)(2,1)} collective-permute-done((bf16[64,3072]{1,0:T(8,128)(2,1)S(1)}, bf16[64,3072]{1,0:T(8,128)(2,1)}, u32[]{:S(2)}, u32[]{:S(2)}) %collective-permute-start.13) | collective-permute-done | bytes 393248 | tf_op jit(solution)/shard_map/ppermute | solution.py:20
  63.4 0.7 copy-done.12
  64.6 6.7 %collective-permute-done.9.rest_6_ = bf16[64,3072]{1,0:T(8,128)(2,1)} collective-permute-done((bf16[64,3072]{1,0:T(8,128)(2,1)S(1)}, bf16[64,3072]{1,0:T(8,128)(2,1)}, u32[]{:S(2)}, u32[]{:S(2)}) %collective-permute-start.9) | collective-permute-done | bytes 393248 | tf_op jit(solution)/shard_map/ppermute | solution.py:20
  71.4 1.0 pad_maximum_fusion.far_ref
  72.5 0.9 collective-permute-done.10.rest_7_
  73.4 0.9 copy-done.1
  74.4 1.0 copy-done.2
  75.4 1.0 copy-done.7
  76.4 1.0 copy-done.10
  77.4 1.0 copy-done.13
  78.4 7.2 %shard_map.64 = bf16[128,1024]{1,0:T(8,128)(2,1)S(1)} custom-call(s32[16]{0:T(128)S(1)} %stack.76.offsets, bf16[128,1024]{1,0:T(8,128)(2,1)S(1)} %bitcast.39, bf16[256,1024]{1,0:T(8,128)(2,1)S(1)} %pad_maximum_fusion.far_ref, f32[1,1024]{1,0:T(1,128)S(1)} %copy-done.15, bf16[1024,1024]{1,0:T(8,128)(2,1)S(1)} %bitcast.37, bf16[64,3072]{1,0:T(8,128)(2,1)S(1)} %bitcast.45, ...), custom_call_target="tpu_custom_call" | custom-call | flops 2400000000 | bytes 9000000 | tf_op jit(solution)/shard_map/pallas_call | solution.py:118
  85.6 4.3 %collective-permute-start.19 = (bf16[128,1024]{1,0:T(8,128)(2,1)S(1)}, bf16[128,1024]{1,0:T(8,128)(2,1)}, u32[]{:S(2)}, u32[]{:S(2)}) collective-permute-start(bf16[128,1024]{1,0:T(8,128)(2,1)S(1)} %shard_map.64), channel_id=1, source_target_pairs={{0,16},{1,17},{2,18},{3,19},{4,20},{5,21},{6,22},{7,23},{8,24},{9,... | collective-permute-start | bytes 786440 | tf_op jit(solution)/shard_map/ppermute | solution.py:26
  89.9 5.1 %collective-permute-done.19 = bf16[128,1024]{1,0:T(8,128)(2,1)} collective-permute-done((bf16[128,1024]{1,0:T(8,128)(2,1)S(1)}, bf16[128,1024]{1,0:T(8,128)(2,1)}, u32[]{:S(2)}, u32[]{:S(2)}) %collective-permute-start.19) | collective-permute-done | bytes 262176 | tf_op jit(solution)/shard_map/ppermute | solution.py:26
  95.0 1.0 broadcast_select_fusion.own_ref
  96.1 2.2 %collective-permute-start.23 = (bf16[64,1024]{1,0:T(8,128)(2,1)S(1)}, bf16[64,1024]{1,0:T(8,128)(2,1)S(1)}, u32[]{:S(2)}, u32[]{:S(2)}) collective-permute-start(bf16[64,1024]{1,0:T(8,128)(2,1)S(1)} %get-tuple-element.6), channel_id=1, source_target_pairs={{0,8},{1,9},{2,10},{3,11},{4,12},{5,13},{6,14},{7,15},{8,0},{9,1},... | collective-permute-start | bytes 393224 | tf_op jit(solution)/shard_map/ppermute | solution.py:20
  98.4 1.9 %collective-permute-start.22 = (bf16[64,1024]{1,0:T(8,128)(2,1)S(1)}, bf16[64,1024]{1,0:T(8,128)(2,1)S(1)}, u32[]{:S(2)}, u32[]{:S(2)}) collective-permute-start(bf16[64,1024]{1,0:T(8,128)(2,1)S(1)} %get-tuple-element.7), channel_id=1, source_target_pairs={{0,4},{1,5},{2,6},{3,7},{4,0},{5,1},{6,2},{7,3},{8,12},{9,13},{10,... | collective-permute-start | bytes 393224 | tf_op jit(solution)/shard_map/ppermute | solution.py:20
  100.8 5.0 %collective-permute-done.23 = bf16[64,1024]{1,0:T(8,128)(2,1)S(1)} collective-permute-done((bf16[64,1024]{1,0:T(8,128)(2,1)S(1)}, bf16[64,1024]{1,0:T(8,128)(2,1)S(1)}, u32[]{:S(2)}, u32[]{:S(2)}) %collective-permute-start.23) | collective-permute-done | bytes 131104 | tf_op jit(solution)/shard_map/ppermute | solution.py:20
  106.1 7.3 %shard_map.65 = bf16[128,1024]{1,0:T(8,128)(2,1)S(1)} custom-call(s32[16]{0:T(128)S(1)} %stack.76.offsets, bf16[128,1024]{1,0:T(8,128)(2,1)S(1)} %broadcast_select_fusion.own_ref, bf16[256,1024]{1,0:T(8,128)(2,1)S(1)} %pad_maximum_fusion.1.far_ref, f32[1,1024]{1,0:T(1,128)S(1)} %copy-done.15, bf16[1024,1024]{1,0:T(8,128)(2,1)S(1)} %bitcast.38, ...), custom_call_target="tpu_custom_call" | custom-call | flops 2400000000 | bytes 9000000 | tf_op jit(solution)/shard_map/pallas_call | solution.py:118
  113.3 0.8 maximum_bitcast_fusion
  (60 shorter events, 4.6 us)
Async XLA Ops:
  0.0 73.4 %copy-start.15 = (f32[1,1024]{1,0:T(1,128)S(1)}, f32[1,1024]{1,0:T(1,128)}, u32[]{:S(2)}) copy-start(f32[1,1024]{1,0:T(1,128)} %gain_ref.3) | copy-start | bytes 12292
  0.0 73.4 %copy-start = (bf16[1,1024,1024]{2,1,0:T(8,128)(2,1)S(1)}, bf16[1,1024,1024]{2,1,0:T(8,128)(2,1)}, u32[]{:S(2)}) copy-start(bf16[1,1024,1024]{2,1,0:T(8,128)(2,1)} %param.10) | copy-start | bytes 6291460
  5.2 7.5 %collective-permute-start = (bf16[64,1024]{1,0:T(8,128)(2,1)S(1)}, bf16[64,1024]{1,0:T(8,128)(2,1)S(1)}, u32[]{:S(2)}, u32[]{:S(2)}) collective-permute-start(bf16[64,1024]{1,0:T(8,128)(2,1)S(1)} %get-tuple-element.9), channel_id=1, source_target_pairs={{0,1},{1,0},{2,3},{3,2},{4,5},{5,4},{6,7},{7,6},{8,9},{9,8},{10,11... | collective-permute-start | bytes 393224 | tf_op jit(solution)/shard_map/ppermute | solution.py:20
  5.7 8.7 %collective-permute-start.1 = (bf16[64,1024]{1,0:T(8,128)(2,1)S(1)}, bf16[64,1024]{1,0:T(8,128)(2,1)S(1)}, u32[]{:S(2)}, u32[]{:S(2)}) collective-permute-start(bf16[64,1024]{1,0:T(8,128)(2,1)S(1)} %get-tuple-element.10), channel_id=1, source_target_pairs={{0,2},{1,3},{2,0},{3,1},{4,6},{5,7},{6,4},{7,5},{8,10},{9,11},{10,... | collective-permute-start | bytes 393224 | tf_op jit(solution)/shard_map/ppermute | solution.py:20
  8.3 10.5 %collective-permute-start.3 = (bf16[64,1024]{1,0:T(8,128)(2,1)S(1)}, bf16[64,1024]{1,0:T(8,128)(2,1)S(1)}, u32[]{:S(2)}, u32[]{:S(2)}) collective-permute-start(bf16[64,1024]{1,0:T(8,128)(2,1)S(1)} %get-tuple-element.11), channel_id=1, source_target_pairs={{0,8},{1,9},{2,10},{3,11},{4,12},{5,13},{6,14},{7,15},{8,0},{9,1},... | collective-permute-start | bytes 393224 | tf_op jit(solution)/shard_map/ppermute | solution.py:20
  10.9 8.6 %collective-permute-start.2 = (bf16[64,1024]{1,0:T(8,128)(2,1)S(1)}, bf16[64,1024]{1,0:T(8,128)(2,1)}, u32[]{:S(2)}, u32[]{:S(2)}) collective-permute-start(bf16[64,1024]{1,0:T(8,128)(2,1)S(1)} %get-tuple-element.12), channel_id=1, source_target_pairs={{0,4},{1,5},{2,6},{3,7},{4,0},{5,1},{6,2},{7,3},{8,12},{9,13},{10,... | collective-permute-start | bytes 393224 | tf_op jit(solution)/shard_map/ppermute | solution.py:20
  12.5 15.5 %collective-permute-start.15 = (bf16[64,3072]{1,0:T(8,128)(2,1)}, bf16[64,3072]{1,0:T(8,128)(2,1)S(1)}, u32[]{:S(2)}, u32[]{:S(2)}) collective-permute-start(bf16[64,3072]{1,0:T(8,128)(2,1)} %bitcast.40), channel_id=1, source_target_pairs={{0,12},{1,13},{2,14},{3,15},{4,8},{5,9},{6,10},{7,11},{8,4},{9,5},... | collective-permute-start | bytes 1179656 | tf_op jit(solution)/shard_map/ppermute | solution.py:20
  12.7 38.6 %collective-permute-start.11 = (bf16[64,3072]{1,0:T(8,128)(2,1)}, bf16[64,3072]{1,0:T(8,128)(2,1)S(1)}, u32[]{:S(2)}, u32[]{:S(2)}) collective-permute-start(bf16[64,3072]{1,0:T(8,128)(2,1)} %bitcast.41), channel_id=1, source_target_pairs={{0,8},{1,9},{2,10},{3,11},{4,12},{5,13},{6,14},{7,15},{8,0},{9,1},... | collective-permute-start | bytes 1179656 | tf_op jit(solution)/shard_map/ppermute | solution.py:20
  14.4 36.9 %collective-permute-start.7 = (bf16[64,3072]{1,0:T(8,128)(2,1)}, bf16[64,3072]{1,0:T(8,128)(2,1)S(1)}, u32[]{:S(2)}, u32[]{:S(2)}) collective-permute-start(bf16[64,3072]{1,0:T(8,128)(2,1)} %bitcast.42), channel_id=1, source_target_pairs={{0,4},{1,5},{2,6},{3,7},{4,0},{5,1},{6,2},{7,3},{8,12},{9,13},{10,... | collective-permute-start | bytes 1179656 | tf_op jit(solution)/shard_map/ppermute | solution.py:20
  18.8 33.0 %collective-permute-start.5 = (bf16[64,3072]{1,0:T(8,128)(2,1)}, bf16[64,3072]{1,0:T(8,128)(2,1)}, u32[]{:S(2)}, u32[]{:S(2)}) collective-permute-start(bf16[64,3072]{1,0:T(8,128)(2,1)} %bitcast.43), channel_id=1, source_target_pairs={{0,2},{1,3},{2,0},{3,1},{4,6},{5,7},{6,4},{7,5},{8,10},{9,11},{10,... | collective-permute-start | bytes 1179656 | tf_op jit(solution)/shard_map/ppermute | solution.py:20
  19.5 32.5 %collective-permute-start.4 = (bf16[64,3072]{1,0:T(8,128)(2,1)}, bf16[64,3072]{1,0:T(8,128)(2,1)S(1)}, u32[]{:S(2)}, u32[]{:S(2)}) collective-permute-start(bf16[64,3072]{1,0:T(8,128)(2,1)} %bitcast.44), channel_id=1, source_target_pairs={{0,1},{1,0},{2,3},{3,2},{4,5},{5,4},{6,7},{7,6},{8,9},{9,8},{10,11... | collective-permute-start | bytes 1179656 | tf_op jit(solution)/shard_map/ppermute | solution.py:20
  27.9 26.4 %collective-permute-start.17 = (bf16[64,3072]{1,0:T(8,128)(2,1)S(1)}, bf16[64,3072]{1,0:T(8,128)(2,1)}, u32[]{:S(2)}, u32[]{:S(2)}) collective-permute-start(bf16[64,3072]{1,0:T(8,128)(2,1)S(1)} %collective-permute-done.15.rest_12_), channel_id=1, source_target_pairs={{0,2},{1,3},{2,0},{3,1},{4,6},{5,7},{6,4},{7,5},{8,10},{9,11},{10,... | collective-permute-start | bytes 1179656 | tf_op jit(solution)/shard_map/ppermute | solution.py:20
  51.3 3.1 %collective-permute-start.16 = (bf16[64,3072]{1,0:T(8,128)(2,1)S(1)}, bf16[64,3072]{1,0:T(8,128)(2,1)S(1)}, u32[]{:S(2)}, u32[]{:S(2)}) collective-permute-start(bf16[64,3072]{1,0:T(8,128)(2,1)S(1)} %collective-permute-done.15.rest_12_), channel_id=1, source_target_pairs={{0,1},{1,0},{2,3},{3,2},{4,5},{5,4},{6,7},{7,6},{8,9},{9,8},{10,11... | collective-permute-start | bytes 1179656 | tf_op jit(solution)/shard_map/ppermute | solution.py:20
  51.3 22.1 %copy-start.4 = (bf16[64,3072]{1,0:T(8,128)(2,1)}, bf16[64,3072]{1,0:T(8,128)(2,1)S(1)}, u32[]{:S(2)}) copy-start(bf16[64,3072]{1,0:T(8,128)(2,1)S(1)} %collective-permute-done.7.rest_4_) | copy-start | bytes 1179652
  51.3 12.1 %collective-permute-start.13 = (bf16[64,3072]{1,0:T(8,128)(2,1)S(1)}, bf16[64,3072]{1,0:T(8,128)(2,1)}, u32[]{:S(2)}, u32[]{:S(2)}) collective-permute-start(bf16[64,3072]{1,0:T(8,128)(2,1)S(1)} %collective-permute-done.11.rest_8_), channel_id=1, source_target_pairs={{0,2},{1,3},{2,0},{3,1},{4,6},{5,7},{6,4},{7,5},{8,10},{9,11},{10,... | collective-permute-start | bytes 1179656 | tf_op jit(solution)/shard_map/ppermute | solution.py:20
  51.8 11.5 %collective-permute-start.12 = (bf16[64,3072]{1,0:T(8,128)(2,1)S(1)}, bf16[64,3072]{1,0:T(8,128)(2,1)S(1)}, u32[]{:S(2)}, u32[]{:S(2)}) collective-permute-start(bf16[64,3072]{1,0:T(8,128)(2,1)S(1)} %collective-permute-done.11.rest_8_), channel_id=1, source_target_pairs={{0,1},{1,0},{2,3},{3,2},{4,5},{5,4},{6,7},{7,6},{8,9},{9,8},{10,11... | collective-permute-start | bytes 1179656 | tf_op jit(solution)/shard_map/ppermute | solution.py:20
  52.7 18.6 %collective-permute-start.9 = (bf16[64,3072]{1,0:T(8,128)(2,1)S(1)}, bf16[64,3072]{1,0:T(8,128)(2,1)}, u32[]{:S(2)}, u32[]{:S(2)}) collective-permute-start(bf16[64,3072]{1,0:T(8,128)(2,1)S(1)} %collective-permute-done.7.rest_4_), channel_id=1, source_target_pairs={{0,2},{1,3},{2,0},{3,1},{4,6},{5,7},{6,4},{7,5},{8,10},{9,11},{10,... | collective-permute-start | bytes 1179656 | tf_op jit(solution)/shard_map/ppermute | solution.py:20
  54.3 18.2 %collective-permute-start.8 = (bf16[64,3072]{1,0:T(8,128)(2,1)S(1)}, bf16[64,3072]{1,0:T(8,128)(2,1)}, u32[]{:S(2)}, u32[]{:S(2)}) collective-permute-start(bf16[64,3072]{1,0:T(8,128)(2,1)S(1)} %collective-permute-done.7.rest_4_), channel_id=1, source_target_pairs={{0,1},{1,0},{2,3},{3,2},{4,5},{5,4},{6,7},{7,6},{8,9},{9,8},{10,11... | collective-permute-start | bytes 1179656 | tf_op jit(solution)/shard_map/ppermute | solution.py:20
  55.1 17.4 %collective-permute-start.6 = (bf16[64,3072]{1,0:T(8,128)(2,1)}, bf16[64,3072]{1,0:T(8,128)(2,1)}, u32[]{:S(2)}, u32[]{:S(2)}) collective-permute-start(bf16[64,3072]{1,0:T(8,128)(2,1)} %collective-permute-done.5.rest_2_), channel_id=1, source_target_pairs={{0,1},{1,0},{2,3},{3,2},{4,5},{5,4},{6,7},{7,6},{8,9},{9,8},{10,11... | collective-permute-start | bytes 1179656 | tf_op jit(solution)/shard_map/ppermute | solution.py:20
  63.4 9.1 %collective-permute-start.18 = (bf16[64,3072]{1,0:T(8,128)(2,1)}, bf16[64,3072]{1,0:T(8,128)(2,1)}, u32[]{:S(2)}, u32[]{:S(2)}) collective-permute-start(bf16[64,3072]{1,0:T(8,128)(2,1)} %collective-permute-done.17.rest_14_), channel_id=1, source_target_pairs={{0,1},{1,0},{2,3},{3,2},{4,5},{5,4},{6,7},{7,6},{8,9},{9,8},{10,11... | collective-permute-start | bytes 1179656 | tf_op jit(solution)/shard_map/ppermute | solution.py:20
  64.1 8.4 %collective-permute-start.14 = (bf16[64,3072]{1,0:T(8,128)(2,1)}, bf16[64,3072]{1,0:T(8,128)(2,1)}, u32[]{:S(2)}, u32[]{:S(2)}) collective-permute-start(bf16[64,3072]{1,0:T(8,128)(2,1)} %collective-permute-done.13.rest_10_), channel_id=1, source_target_pairs={{0,1},{1,0},{2,3},{3,2},{4,5},{5,4},{6,7},{7,6},{8,9},{9,8},{10,11... | collective-permute-start | bytes 1179656 | tf_op jit(solution)/shard_map/ppermute | solution.py:20
  71.3 2.1 %collective-permute-start.10 = (bf16[64,3072]{1,0:T(8,128)(2,1)}, bf16[64,3072]{1,0:T(8,128)(2,1)}, u32[]{:S(2)}, u32[]{:S(2)}) collective-permute-start(bf16[64,3072]{1,0:T(8,128)(2,1)} %collective-permute-done.9.rest_6_), channel_id=1, source_target_pairs={{0,1},{1,0},{2,3},{3,2},{4,5},{5,4},{6,7},{7,6},{8,9},{9,8},{10,11... | collective-permute-start | bytes 1179656 | tf_op jit(solution)/shard_map/ppermute | solution.py:20
  85.6 20.4 %copy-start.3 = (bf16[1,64,3072]{2,1,0:T(8,128)(2,1)S(1)}, bf16[1,64,3072]{2,1,0:T(8,128)(2,1)}, u32[]{:S(2)}) copy-start(bf16[1,64,3072]{2,1,0:T(8,128)(2,1)} %param.9) | copy-start | bytes 1179652
  85.6 9.4 %collective-permute-start.19 = (bf16[128,1024]{1,0:T(8,128)(2,1)S(1)}, bf16[128,1024]{1,0:T(8,128)(2,1)}, u32[]{:S(2)}, u32[]{:S(2)}) collective-permute-start(bf16[128,1024]{1,0:T(8,128)(2,1)S(1)} %shard_map.64), channel_id=1, source_target_pairs={{0,16},{1,17},{2,18},{3,19},{4,20},{5,21},{6,22},{7,23},{8,24},{9,... | collective-permute-start | bytes 786440 | tf_op jit(solution)/shard_map/ppermute | solution.py:26
  89.9 16.1 %copy-start.5 = (bf16[64,3072]{1,0:T(8,128)(2,1)S(1)}, bf16[64,3072]{1,0:T(8,128)(2,1)}, u32[]{:S(2)}) copy-start(bf16[64,3072]{1,0:T(8,128)(2,1)} %copy-done.4) | copy-start | bytes 1179652
  89.9 16.1 %copy-start.8 = (bf16[64,3072]{1,0:T(8,128)(2,1)S(1)}, bf16[64,3072]{1,0:T(8,128)(2,1)}, u32[]{:S(2)}) copy-start(bf16[64,3072]{1,0:T(8,128)(2,1)} %copy-done.6) | copy-start | bytes 1179652
  89.9 16.1 %copy-start.11 = (bf16[64,3072]{1,0:T(8,128)(2,1)S(1)}, bf16[64,3072]{1,0:T(8,128)(2,1)}, u32[]{:S(2)}) copy-start(bf16[64,3072]{1,0:T(8,128)(2,1)} %copy-done.9) | copy-start | bytes 1179652
  89.9 16.2 %copy-start.14 = (bf16[64,3072]{1,0:T(8,128)(2,1)S(1)}, bf16[64,3072]{1,0:T(8,128)(2,1)}, u32[]{:S(2)}) copy-start(bf16[64,3072]{1,0:T(8,128)(2,1)} %copy-done.12) | copy-start | bytes 1179652
  96.1 4.8 %collective-permute-start.20 = (bf16[64,1024]{1,0:T(8,128)(2,1)S(1)}, bf16[64,1024]{1,0:T(8,128)(2,1)S(1)}, u32[]{:S(2)}, u32[]{:S(2)}) collective-permute-start(bf16[64,1024]{1,0:T(8,128)(2,1)S(1)} %get-tuple-element.5), channel_id=1, source_target_pairs={{0,1},{1,0},{2,3},{3,2},{4,5},{5,4},{6,7},{7,6},{8,9},{9,8},{10,11... | collective-permute-start | bytes 393224 | tf_op jit(solution)/shard_map/ppermute | solution.py:20
  96.1 9.7 %collective-permute-start.23 = (bf16[64,1024]{1,0:T(8,128)(2,1)S(1)}, bf16[64,1024]{1,0:T(8,128)(2,1)S(1)}, u32[]{:S(2)}, u32[]{:S(2)}) collective-permute-start(bf16[64,1024]{1,0:T(8,128)(2,1)S(1)} %get-tuple-element.6), channel_id=1, source_target_pairs={{0,8},{1,9},{2,10},{3,11},{4,12},{5,13},{6,14},{7,15},{8,0},{9,1},... | collective-permute-start | bytes 393224 | tf_op jit(solution)/shard_map/ppermute | solution.py:20
  98.4 7.6 %collective-permute-start.22 = (bf16[64,1024]{1,0:T(8,128)(2,1)S(1)}, bf16[64,1024]{1,0:T(8,128)(2,1)S(1)}, u32[]{:S(2)}, u32[]{:S(2)}) collective-permute-start(bf16[64,1024]{1,0:T(8,128)(2,1)S(1)} %get-tuple-element.7), channel_id=1, source_target_pairs={{0,4},{1,5},{2,6},{3,7},{4,0},{5,1},{6,2},{7,3},{8,12},{9,13},{10,... | collective-permute-start | bytes 393224 | tf_op jit(solution)/shard_map/ppermute | solution.py:20
  100.3 5.6 %collective-permute-start.21 = (bf16[64,1024]{1,0:T(8,128)(2,1)S(1)}, bf16[64,1024]{1,0:T(8,128)(2,1)S(1)}, u32[]{:S(2)}, u32[]{:S(2)}) collective-permute-start(bf16[64,1024]{1,0:T(8,128)(2,1)S(1)} %get-tuple-element.8), channel_id=1, source_target_pairs={{0,2},{1,3},{2,0},{3,1},{4,6},{5,7},{6,4},{7,5},{8,10},{9,11},{10,... | collective-permute-start | bytes 393224 | tf_op jit(solution)/shard_map/ppermute | solution.py:20
  (9 other events, 7.8 us)

commit v2 on v1

v2 whole, which is shorter than its diff:
```python
import functools

import jax
import jax.numpy as jnp
from jax import lax
from jax.experimental import pallas as pl
from jax.experimental.pallas import tpu as pltpu
from jax.sharding import PartitionSpec as P

HEADS = 8
HEAD = 128
BLOCK = 64
LEVELS = 4
WIDE = 256
MIB = 1024 * 1024

epsilon = 1e-06

in_vmem = pl.BlockSpec(memory_space=pltpu.VMEM)
in_smem = pl.BlockSpec(memory_space=pltpu.SMEM)
anywhere = pl.BlockSpec(memory_space=pl.ANY)


def swapped(x, axis, mask):
    return lax.ppermute(x, axis, [(i, i ^ mask) for i in range(lax.axis_size(axis))])


def from_behind(block, axis, distance):
    devices = range(lax.axis_size(axis))
    route = [(i - distance, i) for i in devices if i - distance in devices]
    return lax.ppermute(block, axis, route)


def after(x, *others):
    return lax.optimization_barrier((x, *others))[0]


def row_norm(rows, gain):
    widened = rows.astype(jnp.float32)
    mean_square = jnp.mean(widened * widened, axis=-1, keepdims=True)
    return (widened * lax.rsqrt(mean_square + epsilon) * gain).astype(jnp.bfloat16)


def head_norm(one_head):
    mean_square = jnp.mean(one_head * one_head, axis=-1, keepdims=True)
    return (one_head * lax.rsqrt(mean_square + epsilon)).astype(jnp.bfloat16)


def choose_kernel(wanted, moved_ref, arriving_ref, own_ref, *chosen):
    first = lax.axis_index("section") == 0

    @pl.when(first)
    def _():
        own_ref[...] = arriving_ref[...]

    @pl.when(jnp.logical_not(first))
    def _():
        own_ref[...] = moved_ref[...]

    shape = chosen[0].shape
    for level in range(LEVELS):
        asked = jnp.broadcast_to(wanted[level : level + 1, :1], shape)
        block = own_ref[:BLOCK].astype(jnp.float32)
        for i in range(1, own_ref.shape[0] // BLOCK):
            block = jnp.where(asked == i, own_ref[i * BLOCK : (i + 1) * BLOCK].astype(jnp.float32), block)
        chosen[level][...] = block.astype(own_ref.dtype)


def choose(wanted, moved, arriving):
    rows, width = moved.shape
    block = jax.ShapeDtypeStruct((BLOCK, width), moved.dtype)
    own, *chosen = pl.pallas_call(
        choose_kernel,
        out_shape=[jax.ShapeDtypeStruct((rows, width), moved.dtype)] + [block] * LEVELS,
        in_specs=[in_vmem] * 3,
        out_specs=[in_vmem] * (1 + LEVELS),
        compiler_params=pltpu.CompilerParams(vmem_limit_bytes=4 * MIB),
    )(wanted, moved, arriving)
    return own, chosen


def origin(behind, beside, twin):
    me = lax.axis_index("seq")
    plane = lax.rem(me // 4 + 4 - behind, 4)
    return plane * 4 + jnp.bitwise_xor(lax.rem(me, 4), 2 * beside + twin)


def assemble_kernel(places, *refs):
    pieces, (triple, sem) = refs[:-2], refs[-2:]
    rows, width = pieces[0].shape
    copies = []
    for i, (piece, hops) in enumerate(zip(pieces, places)):
        spot = pl.multiple_of(origin(*hops) * rows, rows)
        copies.append(pltpu.make_async_copy(piece, triple.at[pl.ds(spot, rows), :], sem.at[i]))
        copies[-1].start()
    spot = pl.multiple_of(origin(3, 1, 0) // 2 * (2 * rows), 2 * rows)
    triple[pl.ds(spot, 2 * rows), :] = jnp.zeros((2 * rows, width), triple.dtype)
    for copy in copies:
        copy.wait()


def assembled(pieces, places):
    rows, width = pieces[0].shape
    return pl.pallas_call(
        functools.partial(assemble_kernel, places),
        out_shape=pltpu.VMEM((rows * lax.axis_size("seq"), width), pieces[0].dtype),
        in_specs=[anywhere] * len(pieces),
        out_specs=in_vmem,
        scratch_shapes=[pltpu.SemaphoreType.DMA((len(pieces),))],
        compiler_params=pltpu.CompilerParams(vmem_limit_bytes=8 * MIB),
        cost_estimate=pl.CostEstimate(flops=0, bytes_accessed=12_000_000, transcendentals=0),
    )(*pieces)


def attend(own_ref, fars, gain_ref, triple, exit_ref, latest, put, normed, queries, keys, values, attended, last):
    inner = HEADS * HEAD
    rows = own_ref.shape[0]
    far_rows = LEVELS * BLOCK
    gain = gain_ref[...]
    normed[:rows] = row_norm(own_ref[...], gain)
    for level in range(LEVELS):
        normed[rows + level * BLOCK : rows + (level + 1) * BLOCK] = row_norm(fars[level][...], gain)
    if latest:
        part = latest[0].shape[0]
        core = lax.rem(lax.axis_index("seq"), 2)
        last[pl.ds(pl.multiple_of(core * part, part), part), :] = latest[0][...]
        last[pl.ds(pl.multiple_of((1 - core) * part, part), part), :] = latest[1][...]
        spot = pl.multiple_of(origin(3, 1, 0) // 2 * (2 * part), 2 * part)
        late_columns = normed[:, pl.ds(spot, 2 * part)]

    def projection(count, start):
        span = slice(start, start + WIDE)
        result = jnp.dot(normed[:count], triple[:, span], preferred_element_type=jnp.float32)
        if latest:
            result += jnp.dot(late_columns[:count], last[:, span], preferred_element_type=jnp.float32)
        return result

    for start in range(0, inner, WIDE):
        projected = projection(rows, start)
        for head in range(0, WIDE, HEAD):
            queries[:, start + head : start + head + HEAD] = head_norm(projected[:, head : head + HEAD])
    for start in range(0, inner, WIDE):
        projected = projection(rows + far_rows, inner + start)
        for head in range(0, WIDE, HEAD):
            keys[:, start + head : start + head + HEAD] = head_norm(projected[:, head : head + HEAD])
    for start in range(0, inner, WIDE):
        values[:, start : start + WIDE] = projection(rows + far_rows, 2 * inner + start).astype(jnp.bfloat16)
    reader = lax.broadcasted_iota(jnp.int32, (rows, rows + far_rows), 0) // BLOCK
    column = lax.broadcasted_iota(jnp.int32, (rows, rows + far_rows), 1)
    read = jnp.logical_or(column >= rows, column // BLOCK == reader)
    score_scale = HEAD ** (-0.5)
    for start in range(0, inner, HEAD):
        span = slice(start, start + HEAD)
        scores = (
            lax.dot_general(
                queries[:, span],
                keys[:, span],
                (((1,), (1,)), ((), ())),
                preferred_element_type=jnp.float32,
            )
            * score_scale
        )
        exps = jnp.where(read, jnp.exp(scores), 0.0)
        weights = (exps / jnp.sum(exps, axis=-1, keepdims=True)).astype(jnp.bfloat16)
        attended[:, span] = jnp.dot(weights, values[:, span], preferred_element_type=jnp.float32).astype(jnp.bfloat16)
    for start in range(0, own_ref.shape[1], WIDE):
        span = slice(start, start + WIDE)
        put[:, span] = (
            own_ref[:, span].astype(jnp.float32)
            + jnp.dot(attended[...], exit_ref[:, span], preferred_element_type=jnp.float32)
        ).astype(jnp.bfloat16)


def first_kernel(late, triple, own_ref, *refs):
    fars, refs = refs[:LEVELS], refs[LEVELS:]
    gain_ref, exit_ref, *refs = refs
    latest, refs = refs[:late], refs[late:]
    out_ref, *scratch = refs
    attend(own_ref, fars, gain_ref, triple, exit_ref, latest, out_ref, *scratch)


def second_kernel(late, triple, own_ref, *refs):
    fars, refs = refs[:LEVELS], refs[LEVELS:]
    gain_ref, exit_ref, *refs = refs
    latest, refs = refs[:late], refs[late:]
    first_ref, out_ref, result, sems, *scratch = refs
    early = pltpu.make_async_copy(first_ref, out_ref.at[0], sems.at[0])
    early.start()
    attend(own_ref, fars, gain_ref, triple, exit_ref, latest, result, *scratch)
    finish = pltpu.make_async_copy(result, out_ref.at[1], sems.at[1])
    finish.start()
    early.wait()
    finish.wait()


def scratch_of(rows, width, triple, latest):
    inner = HEADS * HEAD
    reach = rows + LEVELS * BLOCK
    late_rows = 2 * latest[0].shape[0] if latest else 16
    return [
        pltpu.VMEM((reach, width), jnp.bfloat16),
        pltpu.VMEM((rows, inner), jnp.bfloat16),
        pltpu.VMEM((reach, inner), jnp.bfloat16),
        pltpu.VMEM((reach, inner), jnp.bfloat16),
        pltpu.VMEM((rows, inner), jnp.bfloat16),
        pltpu.VMEM((late_rows, triple.shape[1]), jnp.bfloat16),
    ]


cost = pl.CostEstimate(flops=2_400_000_000, bytes_accessed=9_000_000, transcendentals=400_000)


def first_layer(triple, own, fars, gain, exit_matrix, latest):
    return pl.pallas_call(
        functools.partial(first_kernel, len(latest)),
        out_shape=jax.ShapeDtypeStruct(own.shape, own.dtype),
        in_specs=[in_vmem] * (4 + LEVELS + len(latest)),
        out_specs=in_vmem,
        scratch_shapes=scratch_of(*own.shape, triple, latest),
        compiler_params=pltpu.CompilerParams(vmem_limit_bytes=16 * MIB),
        cost_estimate=cost,
    )(triple, own, *fars, gain, exit_matrix, *latest)


def second_layer(triple, own, fars, gain, exit_matrix, latest, first_out):
    return pl.pallas_call(
        functools.partial(second_kernel, len(latest)),
        out_shape=jax.ShapeDtypeStruct((2,) + own.shape, own.dtype),
        in_specs=[in_vmem] * (5 + LEVELS + len(latest)),
        out_specs=anywhere,
        scratch_shapes=[pltpu.VMEM(own.shape, own.dtype), pltpu.SemaphoreType.DMA((2,))]
        + scratch_of(*own.shape, triple, latest),
        compiler_params=pltpu.CompilerParams(vmem_limit_bytes=16 * MIB),
        cost_estimate=cost,
    )(triple, own, *fars, gain, exit_matrix, *latest, first_out)


def gathered(shard, chosen):
    def around(x):
        return lax.ppermute(x, "seq", [(i, (i + 4) % 16) for i in range(16)])

    def beside(x):
        return swapped(x, "seq", 2)

    def twin(x):
        return swapped(x, "seq", 1)

    r1 = around(shard)
    x0 = beside(shard)
    c0 = twin(shard)
    r2 = around(r1)
    near = [twin(chosen[0]), beside(chosen[1])]
    x1 = beside(after(r1, near[1]))
    cr1 = twin(after(r1, near[0]))
    cx0 = twin(x0)
    r3 = around(after(r2, c0, cr1, cx0))
    x2 = beside(after(r2, c0))
    x3 = beside(r3)
    far = [swapped(after(chosen[level], r3), "seq", 1 << level) for level in (3, 2)]
    cr2 = twin(r2)
    cx1 = twin(x1)
    cr3 = twin(r3)
    cx2 = twin(x2)
    early = [
        (shard, 0, 0, 0),
        (c0, 0, 0, 1),
        (x0, 0, 1, 0),
        (cx0, 0, 1, 1),
        (r1, 1, 0, 0),
        (cr1, 1, 0, 1),
        (x1, 1, 1, 0),
        (cx1, 1, 1, 1),
        (r2, 2, 0, 0),
        (cr2, 2, 0, 1),
        (x2, 2, 1, 0),
        (cx2, 2, 1, 1),
        (r3, 3, 0, 0),
        (cr3, 3, 0, 1),
    ]
    triple = assembled([piece for piece, *_ in early], [tuple(hops) for _, *hops in early])
    return triple, [x3, twin(after(x3, triple, *far))], near + far[::-1]


def partner_rows(chosen):
    far = [swapped(chosen[level], "seq", 1 << level) for level in range(LEVELS - 1, -1, -1)]
    return far[::-1]


def per_device(resident, arriving, gain, triple, exit_matrix, lookup):
    first_in = resident[0]
    me = lax.axis_index("seq")
    levels = jnp.arange(8, dtype=jnp.int32)
    partner = jnp.bitwise_xor(me, jnp.left_shift(1, levels % LEVELS))
    wanted = jnp.broadcast_to(lookup[partner, levels % LEVELS][:, None], (8, 128))
    _, chosen = choose(wanted, first_in, first_in)
    if lax.axis_size("seq") == 16:
        triple, latest, fars = gathered(triple[0], chosen)
    else:
        triple = lax.all_gather(triple[0], "seq", axis=0, tiled=True)
        latest = []
        fars = partner_rows(chosen)
    first_out = first_layer(triple, first_in, fars, gain, exit_matrix[0], latest)
    moved = from_behind(first_out, "section", 1)
    second_in, chosen = choose(wanted, moved, arriving)
    fars = partner_rows(chosen)
    return second_layer(triple, second_in, fars, gain, exit_matrix[0], latest, first_out)[:, None]


def solution(mesh):
    placed = (
        P("section", "seq", None),
        P("seq", None),
        P("section", None),
        P("section", "seq", None),
        P("section", None, None),
        P(),
    )
    return jax.shard_map(
        per_device,
        mesh=mesh,
        in_specs=placed,
        out_specs=P(None, "section", "seq", None),
        check_vma=False,
    )
```

time: 115 us -> 86 us (0.75)
  waiting for transfers between devices: 58.9 us -> 43.8 us
  local copies, waits for them, and re-layouts: 10.7 us -> 2.84 us
  other arithmetic: 2.9 us -> 0.01 us
  between operations: 2.7 us -> 0.11 us
    ppermute x23 -> x20, waiting for transfers between devices: 53.8 us -> 17.8 us  [swapped(): lax.ppermute(x, axis, [(i, i ^ mask) for i in range(lax.axis_size(axis))])]
    ppermute x0 -> x3, waiting for transfers between devices: none -> 20.2 us  [around(): return lax.ppermute(x, 'seq', [(i, (i + 4) % 16) for i in range(16)])]
    unnamed x34 -> x14, local copies, waits for them, and re-layouts: 7.84 us -> 2.12 us
    ppermute x0 -> x3, starting transfers between devices: none -> 3.03 us  [around(): return lax.ppermute(x, 'seq', [(i, (i + 4) % 16) for i in range(16)])]
    ppermute x23 -> x20, starting transfers between devices: 20.2 us -> 17.3 us  [swapped(): lax.ppermute(x, axis, [(i, i ^ mask) for i in range(lax.axis_size(axis))])]
    dynamic_slice x3 -> x0, local copies, waits for them, and re-layouts: 2.72 us -> none  [the longest x1 1.53 us: partner_rows(): requested = lookup[partner, level]]
    pallas_call x2 -> x5, Pallas kernels: 14.5 us -> 15.3 us  [the longest x1 6.07 us: second_layer(): pl.pallas_call(functools.partial(second_kernel, len(latest)), out_shape=j...]
  transfers between devices with their start and end apart: 24 -> 24, of which waited for: 9 -> 14; matrix products, arithmetic and copies ran while one was open for 1% -> 1% of each run, Pallas kernels for 0% -> 4%
where the time goes in v2:
time: 86 us; the launch traced here: 85.8 us
  waiting for transfers between devices  43.8 us (51%)
  starting transfers between devices  23.8 us (28%)
  Pallas kernels  15.3 us (18%)
  local copies, waits for them, and re-layouts  2.84 us (3%)
    ppermute x3, waiting for transfers between devices, around(): return lax.ppermute(x, 'seq', [(i, (i + 4) % 16) for i in range(16)])  20.2 us
    ppermute x20, waiting for transfers between devices, swapped(): lax.ppermute(x, axis, [(i, i ^ mask) for i in range(lax.axis_size(axis))])  17.8 us
    ppermute x20, starting transfers between devices, swapped(): lax.ppermute(x, axis, [(i, i ^ mask) for i in range(lax.axis_size(axis))])  17.3 us
    pallas_call x1, Pallas kernels, second_layer(): pl.pallas_call(functools.partial(second_kernel, len(latest)), out_shape=j...  6.07 us
    ppermute x1, waiting for transfers between devices, from_behind(): return lax.ppermute(block, axis, route)  5.83 us
    pallas_call x1, Pallas kernels, first_layer(): pl.pallas_call(functools.partial(first_kernel, len(latest)), out_shape=ja...  5.36 us
    ppermute x1, starting transfers between devices, from_behind(): return lax.ppermute(block, axis, route)  3.44 us
    ppermute x3, starting transfers between devices, around(): return lax.ppermute(x, 'seq', [(i, (i + 4) % 16) for i in range(16)])  3.03 us
  transfers between devices with their start and end apart: 24, of which 14 were waited for; matrix products, arithmetic and copies ran while one was open for 1% of the time, Pallas kernels for 4%

profile of v2, /device:TPU:0, one launch (start us, length us, event | category | flops | bytes accessed | tf_op | source)
XLA Modules:
  0.0 85.8 jit_solution(1678982968870423159)
XLA Ops:
  0.0 3.0 %collective-permute-start.3 = (bf16[64,3072]{1,0:T(8,128)(2,1)}, bf16[64,3072]{1,0:T(8,128)(2,1)S(1)}, u32[]{:S(2)}, u32[]{:S(2)}) collective-permute-start(bf16[64,3072]{1,0:T(8,128)(2,1)} %bitcast.13), channel_id=1, source_target_pairs={{0,4},{1,5},{2,6},{3,7},{4,8},{5,9},{6,10},{7,11},{8,12},{9,13},{1... | collective-permute-start | bytes 1179656 | tf_op jit(solution)/shard_map/ppermute | solution.py:240
  3.0 1.5 %collective-permute-start.1 = (bf16[64,3072]{1,0:T(8,128)(2,1)}, bf16[64,3072]{1,0:T(8,128)(2,1)S(1)}, u32[]{:S(2)}, u32[]{:S(2)}) collective-permute-start(bf16[64,3072]{1,0:T(8,128)(2,1)} %bitcast.14), channel_id=1, source_target_pairs={{0,2},{1,3},{2,0},{3,1},{4,6},{5,7},{6,4},{7,5},{8,10},{9,11},{10,... | collective-permute-start | bytes 1179656 | tf_op jit(solution)/shard_map/ppermute | solution.py:25
  4.6 0.7 gather_fusion
  5.3 1.1 %copy-done.2 = bf16[1,128,1024]{2,1,0:T(8,128)(2,1)S(1)} copy-done((bf16[1,128,1024]{2,1,0:T(8,128)(2,1)S(1)}, bf16[1,128,1024]{2,1,0:T(8,128)(2,1)}, u32[]{:S(2)}) %copy-start.2) | copy-done | bytes 262168
  6.4 0.7 shard_map.64
  7.1 0.5 collective-permute-start
  7.6 1.0 %collective-permute-done.4.refs_0_ = bf16[64,1024]{1,0:T(8,128)(2,1)S(1)} collective-permute-done((bf16[64,1024]{1,0:T(8,128)(2,1)S(1)}, bf16[64,1024]{1,0:T(8,128)(2,1)S(1)}, u32[]{:S(2)}, u32[]{:S(2)}) %collective-permute-start.4) | collective-permute-done | bytes 131104 | tf_op jit(solution)/shard_map/ppermute | solution.py:25
  8.6 5.7 %collective-permute-done.3.refs_4_ = bf16[64,3072]{1,0:T(8,128)(2,1)S(1)} collective-permute-done((bf16[64,3072]{1,0:T(8,128)(2,1)}, bf16[64,3072]{1,0:T(8,128)(2,1)S(1)}, u32[]{:S(2)}, u32[]{:S(2)}) %collective-permute-start.3) | collective-permute-done | bytes 393248 | tf_op jit(solution)/shard_map/ppermute | solution.py:240
  14.9 1.5 %collective-permute-start.6 = (bf16[64,1024]{1,0:T(8,128)(2,1)S(1)}, bf16[64,1024]{1,0:T(8,128)(2,1)S(1)}, u32[]{:S(2)}, u32[]{:S(2)}) collective-permute-start(bf16[64,1024]{1,0:T(8,128)(2,1)S(1)} %get-tuple-element.23), channel_id=1, source_target_pairs={{0,2},{1,3},{2,0},{3,1},{4,6},{5,7},{6,4},{7,5},{8,10},{9,11},{10,... | collective-permute-start | bytes 393224 | tf_op jit(solution)/shard_map/ppermute | solution.py:25
  16.4 4.0 %collective-permute-done.6.refs_1_ = bf16[64,1024]{1,0:T(8,128)(2,1)S(1)} collective-permute-done((bf16[64,1024]{1,0:T(8,128)(2,1)S(1)}, bf16[64,1024]{1,0:T(8,128)(2,1)S(1)}, u32[]{:S(2)}, u32[]{:S(2)}) %collective-permute-start.6) | collective-permute-done | bytes 131104 | tf_op jit(solution)/shard_map/ppermute | solution.py:25
  20.4 1.5 %collective-permute-start.7 = (bf16[64,3072]{1,0:T(8,128)(2,1)S(1)}, bf16[64,3072]{1,0:T(8,128)(2,1)S(1)}, u32[]{:S(2)}, u32[]{:S(2)}) collective-permute-start(bf16[64,3072]{1,0:T(8,128)(2,1)S(1)} %collective-permute-done.3.refs_4_), channel_id=1, source_target_pairs={{0,2},{1,3},{2,0},{3,1},{4,6},{5,7},{6,4},{7,5},{8,10},{9,11},{10,... | collective-permute-start | bytes 1179656 | tf_op jit(solution)/shard_map/ppermute | solution.py:25
  21.9 5.8 %collective-permute-done.9.refs_8_ = bf16[64,3072]{1,0:T(8,128)(2,1)S(1)} collective-permute-done((bf16[64,3072]{1,0:T(8,128)(2,1)S(1)}, bf16[64,3072]{1,0:T(8,128)(2,1)S(1)}, u32[]{:S(2)}, u32[]{:S(2)}) %collective-permute-start.9) | collective-permute-done | bytes 393248 | tf_op jit(solution)/shard_map/ppermute | solution.py:240
  27.7 1.5 %collective-permute-start.11 = (bf16[64,3072]{1,0:T(8,128)(2,1)S(1)}, bf16[64,3072]{1,0:T(8,128)(2,1)S(1)}, u32[]{:S(2)}, u32[]{:S(2)}) collective-permute-start(bf16[64,3072]{1,0:T(8,128)(2,1)S(1)} %collective-permute-done.9.refs_8_), channel_id=1, source_target_pairs={{0,2},{1,3},{2,0},{3,1},{4,6},{5,7},{6,4},{7,5},{8,10},{9,11},{10,... | collective-permute-start | bytes 1179656 | tf_op jit(solution)/shard_map/ppermute | solution.py:25
  29.2 1.9 %collective-permute-done.7.refs_6_ = bf16[64,3072]{1,0:T(8,128)(2,1)S(1)} collective-permute-done((bf16[64,3072]{1,0:T(8,128)(2,1)S(1)}, bf16[64,3072]{1,0:T(8,128)(2,1)S(1)}, u32[]{:S(2)}, u32[]{:S(2)}) %collective-permute-start.7) | collective-permute-done | bytes 393248 | tf_op jit(solution)/shard_map/ppermute | solution.py:25
  31.7 8.6 %collective-permute-done.13.refs_12_ = bf16[64,3072]{1,0:T(8,128)(2,1)S(1)} collective-permute-done((bf16[64,3072]{1,0:T(8,128)(2,1)S(1)}, bf16[64,3072]{1,0:T(8,128)(2,1)S(1)}, u32[]{:S(2)}, u32[]{:S(2)}) %collective-permute-start.13) | collective-permute-done | bytes 393248 | tf_op jit(solution)/shard_map/ppermute | solution.py:240
  40.3 0.5 collective-permute-start.12
  40.8 1.5 %collective-permute-start.17 = (bf16[64,3072]{1,0:T(8,128)(2,1)S(1)}, bf16[64,3072]{1,0:T(8,128)(2,1)S(1)}, u32[]{:S(2)}, u32[]{:S(2)}) collective-permute-start(bf16[64,3072]{1,0:T(8,128)(2,1)S(1)} %collective-permute-done.13.refs_12_), channel_id=1, source_target_pairs={{0,2},{1,3},{2,0},{3,1},{4,6},{5,7},{6,4},{7,5},{8,10},{9,11},{10,... | collective-permute-start | bytes 1179656 | tf_op jit(solution)/shard_map/ppermute | solution.py:25
  42.3 2.8 %collective-permute-start.16 = (bf16[64,1024]{1,0:T(8,128)(2,1)S(1)}, bf16[64,1024]{1,0:T(8,128)(2,1)S(1)}, u32[]{:S(2)}, u32[]{:S(2)}) collective-permute-start(bf16[64,1024]{1,0:T(8,128)(2,1)S(1)} %get-tuple-element.30), channel_id=1, source_target_pairs={{0,8},{1,9},{2,10},{3,11},{4,12},{5,13},{6,14},{7,15},{8,0},{9,1},... | collective-permute-start | bytes 393224 | tf_op jit(solution)/shard_map/ppermute | solution.py:25
  45.1 1.0 %copy-done.4 = bf16[1,64,3072]{2,1,0:T(8,128)(2,1)S(1)} copy-done((bf16[1,64,3072]{2,1,0:T(8,128)(2,1)S(1)}, bf16[1,64,3072]{2,1,0:T(8,128)(2,1)}, u32[]{:S(2)}) %copy-start.4) | copy-done | bytes 393240
  46.1 3.0 %shard_map.65.triple = bf16[1024,3072]{1,0:T(8,128)(2,1)S(1)} custom-call(bf16[64,3072]{1,0:T(8,128)(2,1)S(1)} %bitcast.16, bf16[64,3072]{1,0:T(8,128)(2,1)S(1)} %collective-permute-done.refs_1_, bf16[64,3072]{1,0:T(8,128)(2,1)S(1)} %collective-permute-done.1.refs_2_, bf16[64,3072]{1,0:T(8,128)(2,1)S(1)} %collective-permute-done.2.refs_3_, ...), custom_call_target="tpu_custom_call" | custom-call | bytes 12000000 | tf_op jit(solution)/shard_map/pallas_call | solution.py:104
  49.1 0.9 %collective-permute-done.15.refs_2_ = bf16[64,1024]{1,0:T(8,128)(2,1)S(1)} collective-permute-done((bf16[64,1024]{1,0:T(8,128)(2,1)S(1)}, bf16[64,1024]{1,0:T(8,128)(2,1)S(1)}, u32[]{:S(2)}, u32[]{:S(2)}) %collective-permute-start.15) | collective-permute-done | bytes 131104 | tf_op jit(solution)/shard_map/ppermute | solution.py:25
  50.0 1.6 %collective-permute-done.16.refs_3_ = bf16[64,1024]{1,0:T(8,128)(2,1)S(1)} collective-permute-done((bf16[64,1024]{1,0:T(8,128)(2,1)S(1)}, bf16[64,1024]{1,0:T(8,128)(2,1)S(1)}, u32[]{:S(2)}, u32[]{:S(2)}) %collective-permute-start.16) | collective-permute-done | bytes 131104 | tf_op jit(solution)/shard_map/ppermute | solution.py:25
  51.8 1.7 %collective-permute-done.18.refs_7_ = bf16[64,3072]{1,0:T(8,128)(2,1)S(1)} collective-permute-done((bf16[64,3072]{1,0:T(8,128)(2,1)S(1)}, bf16[64,3072]{1,0:T(8,128)(2,1)S(1)}, u32[]{:S(2)}, u32[]{:S(2)}) %collective-permute-start.18) | collective-permute-done | bytes 393248 | tf_op jit(solution)/shard_map/ppermute | solution.py:25
  53.5 5.4 %shard_map.66.refs_8_ = bf16[128,1024]{1,0:T(8,128)(2,1)S(1)} custom-call(bf16[1024,3072]{1,0:T(8,128)(2,1)S(1)} %shard_map.65.triple, bf16[128,1024]{1,0:T(8,128)(2,1)S(1)} %bitcast.12, bf16[64,1024]{1,0:T(8,128)(2,1)S(1)} %collective-permute-done.4.refs_0_, bf16[64,1024]{1,0:T(8,128)(2,1)S(1)} %collective-permute-done.6.refs_1_, ...), custom_call_target="tpu_custom_call" | custom-call | flops 2400000000 | bytes 9000000 | tf_op jit(solution)/shard_map/pallas_call | solution.py:214
  58.9 3.4 %collective-permute-start.19 = (bf16[128,1024]{1,0:T(8,128)(2,1)S(1)}, bf16[128,1024]{1,0:T(8,128)(2,1)S(1)}, u32[]{:S(2)}, u32[]{:S(2)}) collective-permute-start(bf16[128,1024]{1,0:T(8,128)(2,1)S(1)} %shard_map.66.refs_8_), channel_id=1, source_target_pairs={{0,16},{1,17},{2,18},{3,19},{4,20},{5,21},{6,22},{7,23},{8,24},{9,... | collective-permute-start | bytes 786440 | tf_op jit(solution)/shard_map/ppermute | solution.py:31
  62.3 5.8 %collective-permute-done.19.moved_ref = bf16[128,1024]{1,0:T(8,128)(2,1)S(1)} collective-permute-done((bf16[128,1024]{1,0:T(8,128)(2,1)S(1)}, bf16[128,1024]{1,0:T(8,128)(2,1)S(1)}, u32[]{:S(2)}, u32[]{:S(2)}) %collective-permute-start.19) | collective-permute-done | bytes 262176 | tf_op jit(solution)/shard_map/ppermute | solution.py:31
  68.4 1.6 %collective-permute-start.21 = (bf16[64,1024]{1,0:T(8,128)(2,1)S(1)}, bf16[64,1024]{1,0:T(8,128)(2,1)S(1)}, u32[]{:S(2)}, u32[]{:S(2)}) collective-permute-start(bf16[64,1024]{1,0:T(8,128)(2,1)S(1)} %get-tuple-element.34), channel_id=1, source_target_pairs={{0,2},{1,3},{2,0},{3,1},{4,6},{5,7},{6,4},{7,5},{8,10},{9,11},{10,... | collective-permute-start | bytes 393224 | tf_op jit(solution)/shard_map/ppermute | solution.py:25
  70.2 3.1 %collective-permute-start.23 = (bf16[64,1024]{1,0:T(8,128)(2,1)S(1)}, bf16[64,1024]{1,0:T(8,128)(2,1)S(1)}, u32[]{:S(2)}, u32[]{:S(2)}) collective-permute-start(bf16[64,1024]{1,0:T(8,128)(2,1)S(1)} %get-tuple-element.36), channel_id=1, source_target_pairs={{0,8},{1,9},{2,10},{3,11},{4,12},{5,13},{6,14},{7,15},{8,0},{9,1},... | collective-permute-start | bytes 393224 | tf_op jit(solution)/shard_map/ppermute | solution.py:25
  73.3 1.0 %collective-permute-done.21.refs_1_ = bf16[64,1024]{1,0:T(8,128)(2,1)S(1)} collective-permute-done((bf16[64,1024]{1,0:T(8,128)(2,1)S(1)}, bf16[64,1024]{1,0:T(8,128)(2,1)S(1)}, u32[]{:S(2)}, u32[]{:S(2)}) %collective-permute-start.21) | collective-permute-done | bytes 131104 | tf_op jit(solution)/shard_map/ppermute | solution.py:25
  74.4 3.8 %collective-permute-done.22.refs_2_ = bf16[64,1024]{1,0:T(8,128)(2,1)S(1)} collective-permute-done((bf16[64,1024]{1,0:T(8,128)(2,1)S(1)}, bf16[64,1024]{1,0:T(8,128)(2,1)S(1)}, u32[]{:S(2)}, u32[]{:S(2)}) %collective-permute-start.22) | collective-permute-done | bytes 131104 | tf_op jit(solution)/shard_map/ppermute | solution.py:25
  78.2 1.6 %collective-permute-done.23.refs_3_ = bf16[64,1024]{1,0:T(8,128)(2,1)S(1)} collective-permute-done((bf16[64,1024]{1,0:T(8,128)(2,1)S(1)}, bf16[64,1024]{1,0:T(8,128)(2,1)S(1)}, u32[]{:S(2)}, u32[]{:S(2)}) %collective-permute-start.23) | collective-permute-done | bytes 131104 | tf_op jit(solution)/shard_map/ppermute | solution.py:25
  79.7 6.1 %shard_map.68 = bf16[2,128,1024]{2,1,0:T(8,128)(2,1)} custom-call(bf16[1024,3072]{1,0:T(8,128)(2,1)S(1)} %shard_map.65.triple, bf16[128,1024]{1,0:T(8,128)(2,1)S(1)} %get-tuple-element.32.own_ref, bf16[64,1024]{1,0:T(8,128)(2,1)S(1)} %collective-permute-done.20.refs_0_, bf16[64,1024]{1,0:T(8,128)(2,1)S(1)} %collective-permute-done.21.refs_1_, ...), custom_call_target="tpu_custom_call" | custom-call | flops 2400000000 | bytes 9000000 | tf_op jit(solution)/shard_map/pallas_call | solution.py:226
  (38 shorter events, 1.9 us)
Async XLA Ops:
  0.0 4.5 %copy-start = (s32[16,4]{0,1:T(4,128)S(1)}, s32[16,4]{0,1:T(4,128)}, u32[]{:S(2)}) copy-start(s32[16,4]{0,1:T(4,128)} %param.11) | copy-start | bytes 772
  0.0 14.4 %collective-permute-start.3 = (bf16[64,3072]{1,0:T(8,128)(2,1)}, bf16[64,3072]{1,0:T(8,128)(2,1)S(1)}, u32[]{:S(2)}, u32[]{:S(2)}) collective-permute-start(bf16[64,3072]{1,0:T(8,128)(2,1)} %bitcast.13), channel_id=1, source_target_pairs={{0,4},{1,5},{2,6},{3,7},{4,8},{5,9},{6,10},{7,11},{8,12},{9,13},{1... | collective-permute-start | bytes 1179656 | tf_op jit(solution)/shard_map/ppermute | solution.py:240
  3.0 11.4 %collective-permute-start.1 = (bf16[64,3072]{1,0:T(8,128)(2,1)}, bf16[64,3072]{1,0:T(8,128)(2,1)S(1)}, u32[]{:S(2)}, u32[]{:S(2)}) collective-permute-start(bf16[64,3072]{1,0:T(8,128)(2,1)} %bitcast.14), channel_id=1, source_target_pairs={{0,2},{1,3},{2,0},{3,1},{4,6},{5,7},{6,4},{7,5},{8,10},{9,11},{10,... | collective-permute-start | bytes 1179656 | tf_op jit(solution)/shard_map/ppermute | solution.py:25
  4.5 49.0 %copy-start.3 = (bf16[1,128,1024]{2,1,0:T(8,128)(2,1)S(1)}, bf16[1,128,1024]{2,1,0:T(8,128)(2,1)}, u32[]{:S(2)}) copy-start(bf16[1,128,1024]{2,1,0:T(8,128)(2,1)} %param.6) | copy-start | bytes 786436
  4.6 49.0 %copy-start.6 = (f32[1,1024]{1,0:T(1,128)S(1)}, f32[1,1024]{1,0:T(1,128)}, u32[]{:S(2)}) copy-start(f32[1,1024]{1,0:T(1,128)} %refs_4_.3) | copy-start | bytes 12292
  5.2 48.3 %copy-start.1 = (bf16[1,1024,1024]{2,1,0:T(8,128)(2,1)S(1)}, bf16[1,1024,1024]{2,1,0:T(8,128)(2,1)}, u32[]{:S(2)}) copy-start(bf16[1,1024,1024]{2,1,0:T(8,128)(2,1)} %param.10) | copy-start | bytes 6291460
  5.3 1.1 %copy-start.2 = (bf16[1,128,1024]{2,1,0:T(8,128)(2,1)S(1)}, bf16[1,128,1024]{2,1,0:T(8,128)(2,1)}, u32[]{:S(2)}) copy-start(bf16[1,128,1024]{2,1,0:T(8,128)(2,1)} %param.6) | copy-start | bytes 786436
  7.1 1.5 %collective-permute-start.4 = (bf16[64,1024]{1,0:T(8,128)(2,1)S(1)}, bf16[64,1024]{1,0:T(8,128)(2,1)S(1)}, u32[]{:S(2)}, u32[]{:S(2)}) collective-permute-start(bf16[64,1024]{1,0:T(8,128)(2,1)S(1)} %get-tuple-element.21), channel_id=1, source_target_pairs={{0,1},{1,0},{2,3},{3,2},{4,5},{5,4},{6,7},{7,6},{8,9},{9,8},{10,11... | collective-permute-start | bytes 393224 | tf_op jit(solution)/shard_map/ppermute | solution.py:25
  7.1 14.7 %collective-permute-start = (bf16[64,3072]{1,0:T(8,128)(2,1)}, bf16[64,3072]{1,0:T(8,128)(2,1)S(1)}, u32[]{:S(2)}, u32[]{:S(2)}) collective-permute-start(bf16[64,3072]{1,0:T(8,128)(2,1)} %bitcast.15), channel_id=1, source_target_pairs={{0,1},{1,0},{2,3},{3,2},{4,5},{5,4},{6,7},{7,6},{8,9},{9,8},{10,11... | collective-permute-start | bytes 1179656 | tf_op jit(solution)/shard_map/ppermute | solution.py:25
  14.4 7.5 %collective-permute-start.5 = (bf16[64,3072]{1,0:T(8,128)(2,1)S(1)}, bf16[64,3072]{1,0:T(8,128)(2,1)S(1)}, u32[]{:S(2)}, u32[]{:S(2)}) collective-permute-start(bf16[64,3072]{1,0:T(8,128)(2,1)S(1)} %collective-permute-done.3.refs_4_), channel_id=1, source_target_pairs={{0,1},{1,0},{2,3},{3,2},{4,5},{5,4},{6,7},{7,6},{8,9},{9,8},{10,11... | collective-permute-start | bytes 1179656 | tf_op jit(solution)/shard_map/ppermute | solution.py:25
  14.4 13.3 %collective-permute-start.9 = (bf16[64,3072]{1,0:T(8,128)(2,1)S(1)}, bf16[64,3072]{1,0:T(8,128)(2,1)S(1)}, u32[]{:S(2)}, u32[]{:S(2)}) collective-permute-start(bf16[64,3072]{1,0:T(8,128)(2,1)S(1)} %collective-permute-done.3.refs_4_), channel_id=1, source_target_pairs={{0,4},{1,5},{2,6},{3,7},{4,8},{5,9},{6,10},{7,11},{8,12},{9,13},{1... | collective-permute-start | bytes 1179656 | tf_op jit(solution)/shard_map/ppermute | solution.py:240
  14.4 13.3 %collective-permute-start.2 = (bf16[64,3072]{1,0:T(8,128)(2,1)S(1)}, bf16[64,3072]{1,0:T(8,128)(2,1)S(1)}, u32[]{:S(2)}, u32[]{:S(2)}) collective-permute-start(bf16[64,3072]{1,0:T(8,128)(2,1)S(1)} %collective-permute-done.1.refs_2_), channel_id=1, source_target_pairs={{0,1},{1,0},{2,3},{3,2},{4,5},{5,4},{6,7},{7,6},{8,9},{9,8},{10,11... | collective-permute-start | bytes 1179656 | tf_op jit(solution)/shard_map/ppermute | solution.py:25
  14.9 5.5 %collective-permute-start.6 = (bf16[64,1024]{1,0:T(8,128)(2,1)S(1)}, bf16[64,1024]{1,0:T(8,128)(2,1)S(1)}, u32[]{:S(2)}, u32[]{:S(2)}) collective-permute-start(bf16[64,1024]{1,0:T(8,128)(2,1)S(1)} %get-tuple-element.23), channel_id=1, source_target_pairs={{0,2},{1,3},{2,0},{3,1},{4,6},{5,7},{6,4},{7,5},{8,10},{9,11},{10,... | collective-permute-start | bytes 393224 | tf_op jit(solution)/shard_map/ppermute | solution.py:25
  20.4 10.8 %collective-permute-start.7 = (bf16[64,3072]{1,0:T(8,128)(2,1)S(1)}, bf16[64,3072]{1,0:T(8,128)(2,1)S(1)}, u32[]{:S(2)}, u32[]{:S(2)}) collective-permute-start(bf16[64,3072]{1,0:T(8,128)(2,1)S(1)} %collective-permute-done.3.refs_4_), channel_id=1, source_target_pairs={{0,2},{1,3},{2,0},{3,1},{4,6},{5,7},{6,4},{7,5},{8,10},{9,11},{10,... | collective-permute-start | bytes 1179656 | tf_op jit(solution)/shard_map/ppermute | solution.py:25
  27.7 12.5 %collective-permute-start.13 = (bf16[64,3072]{1,0:T(8,128)(2,1)S(1)}, bf16[64,3072]{1,0:T(8,128)(2,1)S(1)}, u32[]{:S(2)}, u32[]{:S(2)}) collective-permute-start(bf16[64,3072]{1,0:T(8,128)(2,1)S(1)} %collective-permute-done.9.refs_8_), channel_id=1, source_target_pairs={{0,4},{1,5},{2,6},{3,7},{4,8},{5,9},{6,10},{7,11},{8,12},{9,13},{1... | collective-permute-start | bytes 1179656 | tf_op jit(solution)/shard_map/ppermute | solution.py:240
  27.7 12.5 %collective-permute-start.11 = (bf16[64,3072]{1,0:T(8,128)(2,1)S(1)}, bf16[64,3072]{1,0:T(8,128)(2,1)S(1)}, u32[]{:S(2)}, u32[]{:S(2)}) collective-permute-start(bf16[64,3072]{1,0:T(8,128)(2,1)S(1)} %collective-permute-done.9.refs_8_), channel_id=1, source_target_pairs={{0,2},{1,3},{2,0},{3,1},{4,6},{5,7},{6,4},{7,5},{8,10},{9,11},{10,... | collective-permute-start | bytes 1179656 | tf_op jit(solution)/shard_map/ppermute | solution.py:25
  31.1 11.1 %collective-permute-start.8 = (bf16[64,3072]{1,0:T(8,128)(2,1)S(1)}, bf16[64,3072]{1,0:T(8,128)(2,1)S(1)}, u32[]{:S(2)}, u32[]{:S(2)}) collective-permute-start(bf16[64,3072]{1,0:T(8,128)(2,1)S(1)} %collective-permute-done.7.refs_6_), channel_id=1, source_target_pairs={{0,1},{1,0},{2,3},{3,2},{4,5},{5,4},{6,7},{7,6},{8,9},{9,8},{10,11... | collective-permute-start | bytes 1179656 | tf_op jit(solution)/shard_map/ppermute | solution.py:25
  31.1 11.1 %collective-permute-start.10 = (bf16[64,3072]{1,0:T(8,128)(2,1)S(1)}, bf16[64,3072]{1,0:T(8,128)(2,1)S(1)}, u32[]{:S(2)}, u32[]{:S(2)}) collective-permute-start(bf16[64,3072]{1,0:T(8,128)(2,1)S(1)} %collective-permute-done.9.refs_8_), channel_id=1, source_target_pairs={{0,1},{1,0},{2,3},{3,2},{4,5},{5,4},{6,7},{7,6},{8,9},{9,8},{10,11... | collective-permute-start | bytes 1179656 | tf_op jit(solution)/shard_map/ppermute | solution.py:25
  40.3 4.9 %collective-permute-start.14 = (bf16[64,3072]{1,0:T(8,128)(2,1)S(1)}, bf16[64,3072]{1,0:T(8,128)(2,1)S(1)}, u32[]{:S(2)}, u32[]{:S(2)}) collective-permute-start(bf16[64,3072]{1,0:T(8,128)(2,1)S(1)} %collective-permute-done.13.refs_12_), channel_id=1, source_target_pairs={{0,1},{1,0},{2,3},{3,2},{4,5},{5,4},{6,7},{7,6},{8,9},{9,8},{10,11... | collective-permute-start | bytes 1179656 | tf_op jit(solution)/shard_map/ppermute | solution.py:25
  40.3 4.8 %collective-permute-start.12 = (bf16[64,3072]{1,0:T(8,128)(2,1)S(1)}, bf16[64,3072]{1,0:T(8,128)(2,1)S(1)}, u32[]{:S(2)}, u32[]{:S(2)}) collective-permute-start(bf16[64,3072]{1,0:T(8,128)(2,1)S(1)} %collective-permute-done.11.refs_10_), channel_id=1, source_target_pairs={{0,1},{1,0},{2,3},{3,2},{4,5},{5,4},{6,7},{7,6},{8,9},{9,8},{10,11... | collective-permute-start | bytes 1179656 | tf_op jit(solution)/shard_map/ppermute | solution.py:25
  40.8 11.0 %collective-permute-start.17 = (bf16[64,3072]{1,0:T(8,128)(2,1)S(1)}, bf16[64,3072]{1,0:T(8,128)(2,1)S(1)}, u32[]{:S(2)}, u32[]{:S(2)}) collective-permute-start(bf16[64,3072]{1,0:T(8,128)(2,1)S(1)} %collective-permute-done.13.refs_12_), channel_id=1, source_target_pairs={{0,2},{1,3},{2,0},{3,1},{4,6},{5,7},{6,4},{7,5},{8,10},{9,11},{10,... | collective-permute-start | bytes 1179656 | tf_op jit(solution)/shard_map/ppermute | solution.py:25
  42.3 7.7 %collective-permute-start.15 = (bf16[64,1024]{1,0:T(8,128)(2,1)S(1)}, bf16[64,1024]{1,0:T(8,128)(2,1)S(1)}, u32[]{:S(2)}, u32[]{:S(2)}) collective-permute-start(bf16[64,1024]{1,0:T(8,128)(2,1)S(1)} %get-tuple-element.28), channel_id=1, source_target_pairs={{0,4},{1,5},{2,6},{3,7},{4,0},{5,1},{6,2},{7,3},{8,12},{9,13},{10,... | collective-permute-start | bytes 393224 | tf_op jit(solution)/shard_map/ppermute | solution.py:25
  42.3 9.3 %collective-permute-start.16 = (bf16[64,1024]{1,0:T(8,128)(2,1)S(1)}, bf16[64,1024]{1,0:T(8,128)(2,1)S(1)}, u32[]{:S(2)}, u32[]{:S(2)}) collective-permute-start(bf16[64,1024]{1,0:T(8,128)(2,1)S(1)} %get-tuple-element.30), channel_id=1, source_target_pairs={{0,8},{1,9},{2,10},{3,11},{4,12},{5,13},{6,14},{7,15},{8,0},{9,1},... | collective-permute-start | bytes 393224 | tf_op jit(solution)/shard_map/ppermute | solution.py:25
  45.1 1.0 %copy-start.4 = (bf16[1,64,3072]{2,1,0:T(8,128)(2,1)S(1)}, bf16[1,64,3072]{2,1,0:T(8,128)(2,1)}, u32[]{:S(2)}) copy-start(bf16[1,64,3072]{2,1,0:T(8,128)(2,1)} %param.9) | copy-start | bytes 1179652
  49.1 19.1 %copy-start.5 = (bf16[128,1024]{1,0:T(8,128)(2,1)S(1)}, bf16[128,1024]{1,0:T(8,128)(2,1)}, u32[]{:S(2)}) copy-start(bf16[128,1024]{1,0:T(8,128)(2,1)} %arriving_ref.1) | copy-start | bytes 786436
  51.8 1.7 %collective-permute-start.18 = (bf16[64,3072]{1,0:T(8,128)(2,1)S(1)}, bf16[64,3072]{1,0:T(8,128)(2,1)S(1)}, u32[]{:S(2)}, u32[]{:S(2)}) collective-permute-start(bf16[64,3072]{1,0:T(8,128)(2,1)S(1)} %collective-permute-done.17.refs_6_), channel_id=1, source_target_pairs={{0,1},{1,0},{2,3},{3,2},{4,5},{5,4},{6,7},{7,6},{8,9},{9,8},{10,11... | collective-permute-start | bytes 1179656 | tf_op jit(solution)/shard_map/ppermute | solution.py:25
  58.9 9.3 %collective-permute-start.19 = (bf16[128,1024]{1,0:T(8,128)(2,1)S(1)}, bf16[128,1024]{1,0:T(8,128)(2,1)S(1)}, u32[]{:S(2)}, u32[]{:S(2)}) collective-permute-start(bf16[128,1024]{1,0:T(8,128)(2,1)S(1)} %shard_map.66.refs_8_), channel_id=1, source_target_pairs={{0,16},{1,17},{2,18},{3,19},{4,20},{5,21},{6,22},{7,23},{8,24},{9,... | collective-permute-start | bytes 786440 | tf_op jit(solution)/shard_map/ppermute | solution.py:31
  68.4 5.0 %collective-permute-start.20 = (bf16[64,1024]{1,0:T(8,128)(2,1)S(1)}, bf16[64,1024]{1,0:T(8,128)(2,1)S(1)}, u32[]{:S(2)}, u32[]{:S(2)}) collective-permute-start(bf16[64,1024]{1,0:T(8,128)(2,1)S(1)} %get-tuple-element.33), channel_id=1, source_target_pairs={{0,1},{1,0},{2,3},{3,2},{4,5},{5,4},{6,7},{7,6},{8,9},{9,8},{10,11... | collective-permute-start | bytes 393224 | tf_op jit(solution)/shard_map/ppermute | solution.py:25
  68.4 5.9 %collective-permute-start.21 = (bf16[64,1024]{1,0:T(8,128)(2,1)S(1)}, bf16[64,1024]{1,0:T(8,128)(2,1)S(1)}, u32[]{:S(2)}, u32[]{:S(2)}) collective-permute-start(bf16[64,1024]{1,0:T(8,128)(2,1)S(1)} %get-tuple-element.34), channel_id=1, source_target_pairs={{0,2},{1,3},{2,0},{3,1},{4,6},{5,7},{6,4},{7,5},{8,10},{9,11},{10,... | collective-permute-start | bytes 393224 | tf_op jit(solution)/shard_map/ppermute | solution.py:25
  70.0 8.2 %collective-permute-start.22 = (bf16[64,1024]{1,0:T(8,128)(2,1)S(1)}, bf16[64,1024]{1,0:T(8,128)(2,1)S(1)}, u32[]{:S(2)}, u32[]{:S(2)}) collective-permute-start(bf16[64,1024]{1,0:T(8,128)(2,1)S(1)} %get-tuple-element.35), channel_id=1, source_target_pairs={{0,4},{1,5},{2,6},{3,7},{4,0},{5,1},{6,2},{7,3},{8,12},{9,13},{10,... | collective-permute-start | bytes 393224 | tf_op jit(solution)/shard_map/ppermute | solution.py:25
  70.2 9.5 %collective-permute-start.23 = (bf16[64,1024]{1,0:T(8,128)(2,1)S(1)}, bf16[64,1024]{1,0:T(8,128)(2,1)S(1)}, u32[]{:S(2)}, u32[]{:S(2)}) collective-permute-start(bf16[64,1024]{1,0:T(8,128)(2,1)S(1)} %get-tuple-element.36), channel_id=1, source_target_pairs={{0,8},{1,9},{2,10},{3,11},{4,12},{5,13},{6,14},{7,15},{8,0},{9,1},... | collective-permute-start | bytes 393224 | tf_op jit(solution)/shard_map/ppermute | solution.py:25

commit v3 on v2

--- a/solution.py
+++ b/solution.py
@@ -1,4 +1,5 @@
 import functools
+import math
 
 import jax
 import jax.numpy as jnp
@@ -81,7 +82,9 @@
 
 def origin(behind, beside, twin):
     me = lax.axis_index("seq")
-    plane = lax.rem(me // 4 + 4 - behind, 4)
+    plane = me // 4
+    spot = jnp.bitwise_and(jnp.bitwise_xor(plane, plane // 2) + 4 - behind, 3)
+    plane = jnp.bitwise_xor(spot, spot // 2)
     return plane * 4 + jnp.bitwise_xor(lax.rem(me, 4), 2 * beside + twin)
 
 
@@ -145,24 +148,25 @@
             keys[:, start + head : start + head + HEAD] = head_norm(projected[:, head : head + HEAD])
     for start in range(0, inner, WIDE):
         values[:, start : start + WIDE] = projection(rows + far_rows, 2 * inner + start).astype(jnp.bfloat16)
-    reader = lax.broadcasted_iota(jnp.int32, (rows, rows + far_rows), 0) // BLOCK
-    column = lax.broadcasted_iota(jnp.int32, (rows, rows + far_rows), 1)
-    read = jnp.logical_or(column >= rows, column // BLOCK == reader)
-    score_scale = HEAD ** (-0.5)
-    for start in range(0, inner, HEAD):
-        span = slice(start, start + HEAD)
-        scores = (
-            lax.dot_general(
-                queries[:, span],
-                keys[:, span],
-                (((1,), (1,)), ((), ())),
-                preferred_element_type=jnp.float32,
-            )
-            * score_scale
+    reader = lax.broadcasted_iota(jnp.int32, (rows, rows), 0) // BLOCK
+    column = lax.broadcasted_iota(jnp.int32, (rows, rows), 1) // BLOCK
+    read = reader == column
+    score_scale = HEAD ** (-0.5) * math.log2(math.e)
+    spans = [slice(start, start + HEAD) for start in range(0, inner, HEAD)]
+    scores = [
+        lax.dot_general(
+            queries[:, span], keys[:, span], (((1,), (1,)), ((), ())), preferred_element_type=jnp.float32
         )
-        exps = jnp.where(read, jnp.exp(scores), 0.0)
-        weights = (exps / jnp.sum(exps, axis=-1, keepdims=True)).astype(jnp.bfloat16)
-        attended[:, span] = jnp.dot(weights, values[:, span], preferred_element_type=jnp.float32).astype(jnp.bfloat16)
+        for span in spans
+    ]
+    weights = []
+    for score in scores:
+        exps = jnp.exp2(score * score_scale)
+        exps = jnp.concatenate([jnp.where(read, exps[:, :rows], 0.0), exps[:, rows:]], axis=1)
+        total = jnp.sum(exps, axis=-1, keepdims=True)
+        weights.append((exps * (1.0 / total)).astype(jnp.bfloat16))
+    for span, weight in zip(spans, weights):
+        attended[:, span] = jnp.dot(weight, values[:, span], preferred_element_type=jnp.float32).astype(jnp.bfloat16)
     for start in range(0, own_ref.shape[1], WIDE):
         span = slice(start, start + WIDE)
         put[:, span] = (
@@ -236,8 +240,14 @@
 
 
 def gathered(shard, chosen):
+    ring = [0, 1, 3, 2]
+    onward = {ring[i]: ring[(i + 1) % 4] for i in range(4)}
+
     def around(x):
-        return lax.ppermute(x, "seq", [(i, (i + 4) % 16) for i in range(16)])
+        return lax.ppermute(x, "seq", [(i, onward[i // 4] * 4 + i % 4) for i in range(16)])
+
+    def back(x):
+        return lax.ppermute(x, "seq", [(onward[i // 4] * 4 + i % 4, i) for i in range(16)])
 
     def beside(x):
         return swapped(x, "seq", 2)
@@ -248,42 +258,43 @@
     r1 = around(shard)
     x0 = beside(shard)
     c0 = twin(shard)
+    near = [twin(chosen[0]), beside(after(chosen[1], c0))]
     r2 = around(r1)
-    near = [twin(chosen[0]), beside(chosen[1])]
+    cr1 = twin(r1)
     x1 = beside(after(r1, near[1]))
-    cr1 = twin(after(r1, near[0]))
+    l1 = back(after(shard, cr1))
     cx0 = twin(x0)
-    r3 = around(after(r2, c0, cr1, cx0))
-    x2 = beside(after(r2, c0))
-    x3 = beside(r3)
-    far = [swapped(after(chosen[level], r3), "seq", 1 << level) for level in (3, 2)]
+    x2 = beside(after(r2, cx0, cr1))
     cr2 = twin(r2)
     cx1 = twin(x1)
-    cr3 = twin(r3)
+    x3 = beside(after(l1, cx1, cr2))
+    far = [swapped(after(chosen[level], l1), "seq", 1 << level) for level in (3, 2)]
+    cl1 = twin(l1)
     cx2 = twin(x2)
     early = [
         (shard, 0, 0, 0),
         (c0, 0, 0, 1),
+        (r1, 1, 0, 0),
+        (cr1, 1, 0, 1),
+        (l1, 3, 0, 0),
+        (cl1, 3, 0, 1),
+        (r2, 2, 0, 0),
+        (cr2, 2, 0, 1),
         (x0, 0, 1, 0),
         (cx0, 0, 1, 1),
-        (r1, 1, 0, 0),
-        (cr1, 1, 0, 1),
         (x1, 1, 1, 0),
         (cx1, 1, 1, 1),
-        (r2, 2, 0, 0),
-        (cr2, 2, 0, 1),
         (x2, 2, 1, 0),
         (cx2, 2, 1, 1),
-        (r3, 3, 0, 0),
-        (cr3, 3, 0, 1),
     ]
     triple = assembled([piece for piece, *_ in early], [tuple(hops) for _, *hops in early])
     return triple, [x3, twin(after(x3, triple, *far))], near + far[::-1]
 
 
 def partner_rows(chosen):
-    far = [swapped(chosen[level], "seq", 1 << level) for level in range(LEVELS - 1, -1, -1)]
-    return far[::-1]
+    twin = swapped(chosen[0], "seq", 1)
+    late = [after(block, twin) for block in chosen[1:-1]] + [chosen[-1]]
+    return [twin] + [swapped(block, "seq", 2 << level) for level, block in enumerate(late)]
 
 
 def per_device(resident, arriving, gain, triple, exit_matrix, lookup):

time: 86 us -> 80.5 us (0.936)
  Pallas kernels: 15.3 us -> 12.3 us
  waiting for transfers between devices: 43.8 us -> 40.9 us
    ppermute x3, waiting for transfers between devices: 20.2 us -> 15.5 us  [the longest x2 14 us: around(): lax.ppermute(x, 'seq', [(i, onward[i // 4] * 4 + i % 4) for i in range(16)])]
    ppermute x3, starting transfers between devices: 3.03 us -> 5.1 us  [the longest x2 3.57 us: around(): lax.ppermute(x, 'seq', [(i, onward[i // 4] * 4 + i % 4) for i in range(16)])]
    ppermute x20, waiting for transfers between devices: 17.8 us -> 19.6 us  [swapped(): lax.ppermute(x, axis, [(i, i ^ mask) for i in range(lax.axis_size(axis))])]
    ppermute x20, starting transfers between devices: 17.3 us -> 15.6 us  [swapped(): lax.ppermute(x, axis, [(i, i ^ mask) for i in range(lax.axis_size(axis))])]
    pallas_call x1, Pallas kernels: 5.36 us -> 3.86 us  [first_layer(): pl.pallas_call(functools.partial(first_kernel, len(latest)), out_shape=ja...]
    pallas_call x1, Pallas kernels: 6.07 us -> 4.59 us  [second_layer(): pl.pallas_call(functools.partial(second_kernel, len(latest)), out_shape=j...]
  transfers between devices with their start and end apart: 24 -> 24, of which waited for: 14 -> 10; matrix products, arithmetic and copies ran while one was open for 1% -> 1% of each run, Pallas kernels for 4% -> 5%
where the time goes in v3:
time: 80.5 us; the launch traced here: 80.4 us
  waiting for transfers between devices  40.9 us (51%)
  starting transfers between devices  24.2 us (30%)
  Pallas kernels  12.3 us (15%)
  local copies, waits for them, and re-layouts  2.84 us (4%)
    ppermute x20, waiting for transfers between devices, swapped(): lax.ppermute(x, axis, [(i, i ^ mask) for i in range(lax.axis_size(axis))])  19.6 us
    ppermute x20, starting transfers between devices, swapped(): lax.ppermute(x, axis, [(i, i ^ mask) for i in range(lax.axis_size(axis))])  15.6 us
    ppermute x2, waiting for transfers between devices, around(): lax.ppermute(x, 'seq', [(i, onward[i // 4] * 4 + i % 4) for i in range(16)])  14 us
    ppermute x1, waiting for transfers between devices, from_behind(): return lax.ppermute(block, axis, route)  5.84 us
    pallas_call x1, Pallas kernels, second_layer(): pl.pallas_call(functools.partial(second_kernel, len(latest)), out_shape=j...  4.59 us
    pallas_call x1, Pallas kernels, first_layer(): pl.pallas_call(functools.partial(first_kernel, len(latest)), out_shape=ja...  3.86 us
    ppermute x2, starting transfers between devices, around(): lax.ppermute(x, 'seq', [(i, onward[i // 4] * 4 + i % 4) for i in range(16)])  3.57 us
    ppermute x1, starting transfers between devices, from_behind(): return lax.ppermute(block, axis, route)  3.44 us
  transfers between devices with their start and end apart: 24, of which 10 were waited for; matrix products, arithmetic and copies ran while one was open for 1% of the time, Pallas kernels for 5%

profile of v3, /device:TPU:0, one launch (start us, length us, event | category | flops | bytes accessed | tf_op | source)
XLA Modules:
  0.0 80.4 jit_solution(17409283732737609337)
XLA Ops:
  0.5 2.6 %collective-permute-start.1 = (bf16[64,3072]{1,0:T(8,128)(2,1)}, bf16[64,3072]{1,0:T(8,128)(2,1)S(1)}, u32[]{:S(2)}, u32[]{:S(2)}) collective-permute-start(bf16[64,3072]{1,0:T(8,128)(2,1)} %bitcast.14), channel_id=1, source_target_pairs={{0,4},{1,5},{2,6},{3,7},{4,12},{5,13},{6,14},{7,15},{8,0},{9,1},{1... | collective-permute-start | bytes 1179656 | tf_op jit(solution)/shard_map/ppermute | solution.py:247
  3.1 1.5 %collective-permute-start.7 = (bf16[64,3072]{1,0:T(8,128)(2,1)}, bf16[64,3072]{1,0:T(8,128)(2,1)S(1)}, u32[]{:S(2)}, u32[]{:S(2)}) collective-permute-start(bf16[64,3072]{1,0:T(8,128)(2,1)} %bitcast.15), channel_id=1, source_target_pairs={{0,2},{1,3},{2,0},{3,1},{4,6},{5,7},{6,4},{7,5},{8,10},{9,11},{10,... | collective-permute-start | bytes 1179656 | tf_op jit(solution)/shard_map/ppermute | solution.py:26
  4.6 0.7 gather_fusion
  5.4 1.1 %copy-done.2 = bf16[1,128,1024]{2,1,0:T(8,128)(2,1)S(1)} copy-done((bf16[1,128,1024]{2,1,0:T(8,128)(2,1)S(1)}, bf16[1,128,1024]{2,1,0:T(8,128)(2,1)}, u32[]{:S(2)}) %copy-start.2) | copy-done | bytes 262168
  6.4 0.7 shard_map.64
  7.2 0.5 collective-permute-start.9
  7.7 6.3 %collective-permute-done.1.refs_2_ = bf16[64,3072]{1,0:T(8,128)(2,1)S(1)} collective-permute-done((bf16[64,3072]{1,0:T(8,128)(2,1)}, bf16[64,3072]{1,0:T(8,128)(2,1)S(1)}, u32[]{:S(2)}, u32[]{:S(2)}) %collective-permute-start.1) | collective-permute-done | bytes 393248 | tf_op jit(solution)/shard_map/ppermute | solution.py:247
  14.0 0.9 %collective-permute-start.5 = (bf16[64,3072]{1,0:T(8,128)(2,1)S(1)}, bf16[64,3072]{1,0:T(8,128)(2,1)S(1)}, u32[]{:S(2)}, u32[]{:S(2)}) collective-permute-start(bf16[64,3072]{1,0:T(8,128)(2,1)S(1)} %collective-permute-done.1.refs_2_), channel_id=1, source_target_pairs={{0,4},{1,5},{2,6},{3,7},{4,12},{5,13},{6,14},{7,15},{8,0},{9,1},{1... | collective-permute-start | bytes 1179656 | tf_op jit(solution)/shard_map/ppermute | solution.py:247
  15.3 2.0 %collective-permute-done.9.refs_1_ = bf16[64,1024]{1,0:T(8,128)(2,1)S(1)} collective-permute-done((bf16[64,1024]{1,0:T(8,128)(2,1)S(1)}, bf16[64,1024]{1,0:T(8,128)(2,1)S(1)}, u32[]{:S(2)}, u32[]{:S(2)}) %collective-permute-start.9) | collective-permute-done | bytes 131104 | tf_op jit(solution)/shard_map/ppermute | solution.py:26
  17.3 1.5 %collective-permute-start.10 = (bf16[64,3072]{1,0:T(8,128)(2,1)S(1)}, bf16[64,3072]{1,0:T(8,128)(2,1)S(1)}, u32[]{:S(2)}, u32[]{:S(2)}) collective-permute-start(bf16[64,3072]{1,0:T(8,128)(2,1)S(1)} %collective-permute-done.1.refs_2_), channel_id=1, source_target_pairs={{0,2},{1,3},{2,0},{3,1},{4,6},{5,7},{6,4},{7,5},{8,10},{9,11},{10,... | collective-permute-start | bytes 1179656 | tf_op jit(solution)/shard_map/ppermute | solution.py:26
  18.8 7.7 %collective-permute-done.5.refs_6_ = bf16[64,3072]{1,0:T(8,128)(2,1)S(1)} collective-permute-done((bf16[64,3072]{1,0:T(8,128)(2,1)S(1)}, bf16[64,3072]{1,0:T(8,128)(2,1)S(1)}, u32[]{:S(2)}, u32[]{:S(2)}) %collective-permute-start.5) | collective-permute-done | bytes 393248 | tf_op jit(solution)/shard_map/ppermute | solution.py:247
  26.5 1.5 %collective-permute-start.12 = (bf16[64,3072]{1,0:T(8,128)(2,1)S(1)}, bf16[64,3072]{1,0:T(8,128)(2,1)S(1)}, u32[]{:S(2)}, u32[]{:S(2)}) collective-permute-start(bf16[64,3072]{1,0:T(8,128)(2,1)S(1)} %collective-permute-done.5.refs_6_), channel_id=1, source_target_pairs={{0,2},{1,3},{2,0},{3,1},{4,6},{5,7},{6,4},{7,5},{8,10},{9,11},{10,... | collective-permute-start | bytes 1179656 | tf_op jit(solution)/shard_map/ppermute | solution.py:26
  28.0 1.5 %collective-permute-start.3 = (bf16[64,3072]{1,0:T(8,128)(2,1)}, bf16[64,3072]{1,0:T(8,128)(2,1)S(1)}, u32[]{:S(2)}, u32[]{:S(2)}) collective-permute-start(bf16[64,3072]{1,0:T(8,128)(2,1)} %bitcast.16), channel_id=1, source_target_pairs={{4,0},{5,1},{6,2},{7,3},{12,4},{13,5},{14,6},{15,7},{0,8},{1,9},{2... | collective-permute-start | bytes 1179656 | tf_op jit(solution)/shard_map/ppermute | solution.py:250
  29.5 0.5 collective-permute-start.11
  30.1 7.2 %collective-permute-done.12.refs_12_ = bf16[64,3072]{1,0:T(8,128)(2,1)S(1)} collective-permute-done((bf16[64,3072]{1,0:T(8,128)(2,1)S(1)}, bf16[64,3072]{1,0:T(8,128)(2,1)S(1)}, u32[]{:S(2)}, u32[]{:S(2)}) %collective-permute-start.12) | collective-permute-done | bytes 393248 | tf_op jit(solution)/shard_map/ppermute | solution.py:26
  37.2 1.5 %collective-permute-done.3.refs_4_ = bf16[64,3072]{1,0:T(8,128)(2,1)S(1)} collective-permute-done((bf16[64,3072]{1,0:T(8,128)(2,1)}, bf16[64,3072]{1,0:T(8,128)(2,1)S(1)}, u32[]{:S(2)}, u32[]{:S(2)}) %collective-permute-start.3) | collective-permute-done | bytes 393248 | tf_op jit(solution)/shard_map/ppermute | solution.py:250
  38.7 0.6 collective-permute-start.17
  39.3 2.4 %collective-permute-start.15 = (bf16[64,1024]{1,0:T(8,128)(2,1)S(1)}, bf16[64,1024]{1,0:T(8,128)(2,1)S(1)}, u32[]{:S(2)}, u32[]{:S(2)}) collective-permute-start(bf16[64,1024]{1,0:T(8,128)(2,1)S(1)} %get-tuple-element.31), channel_id=1, source_target_pairs={{0,4},{1,5},{2,6},{3,7},{4,0},{5,1},{6,2},{7,3},{8,12},{9,13},{10,... | collective-permute-start | bytes 393224 | tf_op jit(solution)/shard_map/ppermute | solution.py:26
  41.7 1.8 %collective-permute-start.16 = (bf16[64,1024]{1,0:T(8,128)(2,1)S(1)}, bf16[64,1024]{1,0:T(8,128)(2,1)S(1)}, u32[]{:S(2)}, u32[]{:S(2)}) collective-permute-start(bf16[64,1024]{1,0:T(8,128)(2,1)S(1)} %get-tuple-element.33), channel_id=1, source_target_pairs={{0,8},{1,9},{2,10},{3,11},{4,12},{5,13},{6,14},{7,15},{8,0},{9,1},... | collective-permute-start | bytes 393224 | tf_op jit(solution)/shard_map/ppermute | solution.py:26
  43.5 1.0 %copy-done.4 = bf16[1,64,3072]{2,1,0:T(8,128)(2,1)S(1)} copy-done((bf16[1,64,3072]{2,1,0:T(8,128)(2,1)S(1)}, bf16[1,64,3072]{2,1,0:T(8,128)(2,1)}, u32[]{:S(2)}) %copy-start.4) | copy-done | bytes 393240
  44.5 3.0 %shard_map.65.triple = bf16[1024,3072]{1,0:T(8,128)(2,1)S(1)} custom-call(bf16[64,3072]{1,0:T(8,128)(2,1)S(1)} %bitcast.17, bf16[64,3072]{1,0:T(8,128)(2,1)S(1)} %collective-permute-done.refs_1_, bf16[64,3072]{1,0:T(8,128)(2,1)S(1)} %collective-permute-done.1.refs_2_, bf16[64,3072]{1,0:T(8,128)(2,1)S(1)} %collective-permute-done.2.refs_3_, ...), custom_call_target="tpu_custom_call" | custom-call | bytes 12000000 | tf_op jit(solution)/shard_map/pallas_call | solution.py:107
  47.5 3.3 %collective-permute-done.16.refs_3_ = bf16[64,1024]{1,0:T(8,128)(2,1)S(1)} collective-permute-done((bf16[64,1024]{1,0:T(8,128)(2,1)S(1)}, bf16[64,1024]{1,0:T(8,128)(2,1)S(1)}, u32[]{:S(2)}, u32[]{:S(2)}) %collective-permute-start.16) | collective-permute-done | bytes 131104 | tf_op jit(solution)/shard_map/ppermute | solution.py:26
  50.8 0.5 collective-permute-start.14
  51.3 1.4 %collective-permute-done.14.refs_0_ = bf16[64,1024]{1,0:T(8,128)(2,1)S(1)} collective-permute-done((bf16[64,1024]{1,0:T(8,128)(2,1)S(1)}, bf16[64,1024]{1,0:T(8,128)(2,1)S(1)}, u32[]{:S(2)}, u32[]{:S(2)}) %collective-permute-start.14) | collective-permute-done | bytes 131104 | tf_op jit(solution)/shard_map/ppermute | solution.py:26
  52.7 3.9 %shard_map.66.refs_8_ = bf16[128,1024]{1,0:T(8,128)(2,1)S(1)} custom-call(bf16[1024,3072]{1,0:T(8,128)(2,1)S(1)} %shard_map.65.triple, bf16[128,1024]{1,0:T(8,128)(2,1)S(1)} %bitcast.12, bf16[64,1024]{1,0:T(8,128)(2,1)S(1)} %collective-permute-done.14.refs_0_, bf16[64,1024]{1,0:T(8,128)(2,1)S(1)} %collective-permute-done.9.refs_1_, ...), custom_call_target="tpu_custom_call" | custom-call | flops 2400000000 | bytes 9000000 | tf_op jit(solution)/shard_map/pallas_call | solution.py:218
  56.6 3.4 %collective-permute-start.19 = (bf16[128,1024]{1,0:T(8,128)(2,1)S(1)}, bf16[128,1024]{1,0:T(8,128)(2,1)S(1)}, u32[]{:S(2)}, u32[]{:S(2)}) collective-permute-start(bf16[128,1024]{1,0:T(8,128)(2,1)S(1)} %shard_map.66.refs_8_), channel_id=1, source_target_pairs={{0,16},{1,17},{2,18},{3,19},{4,20},{5,21},{6,22},{7,23},{8,24},{9,... | collective-permute-start | bytes 786440 | tf_op jit(solution)/shard_map/ppermute | solution.py:32
  60.0 5.8 %collective-permute-done.19.moved_ref = bf16[128,1024]{1,0:T(8,128)(2,1)S(1)} collective-permute-done((bf16[128,1024]{1,0:T(8,128)(2,1)S(1)}, bf16[128,1024]{1,0:T(8,128)(2,1)S(1)}, u32[]{:S(2)}, u32[]{:S(2)}) %collective-permute-start.19) | collective-permute-done | bytes 262176 | tf_op jit(solution)/shard_map/ppermute | solution.py:32
  66.1 2.1 %collective-permute-start.23 = (bf16[64,1024]{1,0:T(8,128)(2,1)S(1)}, bf16[64,1024]{1,0:T(8,128)(2,1)S(1)}, u32[]{:S(2)}, u32[]{:S(2)}) collective-permute-start(bf16[64,1024]{1,0:T(8,128)(2,1)S(1)} %get-tuple-element.42), channel_id=1, source_target_pairs={{0,8},{1,9},{2,10},{3,11},{4,12},{5,13},{6,14},{7,15},{8,0},{9,1},... | collective-permute-start | bytes 393224 | tf_op jit(solution)/shard_map/ppermute | solution.py:26
  68.3 1.5 %collective-permute-start.22 = (bf16[64,1024]{1,0:T(8,128)(2,1)S(1)}, bf16[64,1024]{1,0:T(8,128)(2,1)S(1)}, u32[]{:S(2)}, u32[]{:S(2)}) collective-permute-start(bf16[64,1024]{1,0:T(8,128)(2,1)S(1)} %get-tuple-element.41), channel_id=1, source_target_pairs={{0,4},{1,5},{2,6},{3,7},{4,0},{5,1},{6,2},{7,3},{8,12},{9,13},{10,... | collective-permute-start | bytes 393224 | tf_op jit(solution)/shard_map/ppermute | solution.py:26
  69.8 0.5 collective-permute-start.21
  70.4 5.4 %collective-permute-done.23.refs_3_ = bf16[64,1024]{1,0:T(8,128)(2,1)S(1)} collective-permute-done((bf16[64,1024]{1,0:T(8,128)(2,1)S(1)}, bf16[64,1024]{1,0:T(8,128)(2,1)S(1)}, u32[]{:S(2)}, u32[]{:S(2)}) %collective-permute-start.23) | collective-permute-done | bytes 131104 | tf_op jit(solution)/shard_map/ppermute | solution.py:26
  75.8 4.6 %shard_map.68 = bf16[2,128,1024]{2,1,0:T(8,128)(2,1)} custom-call(bf16[1024,3072]{1,0:T(8,128)(2,1)S(1)} %shard_map.65.triple, bf16[128,1024]{1,0:T(8,128)(2,1)S(1)} %get-tuple-element.36.own_ref, bf16[64,1024]{1,0:T(8,128)(2,1)S(1)} %collective-permute-done.20.refs_0_, bf16[64,1024]{1,0:T(8,128)(2,1)S(1)} %collective-permute-done.21.refs_1_, ...), custom_call_target="tpu_custom_call" | custom-call | flops 2400000000 | bytes 9000000 | tf_op jit(solution)/shard_map/pallas_call | solution.py:230
  (38 shorter events, 1.2 us)
Async XLA Ops:
  0.0 4.6 %copy-start = (s32[16,4]{0,1:T(4,128)S(1)}, s32[16,4]{0,1:T(4,128)}, u32[]{:S(2)}) copy-start(s32[16,4]{0,1:T(4,128)} %param.11) | copy-start | bytes 772
  0.0 7.2 %collective-permute-start = (bf16[64,3072]{1,0:T(8,128)(2,1)}, bf16[64,3072]{1,0:T(8,128)(2,1)S(1)}, u32[]{:S(2)}, u32[]{:S(2)}) collective-permute-start(bf16[64,3072]{1,0:T(8,128)(2,1)} %bitcast.13), channel_id=1, source_target_pairs={{0,1},{1,0},{2,3},{3,2},{4,5},{5,4},{6,7},{7,6},{8,9},{9,8},{10,11... | collective-permute-start | bytes 1179656 | tf_op jit(solution)/shard_map/ppermute | solution.py:26
  0.5 13.6 %collective-permute-start.1 = (bf16[64,3072]{1,0:T(8,128)(2,1)}, bf16[64,3072]{1,0:T(8,128)(2,1)S(1)}, u32[]{:S(2)}, u32[]{:S(2)}) collective-permute-start(bf16[64,3072]{1,0:T(8,128)(2,1)} %bitcast.14), channel_id=1, source_target_pairs={{0,4},{1,5},{2,6},{3,7},{4,12},{5,13},{6,14},{7,15},{8,0},{9,1},{1... | collective-permute-start | bytes 1179656 | tf_op jit(solution)/shard_map/ppermute | solution.py:247
  3.1 12.2 %collective-permute-start.7 = (bf16[64,3072]{1,0:T(8,128)(2,1)}, bf16[64,3072]{1,0:T(8,128)(2,1)S(1)}, u32[]{:S(2)}, u32[]{:S(2)}) collective-permute-start(bf16[64,3072]{1,0:T(8,128)(2,1)} %bitcast.15), channel_id=1, source_target_pairs={{0,2},{1,3},{2,0},{3,1},{4,6},{5,7},{6,4},{7,5},{8,10},{9,11},{10,... | collective-permute-start | bytes 1179656 | tf_op jit(solution)/shard_map/ppermute | solution.py:26
  4.6 48.1 %copy-start.3 = (bf16[1,128,1024]{2,1,0:T(8,128)(2,1)S(1)}, bf16[1,128,1024]{2,1,0:T(8,128)(2,1)}, u32[]{:S(2)}) copy-start(bf16[1,128,1024]{2,1,0:T(8,128)(2,1)} %param.6) | copy-start | bytes 786436
  4.6 48.1 %copy-start.6 = (f32[1,1024]{1,0:T(1,128)S(1)}, f32[1,1024]{1,0:T(1,128)}, u32[]{:S(2)}) copy-start(f32[1,1024]{1,0:T(1,128)} %refs_4_.3) | copy-start | bytes 12292
  5.3 47.4 %copy-start.1 = (bf16[1,1024,1024]{2,1,0:T(8,128)(2,1)S(1)}, bf16[1,1024,1024]{2,1,0:T(8,128)(2,1)}, u32[]{:S(2)}) copy-start(bf16[1,1024,1024]{2,1,0:T(8,128)(2,1)} %param.10) | copy-start | bytes 6291460
  5.3 1.1 %copy-start.2 = (bf16[1,128,1024]{2,1,0:T(8,128)(2,1)S(1)}, bf16[1,128,1024]{2,1,0:T(8,128)(2,1)}, u32[]{:S(2)}) copy-start(bf16[1,128,1024]{2,1,0:T(8,128)(2,1)} %param.6) | copy-start | bytes 786436
  7.2 10.1 %collective-permute-start.9 = (bf16[64,1024]{1,0:T(8,128)(2,1)S(1)}, bf16[64,1024]{1,0:T(8,128)(2,1)S(1)}, u32[]{:S(2)}, u32[]{:S(2)}) collective-permute-start(bf16[64,1024]{1,0:T(8,128)(2,1)S(1)} %get-tuple-element.26), channel_id=1, source_target_pairs={{0,2},{1,3},{2,0},{3,1},{4,6},{5,7},{6,4},{7,5},{8,10},{9,11},{10,... | collective-permute-start | bytes 393224 | tf_op jit(solution)/shard_map/ppermute | solution.py:26
  14.0 4.8 %collective-permute-start.2 = (bf16[64,3072]{1,0:T(8,128)(2,1)S(1)}, bf16[64,3072]{1,0:T(8,128)(2,1)S(1)}, u32[]{:S(2)}, u32[]{:S(2)}) collective-permute-start(bf16[64,3072]{1,0:T(8,128)(2,1)S(1)} %collective-permute-done.1.refs_2_), channel_id=1, source_target_pairs={{0,1},{1,0},{2,3},{3,2},{4,5},{5,4},{6,7},{7,6},{8,9},{9,8},{10,11... | collective-permute-start | bytes 1179656 | tf_op jit(solution)/shard_map/ppermute | solution.py:26
  14.0 12.4 %collective-permute-start.5 = (bf16[64,3072]{1,0:T(8,128)(2,1)S(1)}, bf16[64,3072]{1,0:T(8,128)(2,1)S(1)}, u32[]{:S(2)}, u32[]{:S(2)}) collective-permute-start(bf16[64,3072]{1,0:T(8,128)(2,1)S(1)} %collective-permute-done.1.refs_2_), channel_id=1, source_target_pairs={{0,4},{1,5},{2,6},{3,7},{4,12},{5,13},{6,14},{7,15},{8,0},{9,1},{1... | collective-permute-start | bytes 1179656 | tf_op jit(solution)/shard_map/ppermute | solution.py:247
  15.3 11.2 %collective-permute-start.8 = (bf16[64,3072]{1,0:T(8,128)(2,1)S(1)}, bf16[64,3072]{1,0:T(8,128)(2,1)S(1)}, u32[]{:S(2)}, u32[]{:S(2)}) collective-permute-start(bf16[64,3072]{1,0:T(8,128)(2,1)S(1)} %collective-permute-done.7.refs_8_), channel_id=1, source_target_pairs={{0,1},{1,0},{2,3},{3,2},{4,5},{5,4},{6,7},{7,6},{8,9},{9,8},{10,11... | collective-permute-start | bytes 1179656 | tf_op jit(solution)/shard_map/ppermute | solution.py:26
  17.3 12.2 %collective-permute-start.10 = (bf16[64,3072]{1,0:T(8,128)(2,1)S(1)}, bf16[64,3072]{1,0:T(8,128)(2,1)S(1)}, u32[]{:S(2)}, u32[]{:S(2)}) collective-permute-start(bf16[64,3072]{1,0:T(8,128)(2,1)S(1)} %collective-permute-done.1.refs_2_), channel_id=1, source_target_pairs={{0,2},{1,3},{2,0},{3,1},{4,6},{5,7},{6,4},{7,5},{8,10},{9,11},{10,... | collective-permute-start | bytes 1179656 | tf_op jit(solution)/shard_map/ppermute | solution.py:26
  26.5 10.7 %collective-permute-start.12 = (bf16[64,3072]{1,0:T(8,128)(2,1)S(1)}, bf16[64,3072]{1,0:T(8,128)(2,1)S(1)}, u32[]{:S(2)}, u32[]{:S(2)}) collective-permute-start(bf16[64,3072]{1,0:T(8,128)(2,1)S(1)} %collective-permute-done.5.refs_6_), channel_id=1, source_target_pairs={{0,2},{1,3},{2,0},{3,1},{4,6},{5,7},{6,4},{7,5},{8,10},{9,11},{10,... | collective-permute-start | bytes 1179656 | tf_op jit(solution)/shard_map/ppermute | solution.py:26
  28.0 10.7 %collective-permute-start.3 = (bf16[64,3072]{1,0:T(8,128)(2,1)}, bf16[64,3072]{1,0:T(8,128)(2,1)S(1)}, u32[]{:S(2)}, u32[]{:S(2)}) collective-permute-start(bf16[64,3072]{1,0:T(8,128)(2,1)} %bitcast.16), channel_id=1, source_target_pairs={{4,0},{5,1},{6,2},{7,3},{12,4},{13,5},{14,6},{15,7},{0,8},{1,9},{2... | collective-permute-start | bytes 1179656 | tf_op jit(solution)/shard_map/ppermute | solution.py:250
  29.5 9.2 %collective-permute-start.6 = (bf16[64,3072]{1,0:T(8,128)(2,1)S(1)}, bf16[64,3072]{1,0:T(8,128)(2,1)S(1)}, u32[]{:S(2)}, u32[]{:S(2)}) collective-permute-start(bf16[64,3072]{1,0:T(8,128)(2,1)S(1)} %collective-permute-done.5.refs_6_), channel_id=1, source_target_pairs={{0,1},{1,0},{2,3},{3,2},{4,5},{5,4},{6,7},{7,6},{8,9},{9,8},{10,11... | collective-permute-start | bytes 1179656 | tf_op jit(solution)/shard_map/ppermute | solution.py:26
  29.5 9.2 %collective-permute-start.11 = (bf16[64,3072]{1,0:T(8,128)(2,1)S(1)}, bf16[64,3072]{1,0:T(8,128)(2,1)S(1)}, u32[]{:S(2)}, u32[]{:S(2)}) collective-permute-start(bf16[64,3072]{1,0:T(8,128)(2,1)S(1)} %collective-permute-done.10.refs_10_), channel_id=1, source_target_pairs={{0,1},{1,0},{2,3},{3,2},{4,5},{5,4},{6,7},{7,6},{8,9},{9,8},{10,11... | collective-permute-start | bytes 1179656 | tf_op jit(solution)/shard_map/ppermute | solution.py:26
  37.2 6.3 %collective-permute-start.13 = (bf16[64,3072]{1,0:T(8,128)(2,1)S(1)}, bf16[64,3072]{1,0:T(8,128)(2,1)S(1)}, u32[]{:S(2)}, u32[]{:S(2)}) collective-permute-start(bf16[64,3072]{1,0:T(8,128)(2,1)S(1)} %collective-permute-done.12.refs_12_), channel_id=1, source_target_pairs={{0,1},{1,0},{2,3},{3,2},{4,5},{5,4},{6,7},{7,6},{8,9},{9,8},{10,11... | collective-permute-start | bytes 1179656 | tf_op jit(solution)/shard_map/ppermute | solution.py:26
  38.7 4.8 %collective-permute-start.4 = (bf16[64,3072]{1,0:T(8,128)(2,1)S(1)}, bf16[64,3072]{1,0:T(8,128)(2,1)S(1)}, u32[]{:S(2)}, u32[]{:S(2)}) collective-permute-start(bf16[64,3072]{1,0:T(8,128)(2,1)S(1)} %collective-permute-done.3.refs_4_), channel_id=1, source_target_pairs={{0,1},{1,0},{2,3},{3,2},{4,5},{5,4},{6,7},{7,6},{8,9},{9,8},{10,11... | collective-permute-start | bytes 1179656 | tf_op jit(solution)/shard_map/ppermute | solution.py:26
  38.7 12.1 %collective-permute-start.17 = (bf16[64,3072]{1,0:T(8,128)(2,1)S(1)}, bf16[64,3072]{1,0:T(8,128)(2,1)S(1)}, u32[]{:S(2)}, u32[]{:S(2)}) collective-permute-start(bf16[64,3072]{1,0:T(8,128)(2,1)S(1)} %collective-permute-done.3.refs_4_), channel_id=1, source_target_pairs={{0,2},{1,3},{2,0},{3,1},{4,6},{5,7},{6,4},{7,5},{8,10},{9,11},{10,... | collective-permute-start | bytes 1179656 | tf_op jit(solution)/shard_map/ppermute | solution.py:26
  39.3 8.2 %collective-permute-start.15 = (bf16[64,1024]{1,0:T(8,128)(2,1)S(1)}, bf16[64,1024]{1,0:T(8,128)(2,1)S(1)}, u32[]{:S(2)}, u32[]{:S(2)}) collective-permute-start(bf16[64,1024]{1,0:T(8,128)(2,1)S(1)} %get-tuple-element.31), channel_id=1, source_target_pairs={{0,4},{1,5},{2,6},{3,7},{4,0},{5,1},{6,2},{7,3},{8,12},{9,13},{10,... | collective-permute-start | bytes 393224 | tf_op jit(solution)/shard_map/ppermute | solution.py:26
  41.7 9.0 %collective-permute-start.16 = (bf16[64,1024]{1,0:T(8,128)(2,1)S(1)}, bf16[64,1024]{1,0:T(8,128)(2,1)S(1)}, u32[]{:S(2)}, u32[]{:S(2)}) collective-permute-start(bf16[64,1024]{1,0:T(8,128)(2,1)S(1)} %get-tuple-element.33), channel_id=1, source_target_pairs={{0,8},{1,9},{2,10},{3,11},{4,12},{5,13},{6,14},{7,15},{8,0},{9,1},... | collective-permute-start | bytes 393224 | tf_op jit(solution)/shard_map/ppermute | solution.py:26
  43.5 1.0 %copy-start.4 = (bf16[1,64,3072]{2,1,0:T(8,128)(2,1)S(1)}, bf16[1,64,3072]{2,1,0:T(8,128)(2,1)}, u32[]{:S(2)}) copy-start(bf16[1,64,3072]{2,1,0:T(8,128)(2,1)} %param.9) | copy-start | bytes 1179652
  47.5 18.4 %copy-start.5 = (bf16[128,1024]{1,0:T(8,128)(2,1)S(1)}, bf16[128,1024]{1,0:T(8,128)(2,1)}, u32[]{:S(2)}) copy-start(bf16[128,1024]{1,0:T(8,128)(2,1)} %arriving_ref.1) | copy-start | bytes 786436
  50.8 1.9 %collective-permute-start.18 = (bf16[64,3072]{1,0:T(8,128)(2,1)S(1)}, bf16[64,3072]{1,0:T(8,128)(2,1)S(1)}, u32[]{:S(2)}, u32[]{:S(2)}) collective-permute-start(bf16[64,3072]{1,0:T(8,128)(2,1)S(1)} %collective-permute-done.17.refs_6_), channel_id=1, source_target_pairs={{0,1},{1,0},{2,3},{3,2},{4,5},{5,4},{6,7},{7,6},{8,9},{9,8},{10,11... | collective-permute-start | bytes 1179656 | tf_op jit(solution)/shard_map/ppermute | solution.py:26
  50.8 1.9 %collective-permute-start.14 = (bf16[64,1024]{1,0:T(8,128)(2,1)S(1)}, bf16[64,1024]{1,0:T(8,128)(2,1)S(1)}, u32[]{:S(2)}, u32[]{:S(2)}) collective-permute-start(bf16[64,1024]{1,0:T(8,128)(2,1)S(1)} %get-tuple-element.29), channel_id=1, source_target_pairs={{0,1},{1,0},{2,3},{3,2},{4,5},{5,4},{6,7},{7,6},{8,9},{9,8},{10,11... | collective-permute-start | bytes 393224 | tf_op jit(solution)/shard_map/ppermute | solution.py:26
  56.6 9.3 %collective-permute-start.19 = (bf16[128,1024]{1,0:T(8,128)(2,1)S(1)}, bf16[128,1024]{1,0:T(8,128)(2,1)S(1)}, u32[]{:S(2)}, u32[]{:S(2)}) collective-permute-start(bf16[128,1024]{1,0:T(8,128)(2,1)S(1)} %shard_map.66.refs_8_), channel_id=1, source_target_pairs={{0,16},{1,17},{2,18},{3,19},{4,20},{5,21},{6,22},{7,23},{8,24},{9,... | collective-permute-start | bytes 786440 | tf_op jit(solution)/shard_map/ppermute | solution.py:32
  66.1 2.2 %collective-permute-start.20 = (bf16[64,1024]{1,0:T(8,128)(2,1)S(1)}, bf16[64,1024]{1,0:T(8,128)(2,1)S(1)}, u32[]{:S(2)}, u32[]{:S(2)}) collective-permute-start(bf16[64,1024]{1,0:T(8,128)(2,1)S(1)} %get-tuple-element.37), channel_id=1, source_target_pairs={{0,1},{1,0},{2,3},{3,2},{4,5},{5,4},{6,7},{7,6},{8,9},{9,8},{10,11... | collective-permute-start | bytes 393224 | tf_op jit(solution)/shard_map/ppermute | solution.py:26
  66.1 9.6 %collective-permute-start.23 = (bf16[64,1024]{1,0:T(8,128)(2,1)S(1)}, bf16[64,1024]{1,0:T(8,128)(2,1)S(1)}, u32[]{:S(2)}, u32[]{:S(2)}) collective-permute-start(bf16[64,1024]{1,0:T(8,128)(2,1)S(1)} %get-tuple-element.42), channel_id=1, source_target_pairs={{0,8},{1,9},{2,10},{3,11},{4,12},{5,13},{6,14},{7,15},{8,0},{9,1},... | collective-permute-start | bytes 393224 | tf_op jit(solution)/shard_map/ppermute | solution.py:26
  68.3 7.5 %collective-permute-start.22 = (bf16[64,1024]{1,0:T(8,128)(2,1)S(1)}, bf16[64,1024]{1,0:T(8,128)(2,1)S(1)}, u32[]{:S(2)}, u32[]{:S(2)}) collective-permute-start(bf16[64,1024]{1,0:T(8,128)(2,1)S(1)} %get-tuple-element.41), channel_id=1, source_target_pairs={{0,4},{1,5},{2,6},{3,7},{4,0},{5,1},{6,2},{7,3},{8,12},{9,13},{10,... | collective-permute-start | bytes 393224 | tf_op jit(solution)/shard_map/ppermute | solution.py:26
  69.8 5.9 %collective-permute-start.21 = (bf16[64,1024]{1,0:T(8,128)(2,1)S(1)}, bf16[64,1024]{1,0:T(8,128)(2,1)S(1)}, u32[]{:S(2)}, u32[]{:S(2)}) collective-permute-start(bf16[64,1024]{1,0:T(8,128)(2,1)S(1)} %get-tuple-element.39), channel_id=1, source_target_pairs={{0,2},{1,3},{2,0},{3,1},{4,6},{5,7},{6,4},{7,5},{8,10},{9,11},{10,... | collective-permute-start | bytes 393224 | tf_op jit(solution)/shard_map/ppermute | solution.py:26

commit v4 on v3

--- a/solution.py
+++ b/solution.py
@@ -115,7 +115,27 @@
     )(*pieces)
 
 
-def attend(own_ref, fars, gain_ref, triple, exit_ref, latest, put, normed, queries, keys, values, attended, last):
+def ahead_kernel(triple, own_ref, gain_ref, out_ref, normed):
+    normed[...] = row_norm(own_ref[...], gain_ref[...])
+    for start in range(0, triple.shape[1], WIDE):
+        span = slice(start, start + WIDE)
+        out_ref[:, span] = jnp.dot(normed[...], triple[:, span], preferred_element_type=jnp.float32)
+
+
+def ahead(triple, own, gain):
+    rows, width = own.shape
+    return pl.pallas_call(
+        ahead_kernel,
+        out_shape=pltpu.VMEM((rows, triple.shape[1]), jnp.float32),
+        in_specs=[in_vmem] * 3,
+        out_specs=in_vmem,
+        scratch_shapes=[pltpu.VMEM((rows, width), jnp.bfloat16)],
+        compiler_params=pltpu.CompilerParams(vmem_limit_bytes=4 * MIB),
+        cost_estimate=pl.CostEstimate(flops=800_000_000, bytes_accessed=8_000_000, transcendentals=0),
+    )(triple, own, gain)
+
+
+def attend(own_ref, started, fars, gain_ref, triple, exit_ref, latest, put, normed, queries, keys, values, attended, last):
     inner = HEADS * HEAD
     rows = own_ref.shape[0]
     far_rows = LEVELS * BLOCK
@@ -131,23 +151,34 @@
         spot = pl.multiple_of(origin(3, 1, 0) // 2 * (2 * part), 2 * part)
         late_columns = normed[:, pl.ds(spot, 2 * part)]
 
-    def projection(count, start):
-        span = slice(start, start + WIDE)
-        result = jnp.dot(normed[:count], triple[:, span], preferred_element_type=jnp.float32)
+    def own_part(start):
+        span = slice(start, start + WIDE)
+        result = started[:, span]
         if latest:
-            result += jnp.dot(late_columns[:count], last[:, span], preferred_element_type=jnp.float32)
+            result += jnp.dot(late_columns[:rows], last[:, span], preferred_element_type=jnp.float32)
         return result
 
+    def far_part(start):
+        span = slice(start, start + WIDE)
+        result = jnp.dot(normed[rows:], triple[:, span], preferred_element_type=jnp.float32)
+        if latest:
+            result += jnp.dot(late_columns[rows:], last[:, span], preferred_element_type=jnp.float32)
+        return result
+
     for start in range(0, inner, WIDE):
-        projected = projection(rows, start)
+        projected = own_part(start)
         for head in range(0, WIDE, HEAD):
             queries[:, start + head : start + head + HEAD] = head_norm(projected[:, head : head + HEAD])
     for start in range(0, inner, WIDE):
-        projected = projection(rows + far_rows, inner + start)
+        near, far = own_part(inner + start), far_part(inner + start)
         for head in range(0, WIDE, HEAD):
-            keys[:, start + head : start + head + HEAD] = head_norm(projected[:, head : head + HEAD])
+            span = slice(start + head, start + head + HEAD)
+            keys[:rows, span] = head_norm(near[:, head : head + HEAD])
+            keys[rows:, span] = head_norm(far[:, head : head + HEAD])
     for start in range(0, inner, WIDE):
-        values[:, start : start + WIDE] = projection(rows + far_rows, 2 * inner + start).astype(jnp.bfloat16)
+        span = slice(start, start + WIDE)
+        values[:rows, span] = own_part(2 * inner + start).astype(jnp.bfloat16)
+        values[rows:, span] = far_part(2 * inner + start).astype(jnp.bfloat16)
     reader = lax.broadcasted_iota(jnp.int32, (rows, rows), 0) // BLOCK
     column = lax.broadcasted_iota(jnp.int32, (rows, rows), 1) // BLOCK
     read = reader == column
@@ -175,22 +206,22 @@
         ).astype(jnp.bfloat16)
 
 
-def first_kernel(late, triple, own_ref, *refs):
+def first_kernel(late, triple, own_ref, started, *refs):
     fars, refs = refs[:LEVELS], refs[LEVELS:]
     gain_ref, exit_ref, *refs = refs
     latest, refs = refs[:late], refs[late:]
     out_ref, *scratch = refs
-    attend(own_ref, fars, gain_ref, triple, exit_ref, latest, out_ref, *scratch)
-
-
-def second_kernel(late, triple, own_ref, *refs):
+    attend(own_ref, started, fars, gain_ref, triple, exit_ref, latest, out_ref, *scratch)
+
+
+def second_kernel(late, triple, own_ref, started, *refs):
     fars, refs = refs[:LEVELS], refs[LEVELS:]
     gain_ref, exit_ref, *refs = refs
     latest, refs = refs[:late], refs[late:]
     first_ref, out_ref, result, sems, *scratch = refs
     early = pltpu.make_async_copy(first_ref, out_ref.at[0], sems.at[0])
     early.start()
-    attend(own_ref, fars, gain_ref, triple, exit_ref, latest, result, *scratch)
+    attend(own_ref, started, fars, gain_ref, triple, exit_ref, latest, result, *scratch)
     finish = pltpu.make_async_copy(result, out_ref.at[1], sems.at[1])
     finish.start()
     early.wait()
@@ -214,32 +245,32 @@
 cost = pl.CostEstimate(flops=2_400_000_000, bytes_accessed=9_000_000, transcendentals=400_000)
 
 
-def first_layer(triple, own, fars, gain, exit_matrix, latest):
+def first_layer(triple, own, started, fars, gain, exit_matrix, latest):
     return pl.pallas_call(
         functools.partial(first_kernel, len(latest)),
         out_shape=jax.ShapeDtypeStruct(own.shape, own.dtype),
-        in_specs=[in_vmem] * (4 + LEVELS + len(latest)),
+        in_specs=[in_vmem] * (5 + LEVELS + len(latest)),
         out_specs=in_vmem,
         scratch_shapes=scratch_of(*own.shape, triple, latest),
         compiler_params=pltpu.CompilerParams(vmem_limit_bytes=16 * MIB),
         cost_estimate=cost,
-    )(triple, own, *fars, gain, exit_matrix, *latest)
-
-
-def second_layer(triple, own, fars, gain, exit_matrix, latest, first_out):
+    )(triple, own, started, *fars, gain, exit_matrix, *latest)
+
+
+def second_layer(triple, own, started, fars, gain, exit_matrix, latest, first_out):
     return pl.pallas_call(
         functools.partial(second_kernel, len(latest)),
         out_shape=jax.ShapeDtypeStruct((2,) + own.shape, own.dtype),
-        in_specs=[in_vmem] * (5 + LEVELS + len(latest)),
+        in_specs=[in_vmem] * (6 + LEVELS + len(latest)),
         out_specs=anywhere,
         scratch_shapes=[pltpu.VMEM(own.shape, own.dtype), pltpu.SemaphoreType.DMA((2,))]
         + scratch_of(*own.shape, triple, latest),
         compiler_params=pltpu.CompilerParams(vmem_limit_bytes=16 * MIB),
         cost_estimate=cost,
-    )(triple, own, *fars, gain, exit_matrix, *latest, first_out)
-
-
-def gathered(shard, chosen):
+    )(triple, own, started, *fars, gain, exit_matrix, *latest, first_out)
+
+
+def gathered(shard, chosen, own, gain):
     ring = [0, 1, 3, 2]
     onward = {ring[i]: ring[(i + 1) % 4] for i in range(4)}
 
@@ -268,7 +299,7 @@
     cr2 = twin(r2)
     cx1 = twin(x1)
     x3 = beside(after(l1, cx1, cr2))
-    far = [swapped(after(chosen[level], l1), "seq", 1 << level) for level in (3, 2)]
+    far = [swapped(after(chosen[3], r2), "seq", 8), swapped(after(chosen[2], l1), "seq", 4)]
     cl1 = twin(l1)
     cx2 = twin(x2)
     early = [
@@ -288,7 +319,8 @@
         (cx2, 2, 1, 1),
     ]
     triple = assembled([piece for piece, *_ in early], [tuple(hops) for _, *hops in early])
-    return triple, [x3, twin(after(x3, triple, *far))], near + far[::-1]
+    started = ahead(triple, own, gain)
+    return triple, started, [x3, twin(after(x3, started, *far))], near + far[::-1]
 
 
 def partner_rows(chosen):
@@ -305,16 +337,17 @@
     wanted = jnp.broadcast_to(lookup[partner, levels % LEVELS][:, None], (8, 128))
     _, chosen = choose(wanted, first_in, first_in)
     if lax.axis_size("seq") == 16:
-        triple, latest, fars = gathered(triple[0], chosen)
+        triple, started, latest, fars = gathered(triple[0], chosen, first_in, gain)
     else:
         triple = lax.all_gather(triple[0], "seq", axis=0, tiled=True)
+        started = ahead(triple, first_in, gain)
         latest = []
         fars = partner_rows(chosen)
-    first_out = first_layer(triple, first_in, fars, gain, exit_matrix[0], latest)
+    first_out = first_layer(triple, first_in, started, fars, gain, exit_matrix[0], latest)
     moved = from_behind(first_out, "section", 1)
     second_in, chosen = choose(wanted, moved, arriving)
     fars = partner_rows(chosen)
-    return second_layer(triple, second_in, fars, gain, exit_matrix[0], latest, first_out)[:, None]
+    return second_layer(triple, second_in, ahead(triple, second_in, gain), fars, gain, exit_matrix[0], latest, first_out)[:, None]
 
 
 def solution(mesh):

time: 80.5 us -> 76.9 us (0.955)
  waiting for transfers between devices: 40.9 us -> 36 us
    ppermute x20, waiting for transfers between devices: 19.6 us -> 15.9 us  [swapped(): lax.ppermute(x, axis, [(i, i ^ mask) for i in range(lax.axis_size(axis))])]
    pallas_call x0 -> x2, Pallas kernels: none -> 2.13 us  [ahead(): pl.pallas_call(ahead_kernel, out_shape=pltpu.VMEM((rows, triple.shape[1])...]
  transfers between devices with their start and end apart: 24 -> 24, of which waited for: 10 -> 12; matrix products, arithmetic and copies ran while one was open for 1% -> 1% of each run, Pallas kernels for 5% -> 8%
where the time goes in v4:
time: 76.9 us; the launch traced here: 76.7 us
  waiting for transfers between devices  36 us (47%)
  starting transfers between devices  24.7 us (32%)
  Pallas kernels  13.1 us (17%)
  local copies, waits for them, and re-layouts  2.7 us (4%)
    ppermute x20, starting transfers between devices, swapped(): lax.ppermute(x, axis, [(i, i ^ mask) for i in range(lax.axis_size(axis))])  16.2 us
    ppermute x20, waiting for transfers between devices, swapped(): lax.ppermute(x, axis, [(i, i ^ mask) for i in range(lax.axis_size(axis))])  15.9 us
    ppermute x2, waiting for transfers between devices, around(): lax.ppermute(x, 'seq', [(i, onward[i // 4] * 4 + i % 4) for i in range(16)])  13.5 us
    ppermute x1, waiting for transfers between devices, from_behind(): return lax.ppermute(block, axis, route)  5.83 us
    pallas_call x1, Pallas kernels, second_layer(): pl.pallas_call(functools.partial(second_kernel, len(latest)), out_shape=j...  3.9 us
    ppermute x2, starting transfers between devices, around(): lax.ppermute(x, 'seq', [(i, onward[i // 4] * 4 + i % 4) for i in range(16)])  3.57 us
    ppermute x1, starting transfers between devices, from_behind(): return lax.ppermute(block, axis, route)  3.44 us
    pallas_call x1, Pallas kernels, first_layer(): pl.pallas_call(functools.partial(first_kernel, len(latest)), out_shape=ja...  3.19 us
  transfers between devices with their start and end apart: 24, of which 12 were waited for; matrix products, arithmetic and copies ran while one was open for 1% of the time, Pallas kernels for 8%

profile of v4, /device:TPU:0, one launch (start us, length us, event | category | flops | bytes accessed | tf_op | source)
XLA Modules:
  0.0 76.7 jit_solution(15255933245895067362)
XLA Ops:
  0.5 2.6 %collective-permute-start.1 = (bf16[64,3072]{1,0:T(8,128)(2,1)}, bf16[64,3072]{1,0:T(8,128)(2,1)S(1)}, u32[]{:S(2)}, u32[]{:S(2)}) collective-permute-start(bf16[64,3072]{1,0:T(8,128)(2,1)} %bitcast.15), channel_id=1, source_target_pairs={{0,4},{1,5},{2,6},{3,7},{4,12},{5,13},{6,14},{7,15},{8,0},{9,1},{1... | collective-permute-start | bytes 1179656 | tf_op jit(solution)/shard_map/ppermute | solution.py:278
  3.1 1.5 %collective-permute-start.7 = (bf16[64,3072]{1,0:T(8,128)(2,1)}, bf16[64,3072]{1,0:T(8,128)(2,1)S(1)}, u32[]{:S(2)}, u32[]{:S(2)}) collective-permute-start(bf16[64,3072]{1,0:T(8,128)(2,1)} %bitcast.16), channel_id=1, source_target_pairs={{0,2},{1,3},{2,0},{3,1},{4,6},{5,7},{6,4},{7,5},{8,10},{9,11},{10,... | collective-permute-start | bytes 1179656 | tf_op jit(solution)/shard_map/ppermute | solution.py:26
  4.6 0.7 gather_fusion
  5.3 1.0 %copy-done.2 = bf16[1,128,1024]{2,1,0:T(8,128)(2,1)S(1)} copy-done((bf16[1,128,1024]{2,1,0:T(8,128)(2,1)S(1)}, bf16[1,128,1024]{2,1,0:T(8,128)(2,1)}, u32[]{:S(2)}) %copy-start.2) | copy-done | bytes 262168
  6.3 0.7 shard_map.64
  7.0 0.5 collective-permute-start.9
  7.6 6.5 %collective-permute-done.1.refs_2_ = bf16[64,3072]{1,0:T(8,128)(2,1)S(1)} collective-permute-done((bf16[64,3072]{1,0:T(8,128)(2,1)}, bf16[64,3072]{1,0:T(8,128)(2,1)S(1)}, u32[]{:S(2)}, u32[]{:S(2)}) %collective-permute-start.1) | collective-permute-done | bytes 393248 | tf_op jit(solution)/shard_map/ppermute | solution.py:278
  14.0 0.9 %collective-permute-start.5 = (bf16[64,3072]{1,0:T(8,128)(2,1)S(1)}, bf16[64,3072]{1,0:T(8,128)(2,1)S(1)}, u32[]{:S(2)}, u32[]{:S(2)}) collective-permute-start(bf16[64,3072]{1,0:T(8,128)(2,1)S(1)} %collective-permute-done.1.refs_2_), channel_id=1, source_target_pairs={{0,4},{1,5},{2,6},{3,7},{4,12},{5,13},{6,14},{7,15},{8,0},{9,1},{1... | collective-permute-start | bytes 1179656 | tf_op jit(solution)/shard_map/ppermute | solution.py:278
  15.5 1.8 %collective-permute-done.9.refs_1_ = bf16[64,1024]{1,0:T(8,128)(2,1)S(1)} collective-permute-done((bf16[64,1024]{1,0:T(8,128)(2,1)S(1)}, bf16[64,1024]{1,0:T(8,128)(2,1)S(1)}, u32[]{:S(2)}, u32[]{:S(2)}) %collective-permute-start.9) | collective-permute-done | bytes 131104 | tf_op jit(solution)/shard_map/ppermute | solution.py:26
  17.3 1.5 %collective-permute-start.10 = (bf16[64,3072]{1,0:T(8,128)(2,1)S(1)}, bf16[64,3072]{1,0:T(8,128)(2,1)S(1)}, u32[]{:S(2)}, u32[]{:S(2)}) collective-permute-start(bf16[64,3072]{1,0:T(8,128)(2,1)S(1)} %collective-permute-done.1.refs_2_), channel_id=1, source_target_pairs={{0,2},{1,3},{2,0},{3,1},{4,6},{5,7},{6,4},{7,5},{8,10},{9,11},{10,... | collective-permute-start | bytes 1179656 | tf_op jit(solution)/shard_map/ppermute | solution.py:26
  18.8 7.0 %collective-permute-done.5.refs_6_ = bf16[64,3072]{1,0:T(8,128)(2,1)S(1)} collective-permute-done((bf16[64,3072]{1,0:T(8,128)(2,1)S(1)}, bf16[64,3072]{1,0:T(8,128)(2,1)S(1)}, u32[]{:S(2)}, u32[]{:S(2)}) %collective-permute-start.5) | collective-permute-done | bytes 393248 | tf_op jit(solution)/shard_map/ppermute | solution.py:278
  25.8 1.3 %collective-permute-start.12 = (bf16[64,3072]{1,0:T(8,128)(2,1)S(1)}, bf16[64,3072]{1,0:T(8,128)(2,1)S(1)}, u32[]{:S(2)}, u32[]{:S(2)}) collective-permute-start(bf16[64,3072]{1,0:T(8,128)(2,1)S(1)} %collective-permute-done.5.refs_6_), channel_id=1, source_target_pairs={{0,2},{1,3},{2,0},{3,1},{4,6},{5,7},{6,4},{7,5},{8,10},{9,11},{10,... | collective-permute-start | bytes 1179656 | tf_op jit(solution)/shard_map/ppermute | solution.py:26
  27.2 1.5 %collective-permute-start.3 = (bf16[64,3072]{1,0:T(8,128)(2,1)}, bf16[64,3072]{1,0:T(8,128)(2,1)S(1)}, u32[]{:S(2)}, u32[]{:S(2)}) collective-permute-start(bf16[64,3072]{1,0:T(8,128)(2,1)} %bitcast.17), channel_id=1, source_target_pairs={{4,0},{5,1},{6,2},{7,3},{12,4},{13,5},{14,6},{15,7},{0,8},{1,9},{2... | collective-permute-start | bytes 1179656 | tf_op jit(solution)/shard_map/ppermute | solution.py:281
  29.2 6.9 %collective-permute-done.12.refs_12_ = bf16[64,3072]{1,0:T(8,128)(2,1)S(1)} collective-permute-done((bf16[64,3072]{1,0:T(8,128)(2,1)S(1)}, bf16[64,3072]{1,0:T(8,128)(2,1)S(1)}, u32[]{:S(2)}, u32[]{:S(2)}) %collective-permute-start.12) | collective-permute-done | bytes 393248 | tf_op jit(solution)/shard_map/ppermute | solution.py:26
  36.1 0.8 %collective-permute-done.3.refs_4_ = bf16[64,3072]{1,0:T(8,128)(2,1)S(1)} collective-permute-done((bf16[64,3072]{1,0:T(8,128)(2,1)}, bf16[64,3072]{1,0:T(8,128)(2,1)S(1)}, u32[]{:S(2)}, u32[]{:S(2)}) %collective-permute-start.3) | collective-permute-done | bytes 393248 | tf_op jit(solution)/shard_map/ppermute | solution.py:281
  36.9 1.2 %collective-permute-start.17 = (bf16[64,3072]{1,0:T(8,128)(2,1)S(1)}, bf16[64,3072]{1,0:T(8,128)(2,1)S(1)}, u32[]{:S(2)}, u32[]{:S(2)}) collective-permute-start(bf16[64,3072]{1,0:T(8,128)(2,1)S(1)} %collective-permute-done.3.refs_4_), channel_id=1, source_target_pairs={{0,2},{1,3},{2,0},{3,1},{4,6},{5,7},{6,4},{7,5},{8,10},{9,11},{10,... | collective-permute-start | bytes 1179656 | tf_op jit(solution)/shard_map/ppermute | solution.py:26
  38.1 2.1 %collective-permute-start.16 = (bf16[64,1024]{1,0:T(8,128)(2,1)S(1)}, bf16[64,1024]{1,0:T(8,128)(2,1)S(1)}, u32[]{:S(2)}, u32[]{:S(2)}) collective-permute-start(bf16[64,1024]{1,0:T(8,128)(2,1)S(1)} %get-tuple-element.33), channel_id=1, source_target_pairs={{0,8},{1,9},{2,10},{3,11},{4,12},{5,13},{6,14},{7,15},{8,0},{9,1},... | collective-permute-start | bytes 393224 | tf_op jit(solution)/shard_map/ppermute | solution.py:26
  40.3 1.4 %collective-permute-start.15 = (bf16[64,1024]{1,0:T(8,128)(2,1)S(1)}, bf16[64,1024]{1,0:T(8,128)(2,1)S(1)}, u32[]{:S(2)}, u32[]{:S(2)}) collective-permute-start(bf16[64,1024]{1,0:T(8,128)(2,1)S(1)} %get-tuple-element.31), channel_id=1, source_target_pairs={{0,4},{1,5},{2,6},{3,7},{4,0},{5,1},{6,2},{7,3},{8,12},{9,13},{10,... | collective-permute-start | bytes 393224 | tf_op jit(solution)/shard_map/ppermute | solution.py:26
  41.7 1.0 %copy-done.4 = bf16[1,64,3072]{2,1,0:T(8,128)(2,1)S(1)} copy-done((bf16[1,64,3072]{2,1,0:T(8,128)(2,1)S(1)}, bf16[1,64,3072]{2,1,0:T(8,128)(2,1)}, u32[]{:S(2)}) %copy-start.4) | copy-done | bytes 393240
  42.7 3.0 %shard_map.65.triple = bf16[1024,3072]{1,0:T(8,128)(2,1)S(1)} custom-call(bf16[64,3072]{1,0:T(8,128)(2,1)S(1)} %bitcast.18, bf16[64,3072]{1,0:T(8,128)(2,1)S(1)} %collective-permute-done.refs_1_, bf16[64,3072]{1,0:T(8,128)(2,1)S(1)} %collective-permute-done.1.refs_2_, bf16[64,3072]{1,0:T(8,128)(2,1)S(1)} %collective-permute-done.2.refs_3_, ...), custom_call_target="tpu_custom_call" | custom-call | bytes 12000000 | tf_op jit(solution)/shard_map/pallas_call | solution.py:107
  45.7 1.1 %shard_map.66.started = f32[128,3072]{1,0:T(8,128)S(1)} custom-call(bf16[1024,3072]{1,0:T(8,128)(2,1)S(1)} %shard_map.65.triple, bf16[128,1024]{1,0:T(8,128)(2,1)S(1)} %bitcast.12, f32[1,1024]{1,0:T(1,128)S(1)} %copy-done.6), custom_call_target="tpu_custom_call" | custom-call | flops 800000000 | bytes 8000000 | tf_op jit(solution)/shard_map/pallas_call | solution.py:127
  47.2 1.3 %collective-permute-done.17.refs_6_ = bf16[64,3072]{1,0:T(8,128)(2,1)S(1)} collective-permute-done((bf16[64,3072]{1,0:T(8,128)(2,1)S(1)}, bf16[64,3072]{1,0:T(8,128)(2,1)S(1)}, u32[]{:S(2)}, u32[]{:S(2)}) %collective-permute-start.17) | collective-permute-done | bytes 393248 | tf_op jit(solution)/shard_map/ppermute | solution.py:26
  48.9 1.4 %collective-permute-done.14.refs_0_ = bf16[64,1024]{1,0:T(8,128)(2,1)S(1)} collective-permute-done((bf16[64,1024]{1,0:T(8,128)(2,1)S(1)}, bf16[64,1024]{1,0:T(8,128)(2,1)S(1)}, u32[]{:S(2)}, u32[]{:S(2)}) %collective-permute-start.14) | collective-permute-done | bytes 131104 | tf_op jit(solution)/shard_map/ppermute | solution.py:26
  50.4 3.2 %shard_map.67.refs_8_ = bf16[128,1024]{1,0:T(8,128)(2,1)S(1)} custom-call(bf16[1024,3072]{1,0:T(8,128)(2,1)S(1)} %shard_map.65.triple, bf16[128,1024]{1,0:T(8,128)(2,1)S(1)} %bitcast.13, f32[128,3072]{1,0:T(8,128)S(1)} %shard_map.66.started, bf16[64,1024]{1,0:T(8,128)(2,1)S(1)} %collective-permute-done.14.refs_0_, ...), custom_call_target="tpu_custom_call" | custom-call | flops 2400000000 | bytes 9000000 | tf_op jit(solution)/shard_map/pallas_call | solution.py:249
  53.6 3.4 %collective-permute-start.19 = (bf16[128,1024]{1,0:T(8,128)(2,1)S(1)}, bf16[128,1024]{1,0:T(8,128)(2,1)S(1)}, u32[]{:S(2)}, u32[]{:S(2)}) collective-permute-start(bf16[128,1024]{1,0:T(8,128)(2,1)S(1)} %shard_map.67.refs_8_), channel_id=1, source_target_pairs={{0,16},{1,17},{2,18},{3,19},{4,20},{5,21},{6,22},{7,23},{8,24},{9,... | collective-permute-start | bytes 786440 | tf_op jit(solution)/shard_map/ppermute | solution.py:32
  57.0 5.8 %collective-permute-done.19.moved_ref = bf16[128,1024]{1,0:T(8,128)(2,1)S(1)} collective-permute-done((bf16[128,1024]{1,0:T(8,128)(2,1)S(1)}, bf16[128,1024]{1,0:T(8,128)(2,1)S(1)}, u32[]{:S(2)}, u32[]{:S(2)}) %collective-permute-start.19) | collective-permute-done | bytes 262176 | tf_op jit(solution)/shard_map/ppermute | solution.py:32
  63.1 2.8 %collective-permute-start.23 = (bf16[64,1024]{1,0:T(8,128)(2,1)S(1)}, bf16[64,1024]{1,0:T(8,128)(2,1)S(1)}, u32[]{:S(2)}, u32[]{:S(2)}) collective-permute-start(bf16[64,1024]{1,0:T(8,128)(2,1)S(1)} %get-tuple-element.42), channel_id=1, source_target_pairs={{0,8},{1,9},{2,10},{3,11},{4,12},{5,13},{6,14},{7,15},{8,0},{9,1},... | collective-permute-start | bytes 393224 | tf_op jit(solution)/shard_map/ppermute | solution.py:26
  65.9 1.4 %collective-permute-start.22 = (bf16[64,1024]{1,0:T(8,128)(2,1)S(1)}, bf16[64,1024]{1,0:T(8,128)(2,1)S(1)}, u32[]{:S(2)}, u32[]{:S(2)}) collective-permute-start(bf16[64,1024]{1,0:T(8,128)(2,1)S(1)} %get-tuple-element.41), channel_id=1, source_target_pairs={{0,4},{1,5},{2,6},{3,7},{4,0},{5,1},{6,2},{7,3},{8,12},{9,13},{10,... | collective-permute-start | bytes 393224 | tf_op jit(solution)/shard_map/ppermute | solution.py:26
  67.4 0.5 collective-permute-start.21
  67.9 1.1 %shard_map.69.started = f32[128,3072]{1,0:T(8,128)S(1)} custom-call(bf16[1024,3072]{1,0:T(8,128)(2,1)S(1)} %shard_map.65.triple, bf16[128,1024]{1,0:T(8,128)(2,1)S(1)} %get-tuple-element.36.own_ref, f32[1,1024]{1,0:T(1,128)S(1)} %copy-done.6), custom_call_target="tpu_custom_call" | custom-call | flops 800000000 | bytes 8000000 | tf_op jit(solution)/shard_map/pallas_call | solution.py:127
  69.0 3.8 %collective-permute-done.23.refs_3_ = bf16[64,1024]{1,0:T(8,128)(2,1)S(1)} collective-permute-done((bf16[64,1024]{1,0:T(8,128)(2,1)S(1)}, bf16[64,1024]{1,0:T(8,128)(2,1)S(1)}, u32[]{:S(2)}, u32[]{:S(2)}) %collective-permute-start.23) | collective-permute-done | bytes 131104 | tf_op jit(solution)/shard_map/ppermute | solution.py:26
  72.8 3.9 %shard_map.70 = bf16[2,128,1024]{2,1,0:T(8,128)(2,1)} custom-call(bf16[1024,3072]{1,0:T(8,128)(2,1)S(1)} %shard_map.65.triple, bf16[128,1024]{1,0:T(8,128)(2,1)S(1)} %get-tuple-element.36.own_ref, f32[128,3072]{1,0:T(8,128)S(1)} %shard_map.69.started, bf16[64,1024]{1,0:T(8,128)(2,1)S(1)} %collective-permute-done.20.refs_0_, ...), custom_call_target="tpu_custom_call" | custom-call | flops 2400000000 | bytes 9000000 | tf_op jit(solution)/shard_map/pallas_call | solution.py:261
  (40 shorter events, 2.8 us)
Async XLA Ops:
  0.0 4.6 %copy-start = (s32[16,4]{0,1:T(4,128)S(1)}, s32[16,4]{0,1:T(4,128)}, u32[]{:S(2)}) copy-start(s32[16,4]{0,1:T(4,128)} %param.11) | copy-start | bytes 772
  0.0 7.0 %collective-permute-start = (bf16[64,3072]{1,0:T(8,128)(2,1)}, bf16[64,3072]{1,0:T(8,128)(2,1)S(1)}, u32[]{:S(2)}, u32[]{:S(2)}) collective-permute-start(bf16[64,3072]{1,0:T(8,128)(2,1)} %bitcast.14), channel_id=1, source_target_pairs={{0,1},{1,0},{2,3},{3,2},{4,5},{5,4},{6,7},{7,6},{8,9},{9,8},{10,11... | collective-permute-start | bytes 1179656 | tf_op jit(solution)/shard_map/ppermute | solution.py:26
  0.5 13.6 %collective-permute-start.1 = (bf16[64,3072]{1,0:T(8,128)(2,1)}, bf16[64,3072]{1,0:T(8,128)(2,1)S(1)}, u32[]{:S(2)}, u32[]{:S(2)}) collective-permute-start(bf16[64,3072]{1,0:T(8,128)(2,1)} %bitcast.15), channel_id=1, source_target_pairs={{0,4},{1,5},{2,6},{3,7},{4,12},{5,13},{6,14},{7,15},{8,0},{9,1},{1... | collective-permute-start | bytes 1179656 | tf_op jit(solution)/shard_map/ppermute | solution.py:278
  3.1 12.2 %collective-permute-start.7 = (bf16[64,3072]{1,0:T(8,128)(2,1)}, bf16[64,3072]{1,0:T(8,128)(2,1)S(1)}, u32[]{:S(2)}, u32[]{:S(2)}) collective-permute-start(bf16[64,3072]{1,0:T(8,128)(2,1)} %bitcast.16), channel_id=1, source_target_pairs={{0,2},{1,3},{2,0},{3,1},{4,6},{5,7},{6,4},{7,5},{8,10},{9,11},{10,... | collective-permute-start | bytes 1179656 | tf_op jit(solution)/shard_map/ppermute | solution.py:26
  5.3 1.0 %copy-start.2 = (bf16[1,128,1024]{2,1,0:T(8,128)(2,1)S(1)}, bf16[1,128,1024]{2,1,0:T(8,128)(2,1)}, u32[]{:S(2)}) copy-start(bf16[1,128,1024]{2,1,0:T(8,128)(2,1)} %param.6) | copy-start | bytes 786436
  7.0 10.3 %collective-permute-start.9 = (bf16[64,1024]{1,0:T(8,128)(2,1)S(1)}, bf16[64,1024]{1,0:T(8,128)(2,1)S(1)}, u32[]{:S(2)}, u32[]{:S(2)}) collective-permute-start(bf16[64,1024]{1,0:T(8,128)(2,1)S(1)} %get-tuple-element.26), channel_id=1, source_target_pairs={{0,2},{1,3},{2,0},{3,1},{4,6},{5,7},{6,4},{7,5},{8,10},{9,11},{10,... | collective-permute-start | bytes 393224 | tf_op jit(solution)/shard_map/ppermute | solution.py:26
  14.0 11.8 %collective-permute-start.5 = (bf16[64,3072]{1,0:T(8,128)(2,1)S(1)}, bf16[64,3072]{1,0:T(8,128)(2,1)S(1)}, u32[]{:S(2)}, u32[]{:S(2)}) collective-permute-start(bf16[64,3072]{1,0:T(8,128)(2,1)S(1)} %collective-permute-done.1.refs_2_), channel_id=1, source_target_pairs={{0,4},{1,5},{2,6},{3,7},{4,12},{5,13},{6,14},{7,15},{8,0},{9,1},{1... | collective-permute-start | bytes 1179656 | tf_op jit(solution)/shard_map/ppermute | solution.py:278
  15.0 10.8 %collective-permute-start.2 = (bf16[64,3072]{1,0:T(8,128)(2,1)S(1)}, bf16[64,3072]{1,0:T(8,128)(2,1)S(1)}, u32[]{:S(2)}, u32[]{:S(2)}) collective-permute-start(bf16[64,3072]{1,0:T(8,128)(2,1)S(1)} %collective-permute-done.1.refs_2_), channel_id=1, source_target_pairs={{0,1},{1,0},{2,3},{3,2},{4,5},{5,4},{6,7},{7,6},{8,9},{9,8},{10,11... | collective-permute-start | bytes 1179656 | tf_op jit(solution)/shard_map/ppermute | solution.py:26
  15.3 10.6 %collective-permute-start.8 = (bf16[64,3072]{1,0:T(8,128)(2,1)S(1)}, bf16[64,3072]{1,0:T(8,128)(2,1)S(1)}, u32[]{:S(2)}, u32[]{:S(2)}) collective-permute-start(bf16[64,3072]{1,0:T(8,128)(2,1)S(1)} %collective-permute-done.7.refs_8_), channel_id=1, source_target_pairs={{0,1},{1,0},{2,3},{3,2},{4,5},{5,4},{6,7},{7,6},{8,9},{9,8},{10,11... | collective-permute-start | bytes 1179656 | tf_op jit(solution)/shard_map/ppermute | solution.py:26
  17.3 11.4 %collective-permute-start.10 = (bf16[64,3072]{1,0:T(8,128)(2,1)S(1)}, bf16[64,3072]{1,0:T(8,128)(2,1)S(1)}, u32[]{:S(2)}, u32[]{:S(2)}) collective-permute-start(bf16[64,3072]{1,0:T(8,128)(2,1)S(1)} %collective-permute-done.1.refs_2_), channel_id=1, source_target_pairs={{0,2},{1,3},{2,0},{3,1},{4,6},{5,7},{6,4},{7,5},{8,10},{9,11},{10,... | collective-permute-start | bytes 1179656 | tf_op jit(solution)/shard_map/ppermute | solution.py:26
  25.8 10.3 %collective-permute-start.12 = (bf16[64,3072]{1,0:T(8,128)(2,1)S(1)}, bf16[64,3072]{1,0:T(8,128)(2,1)S(1)}, u32[]{:S(2)}, u32[]{:S(2)}) collective-permute-start(bf16[64,3072]{1,0:T(8,128)(2,1)S(1)} %collective-permute-done.5.refs_6_), channel_id=1, source_target_pairs={{0,2},{1,3},{2,0},{3,1},{4,6},{5,7},{6,4},{7,5},{8,10},{9,11},{10,... | collective-permute-start | bytes 1179656 | tf_op jit(solution)/shard_map/ppermute | solution.py:26
  27.2 9.7 %collective-permute-start.3 = (bf16[64,3072]{1,0:T(8,128)(2,1)}, bf16[64,3072]{1,0:T(8,128)(2,1)S(1)}, u32[]{:S(2)}, u32[]{:S(2)}) collective-permute-start(bf16[64,3072]{1,0:T(8,128)(2,1)} %bitcast.17), channel_id=1, source_target_pairs={{4,0},{5,1},{6,2},{7,3},{12,4},{13,5},{14,6},{15,7},{0,8},{1,9},{2... | collective-permute-start | bytes 1179656 | tf_op jit(solution)/shard_map/ppermute | solution.py:281
  28.7 8.2 %collective-permute-start.6 = (bf16[64,3072]{1,0:T(8,128)(2,1)S(1)}, bf16[64,3072]{1,0:T(8,128)(2,1)S(1)}, u32[]{:S(2)}, u32[]{:S(2)}) collective-permute-start(bf16[64,3072]{1,0:T(8,128)(2,1)S(1)} %collective-permute-done.5.refs_6_), channel_id=1, source_target_pairs={{0,1},{1,0},{2,3},{3,2},{4,5},{5,4},{6,7},{7,6},{8,9},{9,8},{10,11... | collective-permute-start | bytes 1179656 | tf_op jit(solution)/shard_map/ppermute | solution.py:26
  28.7 8.2 %collective-permute-start.11 = (bf16[64,3072]{1,0:T(8,128)(2,1)S(1)}, bf16[64,3072]{1,0:T(8,128)(2,1)S(1)}, u32[]{:S(2)}, u32[]{:S(2)}) collective-permute-start(bf16[64,3072]{1,0:T(8,128)(2,1)S(1)} %collective-permute-done.10.refs_10_), channel_id=1, source_target_pairs={{0,1},{1,0},{2,3},{3,2},{4,5},{5,4},{6,7},{7,6},{8,9},{9,8},{10,11... | collective-permute-start | bytes 1179656 | tf_op jit(solution)/shard_map/ppermute | solution.py:26
  36.1 5.6 %collective-permute-start.13 = (bf16[64,3072]{1,0:T(8,128)(2,1)S(1)}, bf16[64,3072]{1,0:T(8,128)(2,1)S(1)}, u32[]{:S(2)}, u32[]{:S(2)}) collective-permute-start(bf16[64,3072]{1,0:T(8,128)(2,1)S(1)} %collective-permute-done.12.refs_12_), channel_id=1, source_target_pairs={{0,1},{1,0},{2,3},{3,2},{4,5},{5,4},{6,7},{7,6},{8,9},{9,8},{10,11... | collective-permute-start | bytes 1179656 | tf_op jit(solution)/shard_map/ppermute | solution.py:26
  36.9 4.8 %collective-permute-start.4 = (bf16[64,3072]{1,0:T(8,128)(2,1)S(1)}, bf16[64,3072]{1,0:T(8,128)(2,1)S(1)}, u32[]{:S(2)}, u32[]{:S(2)}) collective-permute-start(bf16[64,3072]{1,0:T(8,128)(2,1)S(1)} %collective-permute-done.3.refs_4_), channel_id=1, source_target_pairs={{0,1},{1,0},{2,3},{3,2},{4,5},{5,4},{6,7},{7,6},{8,9},{9,8},{10,11... | collective-permute-start | bytes 1179656 | tf_op jit(solution)/shard_map/ppermute | solution.py:26
  36.9 11.5 %collective-permute-start.17 = (bf16[64,3072]{1,0:T(8,128)(2,1)S(1)}, bf16[64,3072]{1,0:T(8,128)(2,1)S(1)}, u32[]{:S(2)}, u32[]{:S(2)}) collective-permute-start(bf16[64,3072]{1,0:T(8,128)(2,1)S(1)} %collective-permute-done.3.refs_4_), channel_id=1, source_target_pairs={{0,2},{1,3},{2,0},{3,1},{4,6},{5,7},{6,4},{7,5},{8,10},{9,11},{10,... | collective-permute-start | bytes 1179656 | tf_op jit(solution)/shard_map/ppermute | solution.py:26
  38.1 8.8 %collective-permute-start.16 = (bf16[64,1024]{1,0:T(8,128)(2,1)S(1)}, bf16[64,1024]{1,0:T(8,128)(2,1)S(1)}, u32[]{:S(2)}, u32[]{:S(2)}) collective-permute-start(bf16[64,1024]{1,0:T(8,128)(2,1)S(1)} %get-tuple-element.33), channel_id=1, source_target_pairs={{0,8},{1,9},{2,10},{3,11},{4,12},{5,13},{6,14},{7,15},{8,0},{9,1},... | collective-permute-start | bytes 393224 | tf_op jit(solution)/shard_map/ppermute | solution.py:26
  40.3 5.4 %copy-start.3 = (bf16[1,128,1024]{2,1,0:T(8,128)(2,1)S(1)}, bf16[1,128,1024]{2,1,0:T(8,128)(2,1)}, u32[]{:S(2)}) copy-start(bf16[1,128,1024]{2,1,0:T(8,128)(2,1)} %param.6) | copy-start | bytes 786436
  40.3 6.9 %collective-permute-start.15 = (bf16[64,1024]{1,0:T(8,128)(2,1)S(1)}, bf16[64,1024]{1,0:T(8,128)(2,1)S(1)}, u32[]{:S(2)}, u32[]{:S(2)}) collective-permute-start(bf16[64,1024]{1,0:T(8,128)(2,1)S(1)} %get-tuple-element.31), channel_id=1, source_target_pairs={{0,4},{1,5},{2,6},{3,7},{4,0},{5,1},{6,2},{7,3},{8,12},{9,13},{10,... | collective-permute-start | bytes 393224 | tf_op jit(solution)/shard_map/ppermute | solution.py:26
  41.7 1.0 %copy-start.4 = (bf16[1,64,3072]{2,1,0:T(8,128)(2,1)S(1)}, bf16[1,64,3072]{2,1,0:T(8,128)(2,1)}, u32[]{:S(2)}) copy-start(bf16[1,64,3072]{2,1,0:T(8,128)(2,1)} %param.9) | copy-start | bytes 1179652
  42.7 3.0 %copy-start.6 = (f32[1,1024]{1,0:T(1,128)S(1)}, f32[1,1024]{1,0:T(1,128)}, u32[]{:S(2)}) copy-start(f32[1,1024]{1,0:T(1,128)} %refs_4_.3) | copy-start | bytes 12292
  45.7 4.7 %copy-start.1 = (bf16[1,1024,1024]{2,1,0:T(8,128)(2,1)S(1)}, bf16[1,1024,1024]{2,1,0:T(8,128)(2,1)}, u32[]{:S(2)}) copy-start(bf16[1,1024,1024]{2,1,0:T(8,128)(2,1)} %param.10) | copy-start | bytes 6291460
  48.4 1.9 %collective-permute-start.18 = (bf16[64,3072]{1,0:T(8,128)(2,1)S(1)}, bf16[64,3072]{1,0:T(8,128)(2,1)S(1)}, u32[]{:S(2)}, u32[]{:S(2)}) collective-permute-start(bf16[64,3072]{1,0:T(8,128)(2,1)S(1)} %collective-permute-done.17.refs_6_), channel_id=1, source_target_pairs={{0,1},{1,0},{2,3},{3,2},{4,5},{5,4},{6,7},{7,6},{8,9},{9,8},{10,11... | collective-permute-start | bytes 1179656 | tf_op jit(solution)/shard_map/ppermute | solution.py:26
  48.4 1.9 %collective-permute-start.14 = (bf16[64,1024]{1,0:T(8,128)(2,1)S(1)}, bf16[64,1024]{1,0:T(8,128)(2,1)S(1)}, u32[]{:S(2)}, u32[]{:S(2)}) collective-permute-start(bf16[64,1024]{1,0:T(8,128)(2,1)S(1)} %get-tuple-element.29), channel_id=1, source_target_pairs={{0,1},{1,0},{2,3},{3,2},{4,5},{5,4},{6,7},{7,6},{8,9},{9,8},{10,11... | collective-permute-start | bytes 393224 | tf_op jit(solution)/shard_map/ppermute | solution.py:26
  50.4 12.5 %copy-start.5 = (bf16[128,1024]{1,0:T(8,128)(2,1)S(1)}, bf16[128,1024]{1,0:T(8,128)(2,1)}, u32[]{:S(2)}) copy-start(bf16[128,1024]{1,0:T(8,128)(2,1)} %arriving_ref.1) | copy-start | bytes 786436
  53.6 9.3 %collective-permute-start.19 = (bf16[128,1024]{1,0:T(8,128)(2,1)S(1)}, bf16[128,1024]{1,0:T(8,128)(2,1)S(1)}, u32[]{:S(2)}, u32[]{:S(2)}) collective-permute-start(bf16[128,1024]{1,0:T(8,128)(2,1)S(1)} %shard_map.67.refs_8_), channel_id=1, source_target_pairs={{0,16},{1,17},{2,18},{3,19},{4,20},{5,21},{6,22},{7,23},{8,24},{9,... | collective-permute-start | bytes 786440 | tf_op jit(solution)/shard_map/ppermute | solution.py:32
  63.0 2.9 %collective-permute-start.20 = (bf16[64,1024]{1,0:T(8,128)(2,1)S(1)}, bf16[64,1024]{1,0:T(8,128)(2,1)S(1)}, u32[]{:S(2)}, u32[]{:S(2)}) collective-permute-start(bf16[64,1024]{1,0:T(8,128)(2,1)S(1)} %get-tuple-element.37), channel_id=1, source_target_pairs={{0,1},{1,0},{2,3},{3,2},{4,5},{5,4},{6,7},{7,6},{8,9},{9,8},{10,11... | collective-permute-start | bytes 393224 | tf_op jit(solution)/shard_map/ppermute | solution.py:26
  63.1 9.7 %collective-permute-start.23 = (bf16[64,1024]{1,0:T(8,128)(2,1)S(1)}, bf16[64,1024]{1,0:T(8,128)(2,1)S(1)}, u32[]{:S(2)}, u32[]{:S(2)}) collective-permute-start(bf16[64,1024]{1,0:T(8,128)(2,1)S(1)} %get-tuple-element.42), channel_id=1, source_target_pairs={{0,8},{1,9},{2,10},{3,11},{4,12},{5,13},{6,14},{7,15},{8,0},{9,1},... | collective-permute-start | bytes 393224 | tf_op jit(solution)/shard_map/ppermute | solution.py:26
  65.9 6.9 %collective-permute-start.22 = (bf16[64,1024]{1,0:T(8,128)(2,1)S(1)}, bf16[64,1024]{1,0:T(8,128)(2,1)S(1)}, u32[]{:S(2)}, u32[]{:S(2)}) collective-permute-start(bf16[64,1024]{1,0:T(8,128)(2,1)S(1)} %get-tuple-element.41), channel_id=1, source_target_pairs={{0,4},{1,5},{2,6},{3,7},{4,0},{5,1},{6,2},{7,3},{8,12},{9,13},{10,... | collective-permute-start | bytes 393224 | tf_op jit(solution)/shard_map/ppermute | solution.py:26
  67.4 5.5 %collective-permute-start.21 = (bf16[64,1024]{1,0:T(8,128)(2,1)S(1)}, bf16[64,1024]{1,0:T(8,128)(2,1)S(1)}, u32[]{:S(2)}, u32[]{:S(2)}) collective-permute-start(bf16[64,1024]{1,0:T(8,128)(2,1)S(1)} %get-tuple-element.39), channel_id=1, source_target_pairs={{0,2},{1,3},{2,0},{3,1},{4,6},{5,7},{6,4},{7,5},{8,10},{9,11},{10,... | collective-permute-start | bytes 393224 | tf_op jit(solution)/shard_map/ppermute | solution.py:26

commit v5 on v4

--- a/solution.py
+++ b/solution.py
@@ -115,27 +115,36 @@
     )(*pieces)
 
 
-def ahead_kernel(triple, own_ref, gain_ref, out_ref, normed):
-    normed[...] = row_norm(own_ref[...], gain_ref[...])
-    for start in range(0, triple.shape[1], WIDE):
-        span = slice(start, start + WIDE)
-        out_ref[:, span] = jnp.dot(normed[...], triple[:, span], preferred_element_type=jnp.float32)
-
-
-def ahead(triple, own, gain):
-    rows, width = own.shape
+def ahead_kernel(first_column, triple, *refs):
+    tokens, (gain_ref, out_ref, normed) = refs[:-3], refs[-3:]
+    low = 0
+    for part in tokens:
+        high = low + part.shape[0]
+        normed[low:high] = row_norm(part[...], gain_ref[...])
+        low = high
+    for start in range(0, out_ref.shape[1], WIDE):
+        out_ref[:, start : start + WIDE] = jnp.dot(
+            normed[...],
+            triple[:, first_column + start : first_column + start + WIDE],
+            preferred_element_type=jnp.float32,
+        )
+
+
+def ahead(triple, tokens, gain, first_column):
+    rows = sum(part.shape[0] for part in tokens)
+    width = tokens[0].shape[1]
     return pl.pallas_call(
-        ahead_kernel,
-        out_shape=pltpu.VMEM((rows, triple.shape[1]), jnp.float32),
-        in_specs=[in_vmem] * 3,
+        functools.partial(ahead_kernel, first_column),
+        out_shape=pltpu.VMEM((rows, triple.shape[1] - first_column), jnp.float32),
+        in_specs=[in_vmem] * (2 + len(tokens)),
         out_specs=in_vmem,
         scratch_shapes=[pltpu.VMEM((rows, width), jnp.bfloat16)],
         compiler_params=pltpu.CompilerParams(vmem_limit_bytes=4 * MIB),
         cost_estimate=pl.CostEstimate(flops=800_000_000, bytes_accessed=8_000_000, transcendentals=0),
-    )(triple, own, gain)
-
-
-def attend(own_ref, started, fars, gain_ref, triple, exit_ref, latest, put, normed, queries, keys, values, attended, last):
+    )(triple, *tokens, gain)
+
+
+def attend(own_ref, started, far_started, fars, gain_ref, triple, exit_ref, latest, put, normed, queries, keys, values, attended, last):
     inner = HEADS * HEAD
     rows = own_ref.shape[0]
     far_rows = LEVELS * BLOCK
@@ -160,7 +169,10 @@
 
     def far_part(start):
         span = slice(start, start + WIDE)
-        result = jnp.dot(normed[rows:], triple[:, span], preferred_element_type=jnp.float32)
+        if far_started is None:
+            result = jnp.dot(normed[rows:], triple[:, span], preferred_element_type=jnp.float32)
+        else:
+            result = far_started[:, start - inner : start - inner + WIDE]
         if latest:
             result += jnp.dot(late_columns[rows:], last[:, span], preferred_element_type=jnp.float32)
         return result
@@ -206,12 +218,12 @@
         ).astype(jnp.bfloat16)
 
 
-def first_kernel(late, triple, own_ref, started, *refs):
+def first_kernel(late, far_started, own_ref, started, *refs):
     fars, refs = refs[:LEVELS], refs[LEVELS:]
     gain_ref, exit_ref, *refs = refs
     latest, refs = refs[:late], refs[late:]
     out_ref, *scratch = refs
-    attend(own_ref, started, fars, gain_ref, triple, exit_ref, latest, out_ref, *scratch)
+    attend(own_ref, started, far_started, fars, gain_ref, None, exit_ref, latest, out_ref, *scratch)
 
 
 def second_kernel(late, triple, own_ref, started, *refs):
@@ -221,7 +233,7 @@
     first_ref, out_ref, result, sems, *scratch = refs
     early = pltpu.make_async_copy(first_ref, out_ref.at[0], sems.at[0])
     early.start()
-    attend(own_ref, started, fars, gain_ref, triple, exit_ref, latest, result, *scratch)
+    attend(own_ref, started, None, fars, gain_ref, triple, exit_ref, latest, result, *scratch)
     finish = pltpu.make_async_copy(result, out_ref.at[1], sems.at[1])
     finish.start()
     early.wait()
@@ -245,16 +257,16 @@
 cost = pl.CostEstimate(flops=2_400_000_000, bytes_accessed=9_000_000, transcendentals=400_000)
 
 
-def first_layer(triple, own, started, fars, gain, exit_matrix, latest):
+def first_layer(far_started, own, started, fars, gain, exit_matrix, latest):
     return pl.pallas_call(
         functools.partial(first_kernel, len(latest)),
         out_shape=jax.ShapeDtypeStruct(own.shape, own.dtype),
         in_specs=[in_vmem] * (5 + LEVELS + len(latest)),
         out_specs=in_vmem,
-        scratch_shapes=scratch_of(*own.shape, triple, latest),
+        scratch_shapes=scratch_of(*own.shape, started, latest),
         compiler_params=pltpu.CompilerParams(vmem_limit_bytes=16 * MIB),
         cost_estimate=cost,
-    )(triple, own, started, *fars, gain, exit_matrix, *latest)
+    )(far_started, own, started, *fars, gain, exit_matrix, *latest)
 
 
 def second_layer(triple, own, started, fars, gain, exit_matrix, latest, first_out):
@@ -288,9 +300,9 @@
 
     r1 = around(shard)
     x0 = beside(shard)
-    c0 = twin(shard)
-    near = [twin(chosen[0]), beside(after(chosen[1], c0))]
-    r2 = around(r1)
+    near = [twin(chosen[0]), beside(chosen[1])]
+    c0 = twin(after(shard, near[0]))
+    r2 = around(after(r1, near[0]))
     cr1 = twin(r1)
     x1 = beside(after(r1, near[1]))
     l1 = back(after(shard, cr1))
@@ -319,8 +331,10 @@
         (cx2, 2, 1, 1),
     ]
     triple = assembled([piece for piece, *_ in early], [tuple(hops) for _, *hops in early])
-    started = ahead(triple, own, gain)
-    return triple, started, [x3, twin(after(x3, started, *far))], near + far[::-1]
+    fars = near + far[::-1]
+    started = ahead(triple, [own], gain, 0)
+    far_started = ahead(triple, fars, gain, HEADS * HEAD)
+    return triple, started, far_started, [x3, twin(after(x3, started, *far))], fars
 
 
 def partner_rows(chosen):
@@ -337,17 +351,18 @@
     wanted = jnp.broadcast_to(lookup[partner, levels % LEVELS][:, None], (8, 128))
     _, chosen = choose(wanted, first_in, first_in)
     if lax.axis_size("seq") == 16:
-        triple, started, latest, fars = gathered(triple[0], chosen, first_in, gain)
+        triple, started, far_started, latest, fars = gathered(triple[0], chosen, first_in, gain)
     else:
         triple = lax.all_gather(triple[0], "seq", axis=0, tiled=True)
-        started = ahead(triple, first_in, gain)
+        fars = partner_rows(chosen)
+        started = ahead(triple, [first_in], gain, 0)
+        far_started = ahead(triple, fars, gain, HEADS * HEAD)
         latest = []
-        fars = partner_rows(chosen)
-    first_out = first_layer(triple, first_in, started, fars, gain, exit_matrix[0], latest)
+    first_out = first_layer(far_started, first_in, started, fars, gain, exit_matrix[0], latest)
     moved = from_behind(first_out, "section", 1)
     second_in, chosen = choose(wanted, moved, arriving)
     fars = partner_rows(chosen)
-    return second_layer(triple, second_in, ahead(triple, second_in, gain), fars, gain, exit_matrix[0], latest, first_out)[:, None]
+    return second_layer(triple, second_in, ahead(triple, [second_in], gain, 0), fars, gain, exit_matrix[0], latest, first_out)[:, None]
 
 
 def solution(mesh):

time: 76.9 us -> 74.2 us (0.965)
  waiting for transfers between devices: 36 us -> 32.8 us
    ppermute x2, waiting for transfers between devices: 13.5 us -> 11.5 us  [around(): lax.ppermute(x, 'seq', [(i, onward[i // 4] * 4 + i % 4) for i in range(16)])]
    pallas_call x2 -> x3, Pallas kernels: 2.13 us -> 3.52 us  [ahead(): pl.pallas_call(functools.partial(ahead_kernel, first_column), out_shape=p...]
    pallas_call x1, Pallas kernels: 3.19 us -> 2.3 us  [first_layer(): pl.pallas_call(functools.partial(first_kernel, len(latest)), out_shape=ja...]
    ppermute x1, waiting for transfers between devices: 0.8 us -> 0.01 us  [back(): lax.ppermute(x, 'seq', [(onward[i // 4] * 4 + i % 4, i) for i in range(16)])]
  transfers between devices with their start and end apart: 24 -> 24, of which waited for: 12 -> 13; matrix products, arithmetic and copies ran while one was open for 1% -> 1% of each run, Pallas kernels for 8% -> 10%
where the time goes in v5:
time: 74.2 us; the launch traced here: 74 us
  waiting for transfers between devices  32.8 us (44%)
  starting transfers between devices  24.7 us (33%)
  Pallas kernels  13.6 us (18%)
  local copies, waits for them, and re-layouts  2.7 us (4%)
    ppermute x20, starting transfers between devices, swapped(): lax.ppermute(x, axis, [(i, i ^ mask) for i in range(lax.axis_size(axis))])  15.8 us
    ppermute x20, waiting for transfers between devices, swapped(): lax.ppermute(x, axis, [(i, i ^ mask) for i in range(lax.axis_size(axis))])  15.4 us
    ppermute x2, waiting for transfers between devices, around(): lax.ppermute(x, 'seq', [(i, onward[i // 4] * 4 + i % 4) for i in range(16)])  11.5 us
    ppermute x1, waiting for transfers between devices, from_behind(): return lax.ppermute(block, axis, route)  5.9 us
    ppermute x2, starting transfers between devices, around(): lax.ppermute(x, 'seq', [(i, onward[i // 4] * 4 + i % 4) for i in range(16)])  3.97 us
    pallas_call x1, Pallas kernels, second_layer(): pl.pallas_call(functools.partial(second_kernel, len(latest)), out_shape=j...  3.92 us
    pallas_call x3, Pallas kernels, ahead(): pl.pallas_call(functools.partial(ahead_kernel, first_column), out_shape=p...  3.52 us
    ppermute x1, starting transfers between devices, from_behind(): return lax.ppermute(block, axis, route)  3.44 us
  transfers between devices with their start and end apart: 24, of which 13 were waited for; matrix products, arithmetic and copies ran while one was open for 1% of the time, Pallas kernels for 10%

profile of v5, /device:TPU:0, one launch (start us, length us, event | category | flops | bytes accessed | tf_op | source)
XLA Modules:
  0.0 74.0 jit_solution(2961839378900317366)
XLA Ops:
  0.0 3.0 %collective-permute-start.2 = (bf16[64,3072]{1,0:T(8,128)(2,1)}, bf16[64,3072]{1,0:T(8,128)(2,1)S(1)}, u32[]{:S(2)}, u32[]{:S(2)}) collective-permute-start(bf16[64,3072]{1,0:T(8,128)(2,1)} %bitcast.14), channel_id=1, source_target_pairs={{0,4},{1,5},{2,6},{3,7},{4,12},{5,13},{6,14},{7,15},{8,0},{9,1},{1... | collective-permute-start | bytes 1179656 | tf_op jit(solution)/shard_map/ppermute | solution.py:290
  3.0 1.5 %collective-permute-start.8 = (bf16[64,3072]{1,0:T(8,128)(2,1)}, bf16[64,3072]{1,0:T(8,128)(2,1)S(1)}, u32[]{:S(2)}, u32[]{:S(2)}) collective-permute-start(bf16[64,3072]{1,0:T(8,128)(2,1)} %bitcast.15), channel_id=1, source_target_pairs={{0,2},{1,3},{2,0},{3,1},{4,6},{5,7},{6,4},{7,5},{8,10},{9,11},{10,... | collective-permute-start | bytes 1179656 | tf_op jit(solution)/shard_map/ppermute | solution.py:26
  4.5 0.7 gather_fusion
  5.3 1.0 %copy-done.1 = bf16[1,128,1024]{2,1,0:T(8,128)(2,1)S(1)} copy-done((bf16[1,128,1024]{2,1,0:T(8,128)(2,1)S(1)}, bf16[1,128,1024]{2,1,0:T(8,128)(2,1)}, u32[]{:S(2)}) %copy-start.1) | copy-done | bytes 262168
  6.2 0.7 shard_map.64
  7.5 0.8 %collective-permute-done.refs_0_ = bf16[64,1024]{1,0:T(8,128)(2,1)S(1)} collective-permute-done((bf16[64,1024]{1,0:T(8,128)(2,1)S(1)}, bf16[64,1024]{1,0:T(8,128)(2,1)S(1)}, u32[]{:S(2)}, u32[]{:S(2)}) %collective-permute-start) | collective-permute-done | bytes 131104 | tf_op jit(solution)/shard_map/ppermute | solution.py:26
  8.3 5.0 %collective-permute-done.2.refs_2_ = bf16[64,3072]{1,0:T(8,128)(2,1)S(1)} collective-permute-done((bf16[64,3072]{1,0:T(8,128)(2,1)}, bf16[64,3072]{1,0:T(8,128)(2,1)S(1)}, u32[]{:S(2)}, u32[]{:S(2)}) %collective-permute-start.2) | collective-permute-done | bytes 393248 | tf_op jit(solution)/shard_map/ppermute | solution.py:290
  13.4 0.9 %collective-permute-start.6 = (bf16[64,3072]{1,0:T(8,128)(2,1)S(1)}, bf16[64,3072]{1,0:T(8,128)(2,1)S(1)}, u32[]{:S(2)}, u32[]{:S(2)}) collective-permute-start(bf16[64,3072]{1,0:T(8,128)(2,1)S(1)} %collective-permute-done.2.refs_2_), channel_id=1, source_target_pairs={{0,4},{1,5},{2,6},{3,7},{4,12},{5,13},{6,14},{7,15},{8,0},{9,1},{1... | collective-permute-start | bytes 1179656 | tf_op jit(solution)/shard_map/ppermute | solution.py:290
  14.3 0.9 %collective-permute-done.8.refs_8_ = bf16[64,3072]{1,0:T(8,128)(2,1)S(1)} collective-permute-done((bf16[64,3072]{1,0:T(8,128)(2,1)}, bf16[64,3072]{1,0:T(8,128)(2,1)S(1)}, u32[]{:S(2)}, u32[]{:S(2)}) %collective-permute-start.8) | collective-permute-done | bytes 393248 | tf_op jit(solution)/shard_map/ppermute | solution.py:26
  15.2 1.4 %collective-permute-done.10.refs_1_ = bf16[64,1024]{1,0:T(8,128)(2,1)S(1)} collective-permute-done((bf16[64,1024]{1,0:T(8,128)(2,1)S(1)}, bf16[64,1024]{1,0:T(8,128)(2,1)S(1)}, u32[]{:S(2)}, u32[]{:S(2)}) %collective-permute-start.10) | collective-permute-done | bytes 131104 | tf_op jit(solution)/shard_map/ppermute | solution.py:26
  16.6 1.5 %collective-permute-start.11 = (bf16[64,3072]{1,0:T(8,128)(2,1)S(1)}, bf16[64,3072]{1,0:T(8,128)(2,1)S(1)}, u32[]{:S(2)}, u32[]{:S(2)}) collective-permute-start(bf16[64,3072]{1,0:T(8,128)(2,1)S(1)} %collective-permute-done.2.refs_2_), channel_id=1, source_target_pairs={{0,2},{1,3},{2,0},{3,1},{4,6},{5,7},{6,4},{7,5},{8,10},{9,11},{10,... | collective-permute-start | bytes 1179656 | tf_op jit(solution)/shard_map/ppermute | solution.py:26
  18.1 6.4 %collective-permute-done.6.refs_6_ = bf16[64,3072]{1,0:T(8,128)(2,1)S(1)} collective-permute-done((bf16[64,3072]{1,0:T(8,128)(2,1)S(1)}, bf16[64,3072]{1,0:T(8,128)(2,1)S(1)}, u32[]{:S(2)}, u32[]{:S(2)}) %collective-permute-start.6) | collective-permute-done | bytes 393248 | tf_op jit(solution)/shard_map/ppermute | solution.py:290
  24.6 1.2 %collective-permute-start.13 = (bf16[64,3072]{1,0:T(8,128)(2,1)S(1)}, bf16[64,3072]{1,0:T(8,128)(2,1)S(1)}, u32[]{:S(2)}, u32[]{:S(2)}) collective-permute-start(bf16[64,3072]{1,0:T(8,128)(2,1)S(1)} %collective-permute-done.6.refs_6_), channel_id=1, source_target_pairs={{0,2},{1,3},{2,0},{3,1},{4,6},{5,7},{6,4},{7,5},{8,10},{9,11},{10,... | collective-permute-start | bytes 1179656 | tf_op jit(solution)/shard_map/ppermute | solution.py:26
  25.8 1.5 %collective-permute-start.4 = (bf16[64,3072]{1,0:T(8,128)(2,1)}, bf16[64,3072]{1,0:T(8,128)(2,1)S(1)}, u32[]{:S(2)}, u32[]{:S(2)}) collective-permute-start(bf16[64,3072]{1,0:T(8,128)(2,1)} %bitcast.16), channel_id=1, source_target_pairs={{4,0},{5,1},{6,2},{7,3},{12,4},{13,5},{14,6},{15,7},{0,8},{1,9},{2... | collective-permute-start | bytes 1179656 | tf_op jit(solution)/shard_map/ppermute | solution.py:293
  28.4 6.8 %collective-permute-done.13.refs_12_ = bf16[64,3072]{1,0:T(8,128)(2,1)S(1)} collective-permute-done((bf16[64,3072]{1,0:T(8,128)(2,1)S(1)}, bf16[64,3072]{1,0:T(8,128)(2,1)S(1)}, u32[]{:S(2)}, u32[]{:S(2)}) %collective-permute-start.13) | collective-permute-done | bytes 393248 | tf_op jit(solution)/shard_map/ppermute | solution.py:26
  35.7 1.5 %collective-permute-start.17 = (bf16[64,3072]{1,0:T(8,128)(2,1)S(1)}, bf16[64,3072]{1,0:T(8,128)(2,1)S(1)}, u32[]{:S(2)}, u32[]{:S(2)}) collective-permute-start(bf16[64,3072]{1,0:T(8,128)(2,1)S(1)} %collective-permute-done.4.refs_4_), channel_id=1, source_target_pairs={{0,2},{1,3},{2,0},{3,1},{4,6},{5,7},{6,4},{7,5},{8,10},{9,11},{10,... | collective-permute-start | bytes 1179656 | tf_op jit(solution)/shard_map/ppermute | solution.py:26
  37.2 1.4 %collective-permute-start.16 = (bf16[64,1024]{1,0:T(8,128)(2,1)S(1)}, bf16[64,1024]{1,0:T(8,128)(2,1)S(1)}, u32[]{:S(2)}, u32[]{:S(2)}) collective-permute-start(bf16[64,1024]{1,0:T(8,128)(2,1)S(1)} %get-tuple-element.35), channel_id=1, source_target_pairs={{0,8},{1,9},{2,10},{3,11},{4,12},{5,13},{6,14},{7,15},{8,0},{9,1},... | collective-permute-start | bytes 393224 | tf_op jit(solution)/shard_map/ppermute | solution.py:26
  38.6 1.7 %collective-permute-start.15 = (bf16[64,1024]{1,0:T(8,128)(2,1)S(1)}, bf16[64,1024]{1,0:T(8,128)(2,1)S(1)}, u32[]{:S(2)}, u32[]{:S(2)}) collective-permute-start(bf16[64,1024]{1,0:T(8,128)(2,1)S(1)} %get-tuple-element.33), channel_id=1, source_target_pairs={{0,4},{1,5},{2,6},{3,7},{4,0},{5,1},{6,2},{7,3},{8,12},{9,13},{10,... | collective-permute-start | bytes 393224 | tf_op jit(solution)/shard_map/ppermute | solution.py:26
  40.2 1.0 %copy-done.4 = bf16[1,64,3072]{2,1,0:T(8,128)(2,1)S(1)} copy-done((bf16[1,64,3072]{2,1,0:T(8,128)(2,1)S(1)}, bf16[1,64,3072]{2,1,0:T(8,128)(2,1)}, u32[]{:S(2)}) %copy-start.4) | copy-done | bytes 393240
  41.2 3.0 %shard_map.65.triple = bf16[1024,3072]{1,0:T(8,128)(2,1)S(1)} custom-call(bf16[64,3072]{1,0:T(8,128)(2,1)S(1)} %bitcast.18, bf16[64,3072]{1,0:T(8,128)(2,1)S(1)} %collective-permute-done.1.refs_1_, bf16[64,3072]{1,0:T(8,128)(2,1)S(1)} %collective-permute-done.2.refs_2_, bf16[64,3072]{1,0:T(8,128)(2,1)S(1)} %collective-permute-done.3.refs_3_, ...), custom_call_target="tpu_custom_call" | custom-call | bytes 12000000 | tf_op jit(solution)/shard_map/pallas_call | solution.py:107
  44.2 1.1 %shard_map.67.started = f32[128,3072]{1,0:T(8,128)S(1)} custom-call(bf16[1024,3072]{1,0:T(8,128)(2,1)S(1)} %shard_map.65.triple, bf16[128,1024]{1,0:T(8,128)(2,1)S(1)} %bitcast.10, f32[1,1024]{1,0:T(1,128)S(1)} %copy-done.6), custom_call_target="tpu_custom_call" | custom-call | flops 800000000 | bytes 8000000 | tf_op jit(solution)/shard_map/pallas_call | solution.py:136
  46.1 0.7 collective-permute-done.17.refs_6_
  46.8 1.4 %shard_map.66.far_started = f32[256,2048]{1,0:T(8,128)S(1)} custom-call(bf16[1024,3072]{1,0:T(8,128)(2,1)S(1)} %shard_map.65.triple, bf16[64,1024]{1,0:T(8,128)(2,1)S(1)} %collective-permute-done.refs_0_, bf16[64,1024]{1,0:T(8,128)(2,1)S(1)} %collective-permute-done.10.refs_1_, bf16[64,1024]{1,0:T(8,128)(2,1)S(1)} %collective-permute-done.15.refs_2_, ...), custom_call_target="tpu_custom_call" | custom-call | flops 800000000 | bytes 8000000 | tf_op jit(solution)/shard_map/pallas_call | solution.py:136
  48.5 2.3 %shard_map.68.refs_8_ = bf16[128,1024]{1,0:T(8,128)(2,1)S(1)} custom-call(f32[256,2048]{1,0:T(8,128)S(1)} %shard_map.66.far_started, bf16[128,1024]{1,0:T(8,128)(2,1)S(1)} %bitcast.11, f32[128,3072]{1,0:T(8,128)S(1)} %shard_map.67.started, bf16[64,1024]{1,0:T(8,128)(2,1)S(1)} %collective-permute-done.refs_0_, ...), custom_call_target="tpu_custom_call" | custom-call | flops 2400000000 | bytes 9000000 | tf_op jit(solution)/shard_map/pallas_call | solution.py:261
  50.8 3.4 %collective-permute-start.19 = (bf16[128,1024]{1,0:T(8,128)(2,1)S(1)}, bf16[128,1024]{1,0:T(8,128)(2,1)S(1)}, u32[]{:S(2)}, u32[]{:S(2)}) collective-permute-start(bf16[128,1024]{1,0:T(8,128)(2,1)S(1)} %shard_map.68.refs_8_), channel_id=1, source_target_pairs={{0,16},{1,17},{2,18},{3,19},{4,20},{5,21},{6,22},{7,23},{8,24},{9,... | collective-permute-start | bytes 786440 | tf_op jit(solution)/shard_map/ppermute | solution.py:32
  54.3 5.9 %collective-permute-done.19.moved_ref = bf16[128,1024]{1,0:T(8,128)(2,1)S(1)} collective-permute-done((bf16[128,1024]{1,0:T(8,128)(2,1)S(1)}, bf16[128,1024]{1,0:T(8,128)(2,1)S(1)}, u32[]{:S(2)}, u32[]{:S(2)}) %collective-permute-start.19) | collective-permute-done | bytes 262176 | tf_op jit(solution)/shard_map/ppermute | solution.py:32
  60.5 2.3 %collective-permute-start.23 = (bf16[64,1024]{1,0:T(8,128)(2,1)S(1)}, bf16[64,1024]{1,0:T(8,128)(2,1)S(1)}, u32[]{:S(2)}, u32[]{:S(2)}) collective-permute-start(bf16[64,1024]{1,0:T(8,128)(2,1)S(1)} %get-tuple-element.44), channel_id=1, source_target_pairs={{0,8},{1,9},{2,10},{3,11},{4,12},{5,13},{6,14},{7,15},{8,0},{9,1},... | collective-permute-start | bytes 393224 | tf_op jit(solution)/shard_map/ppermute | solution.py:26
  62.8 1.6 %collective-permute-start.22 = (bf16[64,1024]{1,0:T(8,128)(2,1)S(1)}, bf16[64,1024]{1,0:T(8,128)(2,1)S(1)}, u32[]{:S(2)}, u32[]{:S(2)}) collective-permute-start(bf16[64,1024]{1,0:T(8,128)(2,1)S(1)} %get-tuple-element.43), channel_id=1, source_target_pairs={{0,4},{1,5},{2,6},{3,7},{4,0},{5,1},{6,2},{7,3},{8,12},{9,13},{10,... | collective-permute-start | bytes 393224 | tf_op jit(solution)/shard_map/ppermute | solution.py:26
  64.4 1.5 %collective-permute-start.21 = (bf16[64,1024]{1,0:T(8,128)(2,1)S(1)}, bf16[64,1024]{1,0:T(8,128)(2,1)S(1)}, u32[]{:S(2)}, u32[]{:S(2)}) collective-permute-start(bf16[64,1024]{1,0:T(8,128)(2,1)S(1)} %get-tuple-element.41), channel_id=1, source_target_pairs={{0,2},{1,3},{2,0},{3,1},{4,6},{5,7},{6,4},{7,5},{8,10},{9,11},{10,... | collective-permute-start | bytes 393224 | tf_op jit(solution)/shard_map/ppermute | solution.py:26
  65.9 1.1 %shard_map.70.started = f32[128,3072]{1,0:T(8,128)S(1)} custom-call(bf16[1024,3072]{1,0:T(8,128)(2,1)S(1)} %shard_map.65.triple, bf16[128,1024]{1,0:T(8,128)(2,1)S(1)} %get-tuple-element.38.refs_0_.own_ref, f32[1,1024]{1,0:T(1,128)S(1)} %copy-done.6), custom_call_target="tpu_custom_call" | custom-call | flops 800000000 | bytes 8000000 | tf_op jit(solution)/shard_map/pallas_call | solution.py:136
  67.0 3.1 %collective-permute-done.23.refs_3_ = bf16[64,1024]{1,0:T(8,128)(2,1)S(1)} collective-permute-done((bf16[64,1024]{1,0:T(8,128)(2,1)S(1)}, bf16[64,1024]{1,0:T(8,128)(2,1)S(1)}, u32[]{:S(2)}, u32[]{:S(2)}) %collective-permute-start.23) | collective-permute-done | bytes 131104 | tf_op jit(solution)/shard_map/ppermute | solution.py:26
  70.1 3.9 %shard_map.71 = bf16[2,128,1024]{2,1,0:T(8,128)(2,1)} custom-call(bf16[1024,3072]{1,0:T(8,128)(2,1)S(1)} %shard_map.65.triple, bf16[128,1024]{1,0:T(8,128)(2,1)S(1)} %get-tuple-element.38.refs_0_.own_ref, f32[128,3072]{1,0:T(8,128)S(1)} %shard_map.70.started, bf16[64,1024]{1,0:T(8,128)(2,1)S(1)} %collective-permute-done.20.refs_0_, ...), custom_call_target="tpu_custom_call" | custom-call | flops 2400000000 | bytes 9000000 | tf_op jit(solution)/shard_map/pallas_call | solution.py:273
  (41 shorter events, 3.7 us)
Async XLA Ops:
  0.0 4.5 %copy-start = (s32[16,4]{0,1:T(4,128)S(1)}, s32[16,4]{0,1:T(4,128)}, u32[]{:S(2)}) copy-start(s32[16,4]{0,1:T(4,128)} %param.11) | copy-start | bytes 772
  0.0 13.4 %collective-permute-start.2 = (bf16[64,3072]{1,0:T(8,128)(2,1)}, bf16[64,3072]{1,0:T(8,128)(2,1)S(1)}, u32[]{:S(2)}, u32[]{:S(2)}) collective-permute-start(bf16[64,3072]{1,0:T(8,128)(2,1)} %bitcast.14), channel_id=1, source_target_pairs={{0,4},{1,5},{2,6},{3,7},{4,12},{5,13},{6,14},{7,15},{8,0},{9,1},{1... | collective-permute-start | bytes 1179656 | tf_op jit(solution)/shard_map/ppermute | solution.py:290
  3.0 12.2 %collective-permute-start.8 = (bf16[64,3072]{1,0:T(8,128)(2,1)}, bf16[64,3072]{1,0:T(8,128)(2,1)S(1)}, u32[]{:S(2)}, u32[]{:S(2)}) collective-permute-start(bf16[64,3072]{1,0:T(8,128)(2,1)} %bitcast.15), channel_id=1, source_target_pairs={{0,2},{1,3},{2,0},{3,1},{4,6},{5,7},{6,4},{7,5},{8,10},{9,11},{10,... | collective-permute-start | bytes 1179656 | tf_op jit(solution)/shard_map/ppermute | solution.py:26
  5.3 1.0 %copy-start.1 = (bf16[1,128,1024]{2,1,0:T(8,128)(2,1)S(1)}, bf16[1,128,1024]{2,1,0:T(8,128)(2,1)}, u32[]{:S(2)}) copy-start(bf16[1,128,1024]{2,1,0:T(8,128)(2,1)} %param.6) | copy-start | bytes 786436
  7.0 1.3 %collective-permute-start = (bf16[64,1024]{1,0:T(8,128)(2,1)S(1)}, bf16[64,1024]{1,0:T(8,128)(2,1)S(1)}, u32[]{:S(2)}, u32[]{:S(2)}) collective-permute-start(bf16[64,1024]{1,0:T(8,128)(2,1)S(1)} %get-tuple-element.25), channel_id=1, source_target_pairs={{0,1},{1,0},{2,3},{3,2},{4,5},{5,4},{6,7},{7,6},{8,9},{9,8},{10,11... | collective-permute-start | bytes 393224 | tf_op jit(solution)/shard_map/ppermute | solution.py:26
  7.0 9.7 %collective-permute-start.10 = (bf16[64,1024]{1,0:T(8,128)(2,1)S(1)}, bf16[64,1024]{1,0:T(8,128)(2,1)S(1)}, u32[]{:S(2)}, u32[]{:S(2)}) collective-permute-start(bf16[64,1024]{1,0:T(8,128)(2,1)S(1)} %get-tuple-element.29), channel_id=1, source_target_pairs={{0,2},{1,3},{2,0},{3,1},{4,6},{5,7},{6,4},{7,5},{8,10},{9,11},{10,... | collective-permute-start | bytes 393224 | tf_op jit(solution)/shard_map/ppermute | solution.py:26
  13.4 11.2 %collective-permute-start.6 = (bf16[64,3072]{1,0:T(8,128)(2,1)S(1)}, bf16[64,3072]{1,0:T(8,128)(2,1)S(1)}, u32[]{:S(2)}, u32[]{:S(2)}) collective-permute-start(bf16[64,3072]{1,0:T(8,128)(2,1)S(1)} %collective-permute-done.2.refs_2_), channel_id=1, source_target_pairs={{0,4},{1,5},{2,6},{3,7},{4,12},{5,13},{6,14},{7,15},{8,0},{9,1},{1... | collective-permute-start | bytes 1179656 | tf_op jit(solution)/shard_map/ppermute | solution.py:290
  14.3 10.3 %collective-permute-start.3 = (bf16[64,3072]{1,0:T(8,128)(2,1)S(1)}, bf16[64,3072]{1,0:T(8,128)(2,1)S(1)}, u32[]{:S(2)}, u32[]{:S(2)}) collective-permute-start(bf16[64,3072]{1,0:T(8,128)(2,1)S(1)} %collective-permute-done.2.refs_2_), channel_id=1, source_target_pairs={{0,1},{1,0},{2,3},{3,2},{4,5},{5,4},{6,7},{7,6},{8,9},{9,8},{10,11... | collective-permute-start | bytes 1179656 | tf_op jit(solution)/shard_map/ppermute | solution.py:26
  15.2 9.4 %collective-permute-start.9 = (bf16[64,3072]{1,0:T(8,128)(2,1)S(1)}, bf16[64,3072]{1,0:T(8,128)(2,1)S(1)}, u32[]{:S(2)}, u32[]{:S(2)}) collective-permute-start(bf16[64,3072]{1,0:T(8,128)(2,1)S(1)} %collective-permute-done.8.refs_8_), channel_id=1, source_target_pairs={{0,1},{1,0},{2,3},{3,2},{4,5},{5,4},{6,7},{7,6},{8,9},{9,8},{10,11... | collective-permute-start | bytes 1179656 | tf_op jit(solution)/shard_map/ppermute | solution.py:26
  16.6 11.3 %collective-permute-start.11 = (bf16[64,3072]{1,0:T(8,128)(2,1)S(1)}, bf16[64,3072]{1,0:T(8,128)(2,1)S(1)}, u32[]{:S(2)}, u32[]{:S(2)}) collective-permute-start(bf16[64,3072]{1,0:T(8,128)(2,1)S(1)} %collective-permute-done.2.refs_2_), channel_id=1, source_target_pairs={{0,2},{1,3},{2,0},{3,1},{4,6},{5,7},{6,4},{7,5},{8,10},{9,11},{10,... | collective-permute-start | bytes 1179656 | tf_op jit(solution)/shard_map/ppermute | solution.py:26
  24.6 10.6 %collective-permute-start.13 = (bf16[64,3072]{1,0:T(8,128)(2,1)S(1)}, bf16[64,3072]{1,0:T(8,128)(2,1)S(1)}, u32[]{:S(2)}, u32[]{:S(2)}) collective-permute-start(bf16[64,3072]{1,0:T(8,128)(2,1)S(1)} %collective-permute-done.6.refs_6_), channel_id=1, source_target_pairs={{0,2},{1,3},{2,0},{3,1},{4,6},{5,7},{6,4},{7,5},{8,10},{9,11},{10,... | collective-permute-start | bytes 1179656 | tf_op jit(solution)/shard_map/ppermute | solution.py:26
  25.8 9.4 %collective-permute-start.4 = (bf16[64,3072]{1,0:T(8,128)(2,1)}, bf16[64,3072]{1,0:T(8,128)(2,1)S(1)}, u32[]{:S(2)}, u32[]{:S(2)}) collective-permute-start(bf16[64,3072]{1,0:T(8,128)(2,1)} %bitcast.16), channel_id=1, source_target_pairs={{4,0},{5,1},{6,2},{7,3},{12,4},{13,5},{14,6},{15,7},{0,8},{1,9},{2... | collective-permute-start | bytes 1179656 | tf_op jit(solution)/shard_map/ppermute | solution.py:293
  27.3 8.4 %collective-permute-start.7 = (bf16[64,3072]{1,0:T(8,128)(2,1)S(1)}, bf16[64,3072]{1,0:T(8,128)(2,1)S(1)}, u32[]{:S(2)}, u32[]{:S(2)}) collective-permute-start(bf16[64,3072]{1,0:T(8,128)(2,1)S(1)} %collective-permute-done.6.refs_6_), channel_id=1, source_target_pairs={{0,1},{1,0},{2,3},{3,2},{4,5},{5,4},{6,7},{7,6},{8,9},{9,8},{10,11... | collective-permute-start | bytes 1179656 | tf_op jit(solution)/shard_map/ppermute | solution.py:26
  27.9 7.8 %collective-permute-start.12 = (bf16[64,3072]{1,0:T(8,128)(2,1)S(1)}, bf16[64,3072]{1,0:T(8,128)(2,1)S(1)}, u32[]{:S(2)}, u32[]{:S(2)}) collective-permute-start(bf16[64,3072]{1,0:T(8,128)(2,1)S(1)} %collective-permute-done.11.refs_10_), channel_id=1, source_target_pairs={{0,1},{1,0},{2,3},{3,2},{4,5},{5,4},{6,7},{7,6},{8,9},{9,8},{10,11... | collective-permute-start | bytes 1179656 | tf_op jit(solution)/shard_map/ppermute | solution.py:26
  27.9 10.6 %collective-permute-start.1 = (bf16[64,3072]{1,0:T(8,128)(2,1)}, bf16[64,3072]{1,0:T(8,128)(2,1)S(1)}, u32[]{:S(2)}, u32[]{:S(2)}) collective-permute-start(bf16[64,3072]{1,0:T(8,128)(2,1)} %bitcast.17), channel_id=1, source_target_pairs={{0,1},{1,0},{2,3},{3,2},{4,5},{5,4},{6,7},{7,6},{8,9},{9,8},{10,11... | collective-permute-start | bytes 1179656 | tf_op jit(solution)/shard_map/ppermute | solution.py:26
  35.2 5.1 %collective-permute-start.14 = (bf16[64,3072]{1,0:T(8,128)(2,1)S(1)}, bf16[64,3072]{1,0:T(8,128)(2,1)S(1)}, u32[]{:S(2)}, u32[]{:S(2)}) collective-permute-start(bf16[64,3072]{1,0:T(8,128)(2,1)S(1)} %collective-permute-done.13.refs_12_), channel_id=1, source_target_pairs={{0,1},{1,0},{2,3},{3,2},{4,5},{5,4},{6,7},{7,6},{8,9},{9,8},{10,11... | collective-permute-start | bytes 1179656 | tf_op jit(solution)/shard_map/ppermute | solution.py:26
  35.2 5.1 %collective-permute-start.5 = (bf16[64,3072]{1,0:T(8,128)(2,1)S(1)}, bf16[64,3072]{1,0:T(8,128)(2,1)S(1)}, u32[]{:S(2)}, u32[]{:S(2)}) collective-permute-start(bf16[64,3072]{1,0:T(8,128)(2,1)S(1)} %collective-permute-done.4.refs_4_), channel_id=1, source_target_pairs={{0,1},{1,0},{2,3},{3,2},{4,5},{5,4},{6,7},{7,6},{8,9},{9,8},{10,11... | collective-permute-start | bytes 1179656 | tf_op jit(solution)/shard_map/ppermute | solution.py:26
  35.7 11.1 %collective-permute-start.17 = (bf16[64,3072]{1,0:T(8,128)(2,1)S(1)}, bf16[64,3072]{1,0:T(8,128)(2,1)S(1)}, u32[]{:S(2)}, u32[]{:S(2)}) collective-permute-start(bf16[64,3072]{1,0:T(8,128)(2,1)S(1)} %collective-permute-done.4.refs_4_), channel_id=1, source_target_pairs={{0,2},{1,3},{2,0},{3,1},{4,6},{5,7},{6,4},{7,5},{8,10},{9,11},{10,... | collective-permute-start | bytes 1179656 | tf_op jit(solution)/shard_map/ppermute | solution.py:26
  37.2 8.6 %collective-permute-start.16 = (bf16[64,1024]{1,0:T(8,128)(2,1)S(1)}, bf16[64,1024]{1,0:T(8,128)(2,1)S(1)}, u32[]{:S(2)}, u32[]{:S(2)}) collective-permute-start(bf16[64,1024]{1,0:T(8,128)(2,1)S(1)} %get-tuple-element.35), channel_id=1, source_target_pairs={{0,8},{1,9},{2,10},{3,11},{4,12},{5,13},{6,14},{7,15},{8,0},{9,1},... | collective-permute-start | bytes 393224 | tf_op jit(solution)/shard_map/ppermute | solution.py:26
  38.6 5.7 %copy-start.2 = (bf16[1,128,1024]{2,1,0:T(8,128)(2,1)S(1)}, bf16[1,128,1024]{2,1,0:T(8,128)(2,1)}, u32[]{:S(2)}) copy-start(bf16[1,128,1024]{2,1,0:T(8,128)(2,1)} %param.6) | copy-start | bytes 786436
  38.6 7.5 %collective-permute-start.15 = (bf16[64,1024]{1,0:T(8,128)(2,1)S(1)}, bf16[64,1024]{1,0:T(8,128)(2,1)S(1)}, u32[]{:S(2)}, u32[]{:S(2)}) collective-permute-start(bf16[64,1024]{1,0:T(8,128)(2,1)S(1)} %get-tuple-element.33), channel_id=1, source_target_pairs={{0,4},{1,5},{2,6},{3,7},{4,0},{5,1},{6,2},{7,3},{8,12},{9,13},{10,... | collective-permute-start | bytes 393224 | tf_op jit(solution)/shard_map/ppermute | solution.py:26
  40.2 1.0 %copy-start.4 = (bf16[1,64,3072]{2,1,0:T(8,128)(2,1)S(1)}, bf16[1,64,3072]{2,1,0:T(8,128)(2,1)}, u32[]{:S(2)}) copy-start(bf16[1,64,3072]{2,1,0:T(8,128)(2,1)} %param.9) | copy-start | bytes 1179652
  41.2 3.0 %copy-start.6 = (f32[1,1024]{1,0:T(1,128)S(1)}, f32[1,1024]{1,0:T(1,128)}, u32[]{:S(2)}) copy-start(f32[1,1024]{1,0:T(1,128)} %refs_4_.5) | copy-start | bytes 12292
  45.3 3.2 %copy-start.3 = (bf16[1,1024,1024]{2,1,0:T(8,128)(2,1)S(1)}, bf16[1,1024,1024]{2,1,0:T(8,128)(2,1)}, u32[]{:S(2)}) copy-start(bf16[1,1024,1024]{2,1,0:T(8,128)(2,1)} %param.10) | copy-start | bytes 6291460
  46.8 1.7 %collective-permute-start.18 = (bf16[64,3072]{1,0:T(8,128)(2,1)S(1)}, bf16[64,3072]{1,0:T(8,128)(2,1)S(1)}, u32[]{:S(2)}, u32[]{:S(2)}) collective-permute-start(bf16[64,3072]{1,0:T(8,128)(2,1)S(1)} %collective-permute-done.17.refs_6_), channel_id=1, source_target_pairs={{0,1},{1,0},{2,3},{3,2},{4,5},{5,4},{6,7},{7,6},{8,9},{9,8},{10,11... | collective-permute-start | bytes 1179656 | tf_op jit(solution)/shard_map/ppermute | solution.py:26
  48.5 11.7 %copy-start.5 = (bf16[128,1024]{1,0:T(8,128)(2,1)S(1)}, bf16[128,1024]{1,0:T(8,128)(2,1)}, u32[]{:S(2)}) copy-start(bf16[128,1024]{1,0:T(8,128)(2,1)} %arriving_ref.1) | copy-start | bytes 786436
  50.8 9.3 %collective-permute-start.19 = (bf16[128,1024]{1,0:T(8,128)(2,1)S(1)}, bf16[128,1024]{1,0:T(8,128)(2,1)S(1)}, u32[]{:S(2)}, u32[]{:S(2)}) collective-permute-start(bf16[128,1024]{1,0:T(8,128)(2,1)S(1)} %shard_map.68.refs_8_), channel_id=1, source_target_pairs={{0,16},{1,17},{2,18},{3,19},{4,20},{5,21},{6,22},{7,23},{8,24},{9,... | collective-permute-start | bytes 786440 | tf_op jit(solution)/shard_map/ppermute | solution.py:32
  60.4 2.4 %collective-permute-start.20 = (bf16[64,1024]{1,0:T(8,128)(2,1)S(1)}, bf16[64,1024]{1,0:T(8,128)(2,1)S(1)}, u32[]{:S(2)}, u32[]{:S(2)}) collective-permute-start(bf16[64,1024]{1,0:T(8,128)(2,1)S(1)} %get-tuple-element.39), channel_id=1, source_target_pairs={{0,1},{1,0},{2,3},{3,2},{4,5},{5,4},{6,7},{7,6},{8,9},{9,8},{10,11... | collective-permute-start | bytes 393224 | tf_op jit(solution)/shard_map/ppermute | solution.py:26
  60.5 9.6 %collective-permute-start.23 = (bf16[64,1024]{1,0:T(8,128)(2,1)S(1)}, bf16[64,1024]{1,0:T(8,128)(2,1)S(1)}, u32[]{:S(2)}, u32[]{:S(2)}) collective-permute-start(bf16[64,1024]{1,0:T(8,128)(2,1)S(1)} %get-tuple-element.44), channel_id=1, source_target_pairs={{0,8},{1,9},{2,10},{3,11},{4,12},{5,13},{6,14},{7,15},{8,0},{9,1},... | collective-permute-start | bytes 393224 | tf_op jit(solution)/shard_map/ppermute | solution.py:26
  62.8 7.3 %collective-permute-start.22 = (bf16[64,1024]{1,0:T(8,128)(2,1)S(1)}, bf16[64,1024]{1,0:T(8,128)(2,1)S(1)}, u32[]{:S(2)}, u32[]{:S(2)}) collective-permute-start(bf16[64,1024]{1,0:T(8,128)(2,1)S(1)} %get-tuple-element.43), channel_id=1, source_target_pairs={{0,4},{1,5},{2,6},{3,7},{4,0},{5,1},{6,2},{7,3},{8,12},{9,13},{10,... | collective-permute-start | bytes 393224 | tf_op jit(solution)/shard_map/ppermute | solution.py:26
  64.4 5.7 %collective-permute-start.21 = (bf16[64,1024]{1,0:T(8,128)(2,1)S(1)}, bf16[64,1024]{1,0:T(8,128)(2,1)S(1)}, u32[]{:S(2)}, u32[]{:S(2)}) collective-permute-start(bf16[64,1024]{1,0:T(8,128)(2,1)S(1)} %get-tuple-element.41), channel_id=1, source_target_pairs={{0,2},{1,3},{2,0},{3,1},{4,6},{5,7},{6,4},{7,5},{8,10},{9,11},{10,... | collective-permute-start | bytes 393224 | tf_op jit(solution)/shard_map/ppermute | solution.py:26

commit v6 on v5

--- a/solution.py
+++ b/solution.py
@@ -162,7 +162,7 @@
 
     def own_part(start):
         span = slice(start, start + WIDE)
-        result = started[:, span]
+        result = started[:rows, span]
         if latest:
             result += jnp.dot(late_columns[:rows], last[:, span], preferred_element_type=jnp.float32)
         return result
@@ -170,7 +170,10 @@
     def far_part(start):
         span = slice(start, start + WIDE)
         if far_started is None:
-            result = jnp.dot(normed[rows:], triple[:, span], preferred_element_type=jnp.float32)
+            ready = started.shape[0]
+            result = jnp.dot(normed[ready:], triple[:, span], preferred_element_type=jnp.float32)
+            if ready > rows:
+                result = jnp.concatenate([started[rows:, span], result], axis=0)
         else:
             result = far_started[:, start - inner : start - inner + WIDE]
         if latest:
@@ -301,12 +304,12 @@
     r1 = around(shard)
     x0 = beside(shard)
     near = [twin(chosen[0]), beside(chosen[1])]
-    c0 = twin(after(shard, near[0]))
     r2 = around(after(r1, near[0]))
     cr1 = twin(r1)
     x1 = beside(after(r1, near[1]))
     l1 = back(after(shard, cr1))
     cx0 = twin(x0)
+    c0 = twin(after(shard, r2))
     x2 = beside(after(r2, cx0, cr1))
     cr2 = twin(r2)
     cx1 = twin(x1)
@@ -362,7 +365,7 @@
     moved = from_behind(first_out, "section", 1)
     second_in, chosen = choose(wanted, moved, arriving)
     fars = partner_rows(chosen)
-    return second_layer(triple, second_in, ahead(triple, [second_in], gain, 0), fars, gain, exit_matrix[0], latest, first_out)[:, None]
+    return second_layer(triple, second_in, ahead(triple, [second_in, fars[0]], gain, 0), fars, gain, exit_matrix[0], latest, first_out)[:, None]
 
 
 def solution(mesh):

time: 74.2 us -> 74 us (level)
  no operation moved by 1% of the time
where the time goes in v6:
time: 74 us; the launch traced here: 73.8 us
  waiting for transfers between devices  32.4 us (44%)
  starting transfers between devices  24.7 us (33%)
  Pallas kernels  13.9 us (19%)
  local copies, waits for them, and re-layouts  2.7 us (4%)
    ppermute x20, starting transfers between devices, swapped(): lax.ppermute(x, axis, [(i, i ^ mask) for i in range(lax.axis_size(axis))])  15.8 us
    ppermute x20, waiting for transfers between devices, swapped(): lax.ppermute(x, axis, [(i, i ^ mask) for i in range(lax.axis_size(axis))])  15 us
    ppermute x2, waiting for transfers between devices, around(): lax.ppermute(x, 'seq', [(i, onward[i // 4] * 4 + i % 4) for i in range(16)])  11.5 us
    ppermute x1, waiting for transfers between devices, from_behind(): return lax.ppermute(block, axis, route)  5.9 us
    ppermute x2, starting transfers between devices, around(): lax.ppermute(x, 'seq', [(i, onward[i // 4] * 4 + i % 4) for i in range(16)])  3.97 us
    pallas_call x3, Pallas kernels, ahead(): pl.pallas_call(functools.partial(ahead_kernel, first_column), out_shape=p...  3.95 us
    pallas_call x1, Pallas kernels, second_layer(): pl.pallas_call(functools.partial(second_kernel, len(latest)), out_shape=j...  3.72 us
    ppermute x1, starting transfers between devices, from_behind(): return lax.ppermute(block, axis, route)  3.44 us
  transfers between devices with their start and end apart: 24, of which 13 were waited for; matrix products, arithmetic and copies ran while one was open for 1% of the time, Pallas kernels for 10%

profile of v6, /device:TPU:0, one launch (start us, length us, event | category | flops | bytes accessed | tf_op | source)
XLA Modules:
  0.0 73.8 jit_solution(31121283696881917)
XLA Ops:
  0.0 3.0 %collective-permute-start = (bf16[64,3072]{1,0:T(8,128)(2,1)}, bf16[64,3072]{1,0:T(8,128)(2,1)S(1)}, u32[]{:S(2)}, u32[]{:S(2)}) collective-permute-start(bf16[64,3072]{1,0:T(8,128)(2,1)} %bitcast.14), channel_id=1, source_target_pairs={{0,4},{1,5},{2,6},{3,7},{4,12},{5,13},{6,14},{7,15},{8,0},{9,1},{1... | collective-permute-start | bytes 1179656 | tf_op jit(solution)/shard_map/ppermute | solution.py:293
  3.0 1.5 %collective-permute-start.8 = (bf16[64,3072]{1,0:T(8,128)(2,1)}, bf16[64,3072]{1,0:T(8,128)(2,1)S(1)}, u32[]{:S(2)}, u32[]{:S(2)}) collective-permute-start(bf16[64,3072]{1,0:T(8,128)(2,1)} %bitcast.15), channel_id=1, source_target_pairs={{0,2},{1,3},{2,0},{3,1},{4,6},{5,7},{6,4},{7,5},{8,10},{9,11},{10,... | collective-permute-start | bytes 1179656 | tf_op jit(solution)/shard_map/ppermute | solution.py:26
  4.5 0.7 gather_fusion
  5.3 1.0 %copy-done.1 = bf16[1,128,1024]{2,1,0:T(8,128)(2,1)S(1)} copy-done((bf16[1,128,1024]{2,1,0:T(8,128)(2,1)S(1)}, bf16[1,128,1024]{2,1,0:T(8,128)(2,1)}, u32[]{:S(2)}) %copy-start.1) | copy-done | bytes 262168
  6.2 0.7 %shard_map.64 = (bf16[128,1024]{1,0:T(8,128)(2,1)}, bf16[64,1024]{1,0:T(8,128)(2,1)S(1)}, bf16[64,1024]{1,0:T(8,128)(2,1)S(1)}, bf16[64,1024]{1,0:T(8,128)(2,1)S(1)}, bf16[64,1024]{1,0:T(8,128)(2,1)S(1)}) custom-call(s32[8,128]{1,0:T(8,128)S(1)} %broadcast_in_dim.4.wanted, bf16[128,1024]{1,0:T(8,128)(2,1)S(1)} %bitcast.8, bf16[128,1024]{1,0:T(8,128)(2,1)S(1)} %bitcast.9), custom_call_target="tpu_custom_call" | custom-call | tf_op jit(solution)/shard_map/pallas_call | solution.py:73
  7.5 0.8 %collective-permute-done.1.refs_0_ = bf16[64,1024]{1,0:T(8,128)(2,1)S(1)} collective-permute-done((bf16[64,1024]{1,0:T(8,128)(2,1)S(1)}, bf16[64,1024]{1,0:T(8,128)(2,1)S(1)}, u32[]{:S(2)}, u32[]{:S(2)}) %collective-permute-start.1) | collective-permute-done | bytes 131104 | tf_op jit(solution)/shard_map/ppermute | solution.py:26
  8.3 5.0 %collective-permute-done.refs_2_ = bf16[64,3072]{1,0:T(8,128)(2,1)S(1)} collective-permute-done((bf16[64,3072]{1,0:T(8,128)(2,1)}, bf16[64,3072]{1,0:T(8,128)(2,1)S(1)}, u32[]{:S(2)}, u32[]{:S(2)}) %collective-permute-start) | collective-permute-done | bytes 393248 | tf_op jit(solution)/shard_map/ppermute | solution.py:293
  13.4 0.9 %collective-permute-start.2 = (bf16[64,3072]{1,0:T(8,128)(2,1)S(1)}, bf16[64,3072]{1,0:T(8,128)(2,1)S(1)}, u32[]{:S(2)}, u32[]{:S(2)}) collective-permute-start(bf16[64,3072]{1,0:T(8,128)(2,1)S(1)} %collective-permute-done.refs_2_), channel_id=1, source_target_pairs={{0,4},{1,5},{2,6},{3,7},{4,12},{5,13},{6,14},{7,15},{8,0},{9,1},{1... | collective-permute-start | bytes 1179656 | tf_op jit(solution)/shard_map/ppermute | solution.py:293
  14.3 0.9 %collective-permute-done.8.refs_8_ = bf16[64,3072]{1,0:T(8,128)(2,1)S(1)} collective-permute-done((bf16[64,3072]{1,0:T(8,128)(2,1)}, bf16[64,3072]{1,0:T(8,128)(2,1)S(1)}, u32[]{:S(2)}, u32[]{:S(2)}) %collective-permute-start.8) | collective-permute-done | bytes 393248 | tf_op jit(solution)/shard_map/ppermute | solution.py:26
  15.2 1.4 %collective-permute-done.10.refs_1_ = bf16[64,1024]{1,0:T(8,128)(2,1)S(1)} collective-permute-done((bf16[64,1024]{1,0:T(8,128)(2,1)S(1)}, bf16[64,1024]{1,0:T(8,128)(2,1)S(1)}, u32[]{:S(2)}, u32[]{:S(2)}) %collective-permute-start.10) | collective-permute-done | bytes 131104 | tf_op jit(solution)/shard_map/ppermute | solution.py:26
  16.6 1.5 %collective-permute-start.11 = (bf16[64,3072]{1,0:T(8,128)(2,1)S(1)}, bf16[64,3072]{1,0:T(8,128)(2,1)S(1)}, u32[]{:S(2)}, u32[]{:S(2)}) collective-permute-start(bf16[64,3072]{1,0:T(8,128)(2,1)S(1)} %collective-permute-done.refs_2_), channel_id=1, source_target_pairs={{0,2},{1,3},{2,0},{3,1},{4,6},{5,7},{6,4},{7,5},{8,10},{9,11},{10,... | collective-permute-start | bytes 1179656 | tf_op jit(solution)/shard_map/ppermute | solution.py:26
  18.1 6.4 %collective-permute-done.2.refs_6_ = bf16[64,3072]{1,0:T(8,128)(2,1)S(1)} collective-permute-done((bf16[64,3072]{1,0:T(8,128)(2,1)S(1)}, bf16[64,3072]{1,0:T(8,128)(2,1)S(1)}, u32[]{:S(2)}, u32[]{:S(2)}) %collective-permute-start.2) | collective-permute-done | bytes 393248 | tf_op jit(solution)/shard_map/ppermute | solution.py:293
  24.6 1.2 %collective-permute-start.13 = (bf16[64,3072]{1,0:T(8,128)(2,1)S(1)}, bf16[64,3072]{1,0:T(8,128)(2,1)S(1)}, u32[]{:S(2)}, u32[]{:S(2)}) collective-permute-start(bf16[64,3072]{1,0:T(8,128)(2,1)S(1)} %collective-permute-done.2.refs_6_), channel_id=1, source_target_pairs={{0,2},{1,3},{2,0},{3,1},{4,6},{5,7},{6,4},{7,5},{8,10},{9,11},{10,... | collective-permute-start | bytes 1179656 | tf_op jit(solution)/shard_map/ppermute | solution.py:26
  25.8 1.5 %collective-permute-start.5 = (bf16[64,3072]{1,0:T(8,128)(2,1)}, bf16[64,3072]{1,0:T(8,128)(2,1)S(1)}, u32[]{:S(2)}, u32[]{:S(2)}) collective-permute-start(bf16[64,3072]{1,0:T(8,128)(2,1)} %bitcast.16), channel_id=1, source_target_pairs={{4,0},{5,1},{6,2},{7,3},{12,4},{13,5},{14,6},{15,7},{0,8},{1,9},{2... | collective-permute-start | bytes 1179656 | tf_op jit(solution)/shard_map/ppermute | solution.py:296
  28.4 6.8 %collective-permute-done.13.refs_12_ = bf16[64,3072]{1,0:T(8,128)(2,1)S(1)} collective-permute-done((bf16[64,3072]{1,0:T(8,128)(2,1)S(1)}, bf16[64,3072]{1,0:T(8,128)(2,1)S(1)}, u32[]{:S(2)}, u32[]{:S(2)}) %collective-permute-start.13) | collective-permute-done | bytes 393248 | tf_op jit(solution)/shard_map/ppermute | solution.py:26
  35.7 1.5 %collective-permute-start.17 = (bf16[64,3072]{1,0:T(8,128)(2,1)S(1)}, bf16[64,3072]{1,0:T(8,128)(2,1)S(1)}, u32[]{:S(2)}, u32[]{:S(2)}) collective-permute-start(bf16[64,3072]{1,0:T(8,128)(2,1)S(1)} %collective-permute-done.5.refs_4_), channel_id=1, source_target_pairs={{0,2},{1,3},{2,0},{3,1},{4,6},{5,7},{6,4},{7,5},{8,10},{9,11},{10,... | collective-permute-start | bytes 1179656 | tf_op jit(solution)/shard_map/ppermute | solution.py:26
  37.2 1.4 %collective-permute-start.16 = (bf16[64,1024]{1,0:T(8,128)(2,1)S(1)}, bf16[64,1024]{1,0:T(8,128)(2,1)S(1)}, u32[]{:S(2)}, u32[]{:S(2)}) collective-permute-start(bf16[64,1024]{1,0:T(8,128)(2,1)S(1)} %get-tuple-element.35), channel_id=1, source_target_pairs={{0,8},{1,9},{2,10},{3,11},{4,12},{5,13},{6,14},{7,15},{8,0},{9,1},... | collective-permute-start | bytes 393224 | tf_op jit(solution)/shard_map/ppermute | solution.py:26
  38.6 1.7 %collective-permute-start.15 = (bf16[64,1024]{1,0:T(8,128)(2,1)S(1)}, bf16[64,1024]{1,0:T(8,128)(2,1)S(1)}, u32[]{:S(2)}, u32[]{:S(2)}) collective-permute-start(bf16[64,1024]{1,0:T(8,128)(2,1)S(1)} %get-tuple-element.33), channel_id=1, source_target_pairs={{0,4},{1,5},{2,6},{3,7},{4,0},{5,1},{6,2},{7,3},{8,12},{9,13},{10,... | collective-permute-start | bytes 393224 | tf_op jit(solution)/shard_map/ppermute | solution.py:26
  40.2 1.0 %copy-done.4 = bf16[1,64,3072]{2,1,0:T(8,128)(2,1)S(1)} copy-done((bf16[1,64,3072]{2,1,0:T(8,128)(2,1)S(1)}, bf16[1,64,3072]{2,1,0:T(8,128)(2,1)}, u32[]{:S(2)}) %copy-start.4) | copy-done | bytes 393240
  41.2 3.0 %shard_map.65.triple = bf16[1024,3072]{1,0:T(8,128)(2,1)S(1)} custom-call(bf16[64,3072]{1,0:T(8,128)(2,1)S(1)} %bitcast.18, bf16[64,3072]{1,0:T(8,128)(2,1)S(1)} %collective-permute-done.3.refs_1_, bf16[64,3072]{1,0:T(8,128)(2,1)S(1)} %collective-permute-done.refs_2_, bf16[64,3072]{1,0:T(8,128)(2,1)S(1)} %collective-permute-done.4.refs_3_, ...), custom_call_target="tpu_custom_call" | custom-call | bytes 12000000 | tf_op jit(solution)/shard_map/pallas_call | solution.py:107
  44.2 1.1 %shard_map.67.started = f32[128,3072]{1,0:T(8,128)S(1)} custom-call(bf16[1024,3072]{1,0:T(8,128)(2,1)S(1)} %shard_map.65.triple, bf16[128,1024]{1,0:T(8,128)(2,1)S(1)} %bitcast.10, f32[1,1024]{1,0:T(1,128)S(1)} %copy-done.6), custom_call_target="tpu_custom_call" | custom-call | flops 800000000 | bytes 8000000 | tf_op jit(solution)/shard_map/pallas_call | solution.py:136
  46.1 0.7 collective-permute-done.17.refs_6_
  46.8 1.4 %shard_map.66.far_started = f32[256,2048]{1,0:T(8,128)S(1)} custom-call(bf16[1024,3072]{1,0:T(8,128)(2,1)S(1)} %shard_map.65.triple, bf16[64,1024]{1,0:T(8,128)(2,1)S(1)} %collective-permute-done.1.refs_0_, bf16[64,1024]{1,0:T(8,128)(2,1)S(1)} %collective-permute-done.10.refs_1_, bf16[64,1024]{1,0:T(8,128)(2,1)S(1)} %collective-permute-done.15.refs_2_, ...), custom_call_target="tpu_custom_call" | custom-call | flops 800000000 | bytes 8000000 | tf_op jit(solution)/shard_map/pallas_call | solution.py:136
  48.5 2.3 %shard_map.68.refs_8_ = bf16[128,1024]{1,0:T(8,128)(2,1)S(1)} custom-call(f32[256,2048]{1,0:T(8,128)S(1)} %shard_map.66.far_started, bf16[128,1024]{1,0:T(8,128)(2,1)S(1)} %bitcast.11, f32[128,3072]{1,0:T(8,128)S(1)} %shard_map.67.started, bf16[64,1024]{1,0:T(8,128)(2,1)S(1)} %collective-permute-done.1.refs_0_, ...), custom_call_target="tpu_custom_call" | custom-call | flops 2400000000 | bytes 9000000 | tf_op jit(solution)/shard_map/pallas_call | solution.py:264
  50.8 3.4 %collective-permute-start.19 = (bf16[128,1024]{1,0:T(8,128)(2,1)S(1)}, bf16[128,1024]{1,0:T(8,128)(2,1)S(1)}, u32[]{:S(2)}, u32[]{:S(2)}) collective-permute-start(bf16[128,1024]{1,0:T(8,128)(2,1)S(1)} %shard_map.68.refs_8_), channel_id=1, source_target_pairs={{0,16},{1,17},{2,18},{3,19},{4,20},{5,21},{6,22},{7,23},{8,24},{9,... | collective-permute-start | bytes 786440 | tf_op jit(solution)/shard_map/ppermute | solution.py:32
  54.3 5.9 %collective-permute-done.19.moved_ref = bf16[128,1024]{1,0:T(8,128)(2,1)S(1)} collective-permute-done((bf16[128,1024]{1,0:T(8,128)(2,1)S(1)}, bf16[128,1024]{1,0:T(8,128)(2,1)S(1)}, u32[]{:S(2)}, u32[]{:S(2)}) %collective-permute-start.19) | collective-permute-done | bytes 262176 | tf_op jit(solution)/shard_map/ppermute | solution.py:32
  60.5 2.3 %collective-permute-start.23 = (bf16[64,1024]{1,0:T(8,128)(2,1)S(1)}, bf16[64,1024]{1,0:T(8,128)(2,1)S(1)}, u32[]{:S(2)}, u32[]{:S(2)}) collective-permute-start(bf16[64,1024]{1,0:T(8,128)(2,1)S(1)} %get-tuple-element.44), channel_id=1, source_target_pairs={{0,8},{1,9},{2,10},{3,11},{4,12},{5,13},{6,14},{7,15},{8,0},{9,1},... | collective-permute-start | bytes 393224 | tf_op jit(solution)/shard_map/ppermute | solution.py:26
  62.8 1.6 %collective-permute-start.22 = (bf16[64,1024]{1,0:T(8,128)(2,1)S(1)}, bf16[64,1024]{1,0:T(8,128)(2,1)S(1)}, u32[]{:S(2)}, u32[]{:S(2)}) collective-permute-start(bf16[64,1024]{1,0:T(8,128)(2,1)S(1)} %get-tuple-element.43), channel_id=1, source_target_pairs={{0,4},{1,5},{2,6},{3,7},{4,0},{5,1},{6,2},{7,3},{8,12},{9,13},{10,... | collective-permute-start | bytes 393224 | tf_op jit(solution)/shard_map/ppermute | solution.py:26
  64.4 1.5 %collective-permute-start.21 = (bf16[64,1024]{1,0:T(8,128)(2,1)S(1)}, bf16[64,1024]{1,0:T(8,128)(2,1)S(1)}, u32[]{:S(2)}, u32[]{:S(2)}) collective-permute-start(bf16[64,1024]{1,0:T(8,128)(2,1)S(1)} %get-tuple-element.41), channel_id=1, source_target_pairs={{0,2},{1,3},{2,0},{3,1},{4,6},{5,7},{6,4},{7,5},{8,10},{9,11},{10,... | collective-permute-start | bytes 393224 | tf_op jit(solution)/shard_map/ppermute | solution.py:26
  65.9 1.5 %shard_map.70.started = f32[192,3072]{1,0:T(8,128)S(1)} custom-call(bf16[1024,3072]{1,0:T(8,128)(2,1)S(1)} %shard_map.65.triple, bf16[128,1024]{1,0:T(8,128)(2,1)S(1)} %get-tuple-element.38.refs_0_.own_ref, bf16[64,1024]{1,0:T(8,128)(2,1)S(1)} %collective-permute-done.20.refs_1_.refs_0_, f32[1,1024]{1,0:T(1,128)S(1)} %copy-done.6), custom_call_target="tpu_custom_call" | custom-call | flops 800000000 | bytes 8000000 | tf_op jit(solution)/shard_map/pallas_call | solution.py:136
  67.4 2.7 %collective-permute-done.23.refs_3_ = bf16[64,1024]{1,0:T(8,128)(2,1)S(1)} collective-permute-done((bf16[64,1024]{1,0:T(8,128)(2,1)S(1)}, bf16[64,1024]{1,0:T(8,128)(2,1)S(1)}, u32[]{:S(2)}, u32[]{:S(2)}) %collective-permute-start.23) | collective-permute-done | bytes 131104 | tf_op jit(solution)/shard_map/ppermute | solution.py:26
  70.1 3.7 %shard_map.71 = bf16[2,128,1024]{2,1,0:T(8,128)(2,1)} custom-call(bf16[1024,3072]{1,0:T(8,128)(2,1)S(1)} %shard_map.65.triple, bf16[128,1024]{1,0:T(8,128)(2,1)S(1)} %get-tuple-element.38.refs_0_.own_ref, f32[192,3072]{1,0:T(8,128)S(1)} %shard_map.70.started, bf16[64,1024]{1,0:T(8,128)(2,1)S(1)} %collective-permute-done.20.refs_1_.refs_0_, ...), custom_call_target="tpu_custom_call" | custom-call | flops 2400000000 | bytes 9000000 | tf_op jit(solution)/shard_map/pallas_call | solution.py:276
  (41 shorter events, 3.7 us)
Async XLA Ops:
  0.0 4.5 %copy-start = (s32[16,4]{0,1:T(4,128)S(1)}, s32[16,4]{0,1:T(4,128)}, u32[]{:S(2)}) copy-start(s32[16,4]{0,1:T(4,128)} %param.11) | copy-start | bytes 772
  0.0 13.4 %collective-permute-start = (bf16[64,3072]{1,0:T(8,128)(2,1)}, bf16[64,3072]{1,0:T(8,128)(2,1)S(1)}, u32[]{:S(2)}, u32[]{:S(2)}) collective-permute-start(bf16[64,3072]{1,0:T(8,128)(2,1)} %bitcast.14), channel_id=1, source_target_pairs={{0,4},{1,5},{2,6},{3,7},{4,12},{5,13},{6,14},{7,15},{8,0},{9,1},{1... | collective-permute-start | bytes 1179656 | tf_op jit(solution)/shard_map/ppermute | solution.py:293
  3.0 12.2 %collective-permute-start.8 = (bf16[64,3072]{1,0:T(8,128)(2,1)}, bf16[64,3072]{1,0:T(8,128)(2,1)S(1)}, u32[]{:S(2)}, u32[]{:S(2)}) collective-permute-start(bf16[64,3072]{1,0:T(8,128)(2,1)} %bitcast.15), channel_id=1, source_target_pairs={{0,2},{1,3},{2,0},{3,1},{4,6},{5,7},{6,4},{7,5},{8,10},{9,11},{10,... | collective-permute-start | bytes 1179656 | tf_op jit(solution)/shard_map/ppermute | solution.py:26
  5.3 1.0 %copy-start.1 = (bf16[1,128,1024]{2,1,0:T(8,128)(2,1)S(1)}, bf16[1,128,1024]{2,1,0:T(8,128)(2,1)}, u32[]{:S(2)}) copy-start(bf16[1,128,1024]{2,1,0:T(8,128)(2,1)} %param.6) | copy-start | bytes 786436
  7.0 1.3 %collective-permute-start.1 = (bf16[64,1024]{1,0:T(8,128)(2,1)S(1)}, bf16[64,1024]{1,0:T(8,128)(2,1)S(1)}, u32[]{:S(2)}, u32[]{:S(2)}) collective-permute-start(bf16[64,1024]{1,0:T(8,128)(2,1)S(1)} %get-tuple-element.25), channel_id=1, source_target_pairs={{0,1},{1,0},{2,3},{3,2},{4,5},{5,4},{6,7},{7,6},{8,9},{9,8},{10,11... | collective-permute-start | bytes 393224 | tf_op jit(solution)/shard_map/ppermute | solution.py:26
  7.0 9.7 %collective-permute-start.10 = (bf16[64,1024]{1,0:T(8,128)(2,1)S(1)}, bf16[64,1024]{1,0:T(8,128)(2,1)S(1)}, u32[]{:S(2)}, u32[]{:S(2)}) collective-permute-start(bf16[64,1024]{1,0:T(8,128)(2,1)S(1)} %get-tuple-element.29), channel_id=1, source_target_pairs={{0,2},{1,3},{2,0},{3,1},{4,6},{5,7},{6,4},{7,5},{8,10},{9,11},{10,... | collective-permute-start | bytes 393224 | tf_op jit(solution)/shard_map/ppermute | solution.py:26
  13.4 11.2 %collective-permute-start.2 = (bf16[64,3072]{1,0:T(8,128)(2,1)S(1)}, bf16[64,3072]{1,0:T(8,128)(2,1)S(1)}, u32[]{:S(2)}, u32[]{:S(2)}) collective-permute-start(bf16[64,3072]{1,0:T(8,128)(2,1)S(1)} %collective-permute-done.refs_2_), channel_id=1, source_target_pairs={{0,4},{1,5},{2,6},{3,7},{4,12},{5,13},{6,14},{7,15},{8,0},{9,1},{1... | collective-permute-start | bytes 1179656 | tf_op jit(solution)/shard_map/ppermute | solution.py:293
  14.3 10.3 %collective-permute-start.4 = (bf16[64,3072]{1,0:T(8,128)(2,1)S(1)}, bf16[64,3072]{1,0:T(8,128)(2,1)S(1)}, u32[]{:S(2)}, u32[]{:S(2)}) collective-permute-start(bf16[64,3072]{1,0:T(8,128)(2,1)S(1)} %collective-permute-done.refs_2_), channel_id=1, source_target_pairs={{0,1},{1,0},{2,3},{3,2},{4,5},{5,4},{6,7},{7,6},{8,9},{9,8},{10,11... | collective-permute-start | bytes 1179656 | tf_op jit(solution)/shard_map/ppermute | solution.py:26
  15.2 9.4 %collective-permute-start.9 = (bf16[64,3072]{1,0:T(8,128)(2,1)S(1)}, bf16[64,3072]{1,0:T(8,128)(2,1)S(1)}, u32[]{:S(2)}, u32[]{:S(2)}) collective-permute-start(bf16[64,3072]{1,0:T(8,128)(2,1)S(1)} %collective-permute-done.8.refs_8_), channel_id=1, source_target_pairs={{0,1},{1,0},{2,3},{3,2},{4,5},{5,4},{6,7},{7,6},{8,9},{9,8},{10,11... | collective-permute-start | bytes 1179656 | tf_op jit(solution)/shard_map/ppermute | solution.py:26
  16.6 11.3 %collective-permute-start.11 = (bf16[64,3072]{1,0:T(8,128)(2,1)S(1)}, bf16[64,3072]{1,0:T(8,128)(2,1)S(1)}, u32[]{:S(2)}, u32[]{:S(2)}) collective-permute-start(bf16[64,3072]{1,0:T(8,128)(2,1)S(1)} %collective-permute-done.refs_2_), channel_id=1, source_target_pairs={{0,2},{1,3},{2,0},{3,1},{4,6},{5,7},{6,4},{7,5},{8,10},{9,11},{10,... | collective-permute-start | bytes 1179656 | tf_op jit(solution)/shard_map/ppermute | solution.py:26
  24.6 10.6 %collective-permute-start.13 = (bf16[64,3072]{1,0:T(8,128)(2,1)S(1)}, bf16[64,3072]{1,0:T(8,128)(2,1)S(1)}, u32[]{:S(2)}, u32[]{:S(2)}) collective-permute-start(bf16[64,3072]{1,0:T(8,128)(2,1)S(1)} %collective-permute-done.2.refs_6_), channel_id=1, source_target_pairs={{0,2},{1,3},{2,0},{3,1},{4,6},{5,7},{6,4},{7,5},{8,10},{9,11},{10,... | collective-permute-start | bytes 1179656 | tf_op jit(solution)/shard_map/ppermute | solution.py:26
  25.8 9.4 %collective-permute-start.5 = (bf16[64,3072]{1,0:T(8,128)(2,1)}, bf16[64,3072]{1,0:T(8,128)(2,1)S(1)}, u32[]{:S(2)}, u32[]{:S(2)}) collective-permute-start(bf16[64,3072]{1,0:T(8,128)(2,1)} %bitcast.16), channel_id=1, source_target_pairs={{4,0},{5,1},{6,2},{7,3},{12,4},{13,5},{14,6},{15,7},{0,8},{1,9},{2... | collective-permute-start | bytes 1179656 | tf_op jit(solution)/shard_map/ppermute | solution.py:296
  27.3 8.4 %collective-permute-start.7 = (bf16[64,3072]{1,0:T(8,128)(2,1)S(1)}, bf16[64,3072]{1,0:T(8,128)(2,1)S(1)}, u32[]{:S(2)}, u32[]{:S(2)}) collective-permute-start(bf16[64,3072]{1,0:T(8,128)(2,1)S(1)} %collective-permute-done.2.refs_6_), channel_id=1, source_target_pairs={{0,1},{1,0},{2,3},{3,2},{4,5},{5,4},{6,7},{7,6},{8,9},{9,8},{10,11... | collective-permute-start | bytes 1179656 | tf_op jit(solution)/shard_map/ppermute | solution.py:26
  27.9 7.8 %collective-permute-start.12 = (bf16[64,3072]{1,0:T(8,128)(2,1)S(1)}, bf16[64,3072]{1,0:T(8,128)(2,1)S(1)}, u32[]{:S(2)}, u32[]{:S(2)}) collective-permute-start(bf16[64,3072]{1,0:T(8,128)(2,1)S(1)} %collective-permute-done.11.refs_10_), channel_id=1, source_target_pairs={{0,1},{1,0},{2,3},{3,2},{4,5},{5,4},{6,7},{7,6},{8,9},{9,8},{10,11... | collective-permute-start | bytes 1179656 | tf_op jit(solution)/shard_map/ppermute | solution.py:26
  27.9 10.6 %collective-permute-start.3 = (bf16[64,3072]{1,0:T(8,128)(2,1)}, bf16[64,3072]{1,0:T(8,128)(2,1)S(1)}, u32[]{:S(2)}, u32[]{:S(2)}) collective-permute-start(bf16[64,3072]{1,0:T(8,128)(2,1)} %bitcast.17), channel_id=1, source_target_pairs={{0,1},{1,0},{2,3},{3,2},{4,5},{5,4},{6,7},{7,6},{8,9},{9,8},{10,11... | collective-permute-start | bytes 1179656 | tf_op jit(solution)/shard_map/ppermute | solution.py:26
  35.2 5.1 %collective-permute-start.14 = (bf16[64,3072]{1,0:T(8,128)(2,1)S(1)}, bf16[64,3072]{1,0:T(8,128)(2,1)S(1)}, u32[]{:S(2)}, u32[]{:S(2)}) collective-permute-start(bf16[64,3072]{1,0:T(8,128)(2,1)S(1)} %collective-permute-done.13.refs_12_), channel_id=1, source_target_pairs={{0,1},{1,0},{2,3},{3,2},{4,5},{5,4},{6,7},{7,6},{8,9},{9,8},{10,11... | collective-permute-start | bytes 1179656 | tf_op jit(solution)/shard_map/ppermute | solution.py:26
  35.2 5.1 %collective-permute-start.6 = (bf16[64,3072]{1,0:T(8,128)(2,1)S(1)}, bf16[64,3072]{1,0:T(8,128)(2,1)S(1)}, u32[]{:S(2)}, u32[]{:S(2)}) collective-permute-start(bf16[64,3072]{1,0:T(8,128)(2,1)S(1)} %collective-permute-done.5.refs_4_), channel_id=1, source_target_pairs={{0,1},{1,0},{2,3},{3,2},{4,5},{5,4},{6,7},{7,6},{8,9},{9,8},{10,11... | collective-permute-start | bytes 1179656 | tf_op jit(solution)/shard_map/ppermute | solution.py:26
  35.7 11.1 %collective-permute-start.17 = (bf16[64,3072]{1,0:T(8,128)(2,1)S(1)}, bf16[64,3072]{1,0:T(8,128)(2,1)S(1)}, u32[]{:S(2)}, u32[]{:S(2)}) collective-permute-start(bf16[64,3072]{1,0:T(8,128)(2,1)S(1)} %collective-permute-done.5.refs_4_), channel_id=1, source_target_pairs={{0,2},{1,3},{2,0},{3,1},{4,6},{5,7},{6,4},{7,5},{8,10},{9,11},{10,... | collective-permute-start | bytes 1179656 | tf_op jit(solution)/shard_map/ppermute | solution.py:26
  37.2 8.6 %collective-permute-start.16 = (bf16[64,1024]{1,0:T(8,128)(2,1)S(1)}, bf16[64,1024]{1,0:T(8,128)(2,1)S(1)}, u32[]{:S(2)}, u32[]{:S(2)}) collective-permute-start(bf16[64,1024]{1,0:T(8,128)(2,1)S(1)} %get-tuple-element.35), channel_id=1, source_target_pairs={{0,8},{1,9},{2,10},{3,11},{4,12},{5,13},{6,14},{7,15},{8,0},{9,1},... | collective-permute-start | bytes 393224 | tf_op jit(solution)/shard_map/ppermute | solution.py:26
  38.6 5.7 %copy-start.2 = (bf16[1,128,1024]{2,1,0:T(8,128)(2,1)S(1)}, bf16[1,128,1024]{2,1,0:T(8,128)(2,1)}, u32[]{:S(2)}) copy-start(bf16[1,128,1024]{2,1,0:T(8,128)(2,1)} %param.6) | copy-start | bytes 786436
  38.6 7.5 %collective-permute-start.15 = (bf16[64,1024]{1,0:T(8,128)(2,1)S(1)}, bf16[64,1024]{1,0:T(8,128)(2,1)S(1)}, u32[]{:S(2)}, u32[]{:S(2)}) collective-permute-start(bf16[64,1024]{1,0:T(8,128)(2,1)S(1)} %get-tuple-element.33), channel_id=1, source_target_pairs={{0,4},{1,5},{2,6},{3,7},{4,0},{5,1},{6,2},{7,3},{8,12},{9,13},{10,... | collective-permute-start | bytes 393224 | tf_op jit(solution)/shard_map/ppermute | solution.py:26
  40.2 1.0 %copy-start.4 = (bf16[1,64,3072]{2,1,0:T(8,128)(2,1)S(1)}, bf16[1,64,3072]{2,1,0:T(8,128)(2,1)}, u32[]{:S(2)}) copy-start(bf16[1,64,3072]{2,1,0:T(8,128)(2,1)} %param.9) | copy-start | bytes 1179652
  41.2 3.0 %copy-start.6 = (f32[1,1024]{1,0:T(1,128)S(1)}, f32[1,1024]{1,0:T(1,128)}, u32[]{:S(2)}) copy-start(f32[1,1024]{1,0:T(1,128)} %refs_4_.5) | copy-start | bytes 12292
  45.3 3.2 %copy-start.3 = (bf16[1,1024,1024]{2,1,0:T(8,128)(2,1)S(1)}, bf16[1,1024,1024]{2,1,0:T(8,128)(2,1)}, u32[]{:S(2)}) copy-start(bf16[1,1024,1024]{2,1,0:T(8,128)(2,1)} %param.10) | copy-start | bytes 6291460
  46.8 1.7 %collective-permute-start.18 = (bf16[64,3072]{1,0:T(8,128)(2,1)S(1)}, bf16[64,3072]{1,0:T(8,128)(2,1)S(1)}, u32[]{:S(2)}, u32[]{:S(2)}) collective-permute-start(bf16[64,3072]{1,0:T(8,128)(2,1)S(1)} %collective-permute-done.17.refs_6_), channel_id=1, source_target_pairs={{0,1},{1,0},{2,3},{3,2},{4,5},{5,4},{6,7},{7,6},{8,9},{9,8},{10,11... | collective-permute-start | bytes 1179656 | tf_op jit(solution)/shard_map/ppermute | solution.py:26
  48.5 11.7 %copy-start.5 = (bf16[128,1024]{1,0:T(8,128)(2,1)S(1)}, bf16[128,1024]{1,0:T(8,128)(2,1)}, u32[]{:S(2)}) copy-start(bf16[128,1024]{1,0:T(8,128)(2,1)} %arriving_ref.1) | copy-start | bytes 786436
  50.8 9.3 %collective-permute-start.19 = (bf16[128,1024]{1,0:T(8,128)(2,1)S(1)}, bf16[128,1024]{1,0:T(8,128)(2,1)S(1)}, u32[]{:S(2)}, u32[]{:S(2)}) collective-permute-start(bf16[128,1024]{1,0:T(8,128)(2,1)S(1)} %shard_map.68.refs_8_), channel_id=1, source_target_pairs={{0,16},{1,17},{2,18},{3,19},{4,20},{5,21},{6,22},{7,23},{8,24},{9,... | collective-permute-start | bytes 786440 | tf_op jit(solution)/shard_map/ppermute | solution.py:32
  60.4 2.4 %collective-permute-start.20 = (bf16[64,1024]{1,0:T(8,128)(2,1)S(1)}, bf16[64,1024]{1,0:T(8,128)(2,1)S(1)}, u32[]{:S(2)}, u32[]{:S(2)}) collective-permute-start(bf16[64,1024]{1,0:T(8,128)(2,1)S(1)} %get-tuple-element.39), channel_id=1, source_target_pairs={{0,1},{1,0},{2,3},{3,2},{4,5},{5,4},{6,7},{7,6},{8,9},{9,8},{10,11... | collective-permute-start | bytes 393224 | tf_op jit(solution)/shard_map/ppermute | solution.py:26
  60.5 9.6 %collective-permute-start.23 = (bf16[64,1024]{1,0:T(8,128)(2,1)S(1)}, bf16[64,1024]{1,0:T(8,128)(2,1)S(1)}, u32[]{:S(2)}, u32[]{:S(2)}) collective-permute-start(bf16[64,1024]{1,0:T(8,128)(2,1)S(1)} %get-tuple-element.44), channel_id=1, source_target_pairs={{0,8},{1,9},{2,10},{3,11},{4,12},{5,13},{6,14},{7,15},{8,0},{9,1},... | collective-permute-start | bytes 393224 | tf_op jit(solution)/shard_map/ppermute | solution.py:26
  62.8 7.3 %collective-permute-start.22 = (bf16[64,1024]{1,0:T(8,128)(2,1)S(1)}, bf16[64,1024]{1,0:T(8,128)(2,1)S(1)}, u32[]{:S(2)}, u32[]{:S(2)}) collective-permute-start(bf16[64,1024]{1,0:T(8,128)(2,1)S(1)} %get-tuple-element.43), channel_id=1, source_target_pairs={{0,4},{1,5},{2,6},{3,7},{4,0},{5,1},{6,2},{7,3},{8,12},{9,13},{10,... | collective-permute-start | bytes 393224 | tf_op jit(solution)/shard_map/ppermute | solution.py:26
  64.4 5.7 %collective-permute-start.21 = (bf16[64,1024]{1,0:T(8,128)(2,1)S(1)}, bf16[64,1024]{1,0:T(8,128)(2,1)S(1)}, u32[]{:S(2)}, u32[]{:S(2)}) collective-permute-start(bf16[64,1024]{1,0:T(8,128)(2,1)S(1)} %get-tuple-element.41), channel_id=1, source_target_pairs={{0,2},{1,3},{2,0},{3,1},{4,6},{5,7},{6,4},{7,5},{8,10},{9,11},{10,... | collective-permute-start | bytes 393224 | tf_op jit(solution)/shard_map/ppermute | solution.py:26

commit v7 on v6

--- a/solution.py
+++ b/solution.py
@@ -12,7 +12,7 @@
 HEAD = 128
 BLOCK = 64
 LEVELS = 4
-WIDE = 256
+WIDE = 512
 MIB = 1024 * 1024
 
 epsilon = 1e-06

time: 74 us -> 74 us (level)
  no operation moved by 1% of the time
where the time goes in v7:
time: 74 us; the launch traced here: 73.8 us
  waiting for transfers between devices  32.4 us (44%)
  starting transfers between devices  24.7 us (33%)
  Pallas kernels  13.8 us (19%)
  local copies, waits for them, and re-layouts  2.7 us (4%)
    ppermute x20, starting transfers between devices, swapped(): lax.ppermute(x, axis, [(i, i ^ mask) for i in range(lax.axis_size(axis))])  15.8 us
    ppermute x20, waiting for transfers between devices, swapped(): lax.ppermute(x, axis, [(i, i ^ mask) for i in range(lax.axis_size(axis))])  15 us
    ppermute x2, waiting for transfers between devices, around(): lax.ppermute(x, 'seq', [(i, onward[i // 4] * 4 + i % 4) for i in range(16)])  11.5 us
    ppermute x1, waiting for transfers between devices, from_behind(): return lax.ppermute(block, axis, route)  5.9 us
    ppermute x2, starting transfers between devices, around(): lax.ppermute(x, 'seq', [(i, onward[i // 4] * 4 + i % 4) for i in range(16)])  3.97 us
    pallas_call x3, Pallas kernels, ahead(): pl.pallas_call(functools.partial(ahead_kernel, first_column), out_shape=p...  3.95 us
    pallas_call x1, Pallas kernels, second_layer(): pl.pallas_call(functools.partial(second_kernel, len(latest)), out_shape=j...  3.68 us
    ppermute x1, starting transfers between devices, from_behind(): return lax.ppermute(block, axis, route)  3.44 us
  transfers between devices with their start and end apart: 24, of which 13 were waited for; matrix products, arithmetic and copies ran while one was open for 1% of the time, Pallas kernels for 10%

profile of v7, /device:TPU:0, one launch (start us, length us, event | category | flops | bytes accessed | tf_op | source)
XLA Modules:
  0.0 73.8 jit_solution(5621935578808173576)
XLA Ops:
  0.0 3.0 %collective-permute-start = (bf16[64,3072]{1,0:T(8,128)(2,1)}, bf16[64,3072]{1,0:T(8,128)(2,1)S(1)}, u32[]{:S(2)}, u32[]{:S(2)}) collective-permute-start(bf16[64,3072]{1,0:T(8,128)(2,1)} %bitcast.14), channel_id=1, source_target_pairs={{0,4},{1,5},{2,6},{3,7},{4,12},{5,13},{6,14},{7,15},{8,0},{9,1},{1... | collective-permute-start | bytes 1179656 | tf_op jit(solution)/shard_map/ppermute | solution.py:293
  3.0 1.5 %collective-permute-start.8 = (bf16[64,3072]{1,0:T(8,128)(2,1)}, bf16[64,3072]{1,0:T(8,128)(2,1)S(1)}, u32[]{:S(2)}, u32[]{:S(2)}) collective-permute-start(bf16[64,3072]{1,0:T(8,128)(2,1)} %bitcast.15), channel_id=1, source_target_pairs={{0,2},{1,3},{2,0},{3,1},{4,6},{5,7},{6,4},{7,5},{8,10},{9,11},{10,... | collective-permute-start | bytes 1179656 | tf_op jit(solution)/shard_map/ppermute | solution.py:26
  4.5 0.7 gather_fusion
  5.3 1.0 %copy-done.1 = bf16[1,128,1024]{2,1,0:T(8,128)(2,1)S(1)} copy-done((bf16[1,128,1024]{2,1,0:T(8,128)(2,1)S(1)}, bf16[1,128,1024]{2,1,0:T(8,128)(2,1)}, u32[]{:S(2)}) %copy-start.1) | copy-done | bytes 262168
  6.2 0.7 %shard_map.64 = (bf16[128,1024]{1,0:T(8,128)(2,1)}, bf16[64,1024]{1,0:T(8,128)(2,1)S(1)}, bf16[64,1024]{1,0:T(8,128)(2,1)S(1)}, bf16[64,1024]{1,0:T(8,128)(2,1)S(1)}, bf16[64,1024]{1,0:T(8,128)(2,1)S(1)}) custom-call(s32[8,128]{1,0:T(8,128)S(1)} %broadcast_in_dim.4.wanted, bf16[128,1024]{1,0:T(8,128)(2,1)S(1)} %bitcast.8, bf16[128,1024]{1,0:T(8,128)(2,1)S(1)} %bitcast.9), custom_call_target="tpu_custom_call" | custom-call | tf_op jit(solution)/shard_map/pallas_call | solution.py:73
  7.5 0.8 %collective-permute-done.1.refs_0_ = bf16[64,1024]{1,0:T(8,128)(2,1)S(1)} collective-permute-done((bf16[64,1024]{1,0:T(8,128)(2,1)S(1)}, bf16[64,1024]{1,0:T(8,128)(2,1)S(1)}, u32[]{:S(2)}, u32[]{:S(2)}) %collective-permute-start.1) | collective-permute-done | bytes 131104 | tf_op jit(solution)/shard_map/ppermute | solution.py:26
  8.3 5.0 %collective-permute-done.refs_2_ = bf16[64,3072]{1,0:T(8,128)(2,1)S(1)} collective-permute-done((bf16[64,3072]{1,0:T(8,128)(2,1)}, bf16[64,3072]{1,0:T(8,128)(2,1)S(1)}, u32[]{:S(2)}, u32[]{:S(2)}) %collective-permute-start) | collective-permute-done | bytes 393248 | tf_op jit(solution)/shard_map/ppermute | solution.py:293
  13.4 0.9 %collective-permute-start.2 = (bf16[64,3072]{1,0:T(8,128)(2,1)S(1)}, bf16[64,3072]{1,0:T(8,128)(2,1)S(1)}, u32[]{:S(2)}, u32[]{:S(2)}) collective-permute-start(bf16[64,3072]{1,0:T(8,128)(2,1)S(1)} %collective-permute-done.refs_2_), channel_id=1, source_target_pairs={{0,4},{1,5},{2,6},{3,7},{4,12},{5,13},{6,14},{7,15},{8,0},{9,1},{1... | collective-permute-start | bytes 1179656 | tf_op jit(solution)/shard_map/ppermute | solution.py:293
  14.3 0.9 %collective-permute-done.8.refs_8_ = bf16[64,3072]{1,0:T(8,128)(2,1)S(1)} collective-permute-done((bf16[64,3072]{1,0:T(8,128)(2,1)}, bf16[64,3072]{1,0:T(8,128)(2,1)S(1)}, u32[]{:S(2)}, u32[]{:S(2)}) %collective-permute-start.8) | collective-permute-done | bytes 393248 | tf_op jit(solution)/shard_map/ppermute | solution.py:26
  15.2 1.4 %collective-permute-done.10.refs_1_ = bf16[64,1024]{1,0:T(8,128)(2,1)S(1)} collective-permute-done((bf16[64,1024]{1,0:T(8,128)(2,1)S(1)}, bf16[64,1024]{1,0:T(8,128)(2,1)S(1)}, u32[]{:S(2)}, u32[]{:S(2)}) %collective-permute-start.10) | collective-permute-done | bytes 131104 | tf_op jit(solution)/shard_map/ppermute | solution.py:26
  16.6 1.5 %collective-permute-start.11 = (bf16[64,3072]{1,0:T(8,128)(2,1)S(1)}, bf16[64,3072]{1,0:T(8,128)(2,1)S(1)}, u32[]{:S(2)}, u32[]{:S(2)}) collective-permute-start(bf16[64,3072]{1,0:T(8,128)(2,1)S(1)} %collective-permute-done.refs_2_), channel_id=1, source_target_pairs={{0,2},{1,3},{2,0},{3,1},{4,6},{5,7},{6,4},{7,5},{8,10},{9,11},{10,... | collective-permute-start | bytes 1179656 | tf_op jit(solution)/shard_map/ppermute | solution.py:26
  18.1 6.4 %collective-permute-done.2.refs_6_ = bf16[64,3072]{1,0:T(8,128)(2,1)S(1)} collective-permute-done((bf16[64,3072]{1,0:T(8,128)(2,1)S(1)}, bf16[64,3072]{1,0:T(8,128)(2,1)S(1)}, u32[]{:S(2)}, u32[]{:S(2)}) %collective-permute-start.2) | collective-permute-done | bytes 393248 | tf_op jit(solution)/shard_map/ppermute | solution.py:293
  24.6 1.2 %collective-permute-start.13 = (bf16[64,3072]{1,0:T(8,128)(2,1)S(1)}, bf16[64,3072]{1,0:T(8,128)(2,1)S(1)}, u32[]{:S(2)}, u32[]{:S(2)}) collective-permute-start(bf16[64,3072]{1,0:T(8,128)(2,1)S(1)} %collective-permute-done.2.refs_6_), channel_id=1, source_target_pairs={{0,2},{1,3},{2,0},{3,1},{4,6},{5,7},{6,4},{7,5},{8,10},{9,11},{10,... | collective-permute-start | bytes 1179656 | tf_op jit(solution)/shard_map/ppermute | solution.py:26
  25.8 1.5 %collective-permute-start.5 = (bf16[64,3072]{1,0:T(8,128)(2,1)}, bf16[64,3072]{1,0:T(8,128)(2,1)S(1)}, u32[]{:S(2)}, u32[]{:S(2)}) collective-permute-start(bf16[64,3072]{1,0:T(8,128)(2,1)} %bitcast.16), channel_id=1, source_target_pairs={{4,0},{5,1},{6,2},{7,3},{12,4},{13,5},{14,6},{15,7},{0,8},{1,9},{2... | collective-permute-start | bytes 1179656 | tf_op jit(solution)/shard_map/ppermute | solution.py:296
  28.4 6.8 %collective-permute-done.13.refs_12_ = bf16[64,3072]{1,0:T(8,128)(2,1)S(1)} collective-permute-done((bf16[64,3072]{1,0:T(8,128)(2,1)S(1)}, bf16[64,3072]{1,0:T(8,128)(2,1)S(1)}, u32[]{:S(2)}, u32[]{:S(2)}) %collective-permute-start.13) | collective-permute-done | bytes 393248 | tf_op jit(solution)/shard_map/ppermute | solution.py:26
  35.7 1.5 %collective-permute-start.17 = (bf16[64,3072]{1,0:T(8,128)(2,1)S(1)}, bf16[64,3072]{1,0:T(8,128)(2,1)S(1)}, u32[]{:S(2)}, u32[]{:S(2)}) collective-permute-start(bf16[64,3072]{1,0:T(8,128)(2,1)S(1)} %collective-permute-done.5.refs_4_), channel_id=1, source_target_pairs={{0,2},{1,3},{2,0},{3,1},{4,6},{5,7},{6,4},{7,5},{8,10},{9,11},{10,... | collective-permute-start | bytes 1179656 | tf_op jit(solution)/shard_map/ppermute | solution.py:26
  37.2 1.4 %collective-permute-start.16 = (bf16[64,1024]{1,0:T(8,128)(2,1)S(1)}, bf16[64,1024]{1,0:T(8,128)(2,1)S(1)}, u32[]{:S(2)}, u32[]{:S(2)}) collective-permute-start(bf16[64,1024]{1,0:T(8,128)(2,1)S(1)} %get-tuple-element.35), channel_id=1, source_target_pairs={{0,8},{1,9},{2,10},{3,11},{4,12},{5,13},{6,14},{7,15},{8,0},{9,1},... | collective-permute-start | bytes 393224 | tf_op jit(solution)/shard_map/ppermute | solution.py:26
  38.6 1.7 %collective-permute-start.15 = (bf16[64,1024]{1,0:T(8,128)(2,1)S(1)}, bf16[64,1024]{1,0:T(8,128)(2,1)S(1)}, u32[]{:S(2)}, u32[]{:S(2)}) collective-permute-start(bf16[64,1024]{1,0:T(8,128)(2,1)S(1)} %get-tuple-element.33), channel_id=1, source_target_pairs={{0,4},{1,5},{2,6},{3,7},{4,0},{5,1},{6,2},{7,3},{8,12},{9,13},{10,... | collective-permute-start | bytes 393224 | tf_op jit(solution)/shard_map/ppermute | solution.py:26
  40.2 1.0 %copy-done.4 = bf16[1,64,3072]{2,1,0:T(8,128)(2,1)S(1)} copy-done((bf16[1,64,3072]{2,1,0:T(8,128)(2,1)S(1)}, bf16[1,64,3072]{2,1,0:T(8,128)(2,1)}, u32[]{:S(2)}) %copy-start.4) | copy-done | bytes 393240
  41.2 3.0 %shard_map.65.triple = bf16[1024,3072]{1,0:T(8,128)(2,1)S(1)} custom-call(bf16[64,3072]{1,0:T(8,128)(2,1)S(1)} %bitcast.18, bf16[64,3072]{1,0:T(8,128)(2,1)S(1)} %collective-permute-done.3.refs_1_, bf16[64,3072]{1,0:T(8,128)(2,1)S(1)} %collective-permute-done.refs_2_, bf16[64,3072]{1,0:T(8,128)(2,1)S(1)} %collective-permute-done.4.refs_3_, ...), custom_call_target="tpu_custom_call" | custom-call | bytes 12000000 | tf_op jit(solution)/shard_map/pallas_call | solution.py:107
  44.2 1.1 %shard_map.67.started = f32[128,3072]{1,0:T(8,128)S(1)} custom-call(bf16[1024,3072]{1,0:T(8,128)(2,1)S(1)} %shard_map.65.triple, bf16[128,1024]{1,0:T(8,128)(2,1)S(1)} %bitcast.10, f32[1,1024]{1,0:T(1,128)S(1)} %copy-done.6), custom_call_target="tpu_custom_call" | custom-call | flops 800000000 | bytes 8000000 | tf_op jit(solution)/shard_map/pallas_call | solution.py:136
  46.1 0.7 collective-permute-done.17.refs_6_
  46.8 1.4 %shard_map.66.far_started = f32[256,2048]{1,0:T(8,128)S(1)} custom-call(bf16[1024,3072]{1,0:T(8,128)(2,1)S(1)} %shard_map.65.triple, bf16[64,1024]{1,0:T(8,128)(2,1)S(1)} %collective-permute-done.1.refs_0_, bf16[64,1024]{1,0:T(8,128)(2,1)S(1)} %collective-permute-done.10.refs_1_, bf16[64,1024]{1,0:T(8,128)(2,1)S(1)} %collective-permute-done.15.refs_2_, ...), custom_call_target="tpu_custom_call" | custom-call | flops 800000000 | bytes 8000000 | tf_op jit(solution)/shard_map/pallas_call | solution.py:136
  48.5 2.3 %shard_map.68.refs_8_ = bf16[128,1024]{1,0:T(8,128)(2,1)S(1)} custom-call(f32[256,2048]{1,0:T(8,128)S(1)} %shard_map.66.far_started, bf16[128,1024]{1,0:T(8,128)(2,1)S(1)} %bitcast.11, f32[128,3072]{1,0:T(8,128)S(1)} %shard_map.67.started, bf16[64,1024]{1,0:T(8,128)(2,1)S(1)} %collective-permute-done.1.refs_0_, ...), custom_call_target="tpu_custom_call" | custom-call | flops 2400000000 | bytes 9000000 | tf_op jit(solution)/shard_map/pallas_call | solution.py:264
  50.8 3.4 %collective-permute-start.19 = (bf16[128,1024]{1,0:T(8,128)(2,1)S(1)}, bf16[128,1024]{1,0:T(8,128)(2,1)S(1)}, u32[]{:S(2)}, u32[]{:S(2)}) collective-permute-start(bf16[128,1024]{1,0:T(8,128)(2,1)S(1)} %shard_map.68.refs_8_), channel_id=1, source_target_pairs={{0,16},{1,17},{2,18},{3,19},{4,20},{5,21},{6,22},{7,23},{8,24},{9,... | collective-permute-start | bytes 786440 | tf_op jit(solution)/shard_map/ppermute | solution.py:32
  54.3 5.9 %collective-permute-done.19.moved_ref = bf16[128,1024]{1,0:T(8,128)(2,1)S(1)} collective-permute-done((bf16[128,1024]{1,0:T(8,128)(2,1)S(1)}, bf16[128,1024]{1,0:T(8,128)(2,1)S(1)}, u32[]{:S(2)}, u32[]{:S(2)}) %collective-permute-start.19) | collective-permute-done | bytes 262176 | tf_op jit(solution)/shard_map/ppermute | solution.py:32
  60.4 2.3 %collective-permute-start.23 = (bf16[64,1024]{1,0:T(8,128)(2,1)S(1)}, bf16[64,1024]{1,0:T(8,128)(2,1)S(1)}, u32[]{:S(2)}, u32[]{:S(2)}) collective-permute-start(bf16[64,1024]{1,0:T(8,128)(2,1)S(1)} %get-tuple-element.44), channel_id=1, source_target_pairs={{0,8},{1,9},{2,10},{3,11},{4,12},{5,13},{6,14},{7,15},{8,0},{9,1},... | collective-permute-start | bytes 393224 | tf_op jit(solution)/shard_map/ppermute | solution.py:26
  62.7 1.6 %collective-permute-start.22 = (bf16[64,1024]{1,0:T(8,128)(2,1)S(1)}, bf16[64,1024]{1,0:T(8,128)(2,1)S(1)}, u32[]{:S(2)}, u32[]{:S(2)}) collective-permute-start(bf16[64,1024]{1,0:T(8,128)(2,1)S(1)} %get-tuple-element.43), channel_id=1, source_target_pairs={{0,4},{1,5},{2,6},{3,7},{4,0},{5,1},{6,2},{7,3},{8,12},{9,13},{10,... | collective-permute-start | bytes 393224 | tf_op jit(solution)/shard_map/ppermute | solution.py:26
  64.4 1.5 %collective-permute-start.21 = (bf16[64,1024]{1,0:T(8,128)(2,1)S(1)}, bf16[64,1024]{1,0:T(8,128)(2,1)S(1)}, u32[]{:S(2)}, u32[]{:S(2)}) collective-permute-start(bf16[64,1024]{1,0:T(8,128)(2,1)S(1)} %get-tuple-element.41), channel_id=1, source_target_pairs={{0,2},{1,3},{2,0},{3,1},{4,6},{5,7},{6,4},{7,5},{8,10},{9,11},{10,... | collective-permute-start | bytes 393224 | tf_op jit(solution)/shard_map/ppermute | solution.py:26
  65.9 1.5 %shard_map.70.started = f32[192,3072]{1,0:T(8,128)S(1)} custom-call(bf16[1024,3072]{1,0:T(8,128)(2,1)S(1)} %shard_map.65.triple, bf16[128,1024]{1,0:T(8,128)(2,1)S(1)} %get-tuple-element.38.refs_0_.own_ref, bf16[64,1024]{1,0:T(8,128)(2,1)S(1)} %collective-permute-done.20.refs_1_.refs_0_, f32[1,1024]{1,0:T(1,128)S(1)} %copy-done.6), custom_call_target="tpu_custom_call" | custom-call | flops 800000000 | bytes 8000000 | tf_op jit(solution)/shard_map/pallas_call | solution.py:136
  67.4 2.7 %collective-permute-done.23.refs_3_ = bf16[64,1024]{1,0:T(8,128)(2,1)S(1)} collective-permute-done((bf16[64,1024]{1,0:T(8,128)(2,1)S(1)}, bf16[64,1024]{1,0:T(8,128)(2,1)S(1)}, u32[]{:S(2)}, u32[]{:S(2)}) %collective-permute-start.23) | collective-permute-done | bytes 131104 | tf_op jit(solution)/shard_map/ppermute | solution.py:26
  70.1 3.7 %shard_map.71 = bf16[2,128,1024]{2,1,0:T(8,128)(2,1)} custom-call(bf16[1024,3072]{1,0:T(8,128)(2,1)S(1)} %shard_map.65.triple, bf16[128,1024]{1,0:T(8,128)(2,1)S(1)} %get-tuple-element.38.refs_0_.own_ref, f32[192,3072]{1,0:T(8,128)S(1)} %shard_map.70.started, bf16[64,1024]{1,0:T(8,128)(2,1)S(1)} %collective-permute-done.20.refs_1_.refs_0_, ...), custom_call_target="tpu_custom_call" | custom-call | flops 2400000000 | bytes 9000000 | tf_op jit(solution)/shard_map/pallas_call | solution.py:276
  (41 shorter events, 3.7 us)
Async XLA Ops:
  0.0 4.5 %copy-start = (s32[16,4]{0,1:T(4,128)S(1)}, s32[16,4]{0,1:T(4,128)}, u32[]{:S(2)}) copy-start(s32[16,4]{0,1:T(4,128)} %param.11) | copy-start | bytes 772
  0.0 13.4 %collective-permute-start = (bf16[64,3072]{1,0:T(8,128)(2,1)}, bf16[64,3072]{1,0:T(8,128)(2,1)S(1)}, u32[]{:S(2)}, u32[]{:S(2)}) collective-permute-start(bf16[64,3072]{1,0:T(8,128)(2,1)} %bitcast.14), channel_id=1, source_target_pairs={{0,4},{1,5},{2,6},{3,7},{4,12},{5,13},{6,14},{7,15},{8,0},{9,1},{1... | collective-permute-start | bytes 1179656 | tf_op jit(solution)/shard_map/ppermute | solution.py:293
  3.0 12.2 %collective-permute-start.8 = (bf16[64,3072]{1,0:T(8,128)(2,1)}, bf16[64,3072]{1,0:T(8,128)(2,1)S(1)}, u32[]{:S(2)}, u32[]{:S(2)}) collective-permute-start(bf16[64,3072]{1,0:T(8,128)(2,1)} %bitcast.15), channel_id=1, source_target_pairs={{0,2},{1,3},{2,0},{3,1},{4,6},{5,7},{6,4},{7,5},{8,10},{9,11},{10,... | collective-permute-start | bytes 1179656 | tf_op jit(solution)/shard_map/ppermute | solution.py:26
  5.3 1.0 %copy-start.1 = (bf16[1,128,1024]{2,1,0:T(8,128)(2,1)S(1)}, bf16[1,128,1024]{2,1,0:T(8,128)(2,1)}, u32[]{:S(2)}) copy-start(bf16[1,128,1024]{2,1,0:T(8,128)(2,1)} %param.6) | copy-start | bytes 786436
  7.0 1.3 %collective-permute-start.1 = (bf16[64,1024]{1,0:T(8,128)(2,1)S(1)}, bf16[64,1024]{1,0:T(8,128)(2,1)S(1)}, u32[]{:S(2)}, u32[]{:S(2)}) collective-permute-start(bf16[64,1024]{1,0:T(8,128)(2,1)S(1)} %get-tuple-element.25), channel_id=1, source_target_pairs={{0,1},{1,0},{2,3},{3,2},{4,5},{5,4},{6,7},{7,6},{8,9},{9,8},{10,11... | collective-permute-start | bytes 393224 | tf_op jit(solution)/shard_map/ppermute | solution.py:26
  7.0 9.7 %collective-permute-start.10 = (bf16[64,1024]{1,0:T(8,128)(2,1)S(1)}, bf16[64,1024]{1,0:T(8,128)(2,1)S(1)}, u32[]{:S(2)}, u32[]{:S(2)}) collective-permute-start(bf16[64,1024]{1,0:T(8,128)(2,1)S(1)} %get-tuple-element.29), channel_id=1, source_target_pairs={{0,2},{1,3},{2,0},{3,1},{4,6},{5,7},{6,4},{7,5},{8,10},{9,11},{10,... | collective-permute-start | bytes 393224 | tf_op jit(solution)/shard_map/ppermute | solution.py:26
  13.4 11.2 %collective-permute-start.2 = (bf16[64,3072]{1,0:T(8,128)(2,1)S(1)}, bf16[64,3072]{1,0:T(8,128)(2,1)S(1)}, u32[]{:S(2)}, u32[]{:S(2)}) collective-permute-start(bf16[64,3072]{1,0:T(8,128)(2,1)S(1)} %collective-permute-done.refs_2_), channel_id=1, source_target_pairs={{0,4},{1,5},{2,6},{3,7},{4,12},{5,13},{6,14},{7,15},{8,0},{9,1},{1... | collective-permute-start | bytes 1179656 | tf_op jit(solution)/shard_map/ppermute | solution.py:293
  14.3 10.3 %collective-permute-start.4 = (bf16[64,3072]{1,0:T(8,128)(2,1)S(1)}, bf16[64,3072]{1,0:T(8,128)(2,1)S(1)}, u32[]{:S(2)}, u32[]{:S(2)}) collective-permute-start(bf16[64,3072]{1,0:T(8,128)(2,1)S(1)} %collective-permute-done.refs_2_), channel_id=1, source_target_pairs={{0,1},{1,0},{2,3},{3,2},{4,5},{5,4},{6,7},{7,6},{8,9},{9,8},{10,11... | collective-permute-start | bytes 1179656 | tf_op jit(solution)/shard_map/ppermute | solution.py:26
  15.2 9.4 %collective-permute-start.9 = (bf16[64,3072]{1,0:T(8,128)(2,1)S(1)}, bf16[64,3072]{1,0:T(8,128)(2,1)S(1)}, u32[]{:S(2)}, u32[]{:S(2)}) collective-permute-start(bf16[64,3072]{1,0:T(8,128)(2,1)S(1)} %collective-permute-done.8.refs_8_), channel_id=1, source_target_pairs={{0,1},{1,0},{2,3},{3,2},{4,5},{5,4},{6,7},{7,6},{8,9},{9,8},{10,11... | collective-permute-start | bytes 1179656 | tf_op jit(solution)/shard_map/ppermute | solution.py:26
  16.6 11.3 %collective-permute-start.11 = (bf16[64,3072]{1,0:T(8,128)(2,1)S(1)}, bf16[64,3072]{1,0:T(8,128)(2,1)S(1)}, u32[]{:S(2)}, u32[]{:S(2)}) collective-permute-start(bf16[64,3072]{1,0:T(8,128)(2,1)S(1)} %collective-permute-done.refs_2_), channel_id=1, source_target_pairs={{0,2},{1,3},{2,0},{3,1},{4,6},{5,7},{6,4},{7,5},{8,10},{9,11},{10,... | collective-permute-start | bytes 1179656 | tf_op jit(solution)/shard_map/ppermute | solution.py:26
  24.6 10.6 %collective-permute-start.13 = (bf16[64,3072]{1,0:T(8,128)(2,1)S(1)}, bf16[64,3072]{1,0:T(8,128)(2,1)S(1)}, u32[]{:S(2)}, u32[]{:S(2)}) collective-permute-start(bf16[64,3072]{1,0:T(8,128)(2,1)S(1)} %collective-permute-done.2.refs_6_), channel_id=1, source_target_pairs={{0,2},{1,3},{2,0},{3,1},{4,6},{5,7},{6,4},{7,5},{8,10},{9,11},{10,... | collective-permute-start | bytes 1179656 | tf_op jit(solution)/shard_map/ppermute | solution.py:26
  25.8 9.4 %collective-permute-start.5 = (bf16[64,3072]{1,0:T(8,128)(2,1)}, bf16[64,3072]{1,0:T(8,128)(2,1)S(1)}, u32[]{:S(2)}, u32[]{:S(2)}) collective-permute-start(bf16[64,3072]{1,0:T(8,128)(2,1)} %bitcast.16), channel_id=1, source_target_pairs={{4,0},{5,1},{6,2},{7,3},{12,4},{13,5},{14,6},{15,7},{0,8},{1,9},{2... | collective-permute-start | bytes 1179656 | tf_op jit(solution)/shard_map/ppermute | solution.py:296
  27.3 8.4 %collective-permute-start.7 = (bf16[64,3072]{1,0:T(8,128)(2,1)S(1)}, bf16[64,3072]{1,0:T(8,128)(2,1)S(1)}, u32[]{:S(2)}, u32[]{:S(2)}) collective-permute-start(bf16[64,3072]{1,0:T(8,128)(2,1)S(1)} %collective-permute-done.2.refs_6_), channel_id=1, source_target_pairs={{0,1},{1,0},{2,3},{3,2},{4,5},{5,4},{6,7},{7,6},{8,9},{9,8},{10,11... | collective-permute-start | bytes 1179656 | tf_op jit(solution)/shard_map/ppermute | solution.py:26
  27.9 7.8 %collective-permute-start.12 = (bf16[64,3072]{1,0:T(8,128)(2,1)S(1)}, bf16[64,3072]{1,0:T(8,128)(2,1)S(1)}, u32[]{:S(2)}, u32[]{:S(2)}) collective-permute-start(bf16[64,3072]{1,0:T(8,128)(2,1)S(1)} %collective-permute-done.11.refs_10_), channel_id=1, source_target_pairs={{0,1},{1,0},{2,3},{3,2},{4,5},{5,4},{6,7},{7,6},{8,9},{9,8},{10,11... | collective-permute-start | bytes 1179656 | tf_op jit(solution)/shard_map/ppermute | solution.py:26
  27.9 10.6 %collective-permute-start.3 = (bf16[64,3072]{1,0:T(8,128)(2,1)}, bf16[64,3072]{1,0:T(8,128)(2,1)S(1)}, u32[]{:S(2)}, u32[]{:S(2)}) collective-permute-start(bf16[64,3072]{1,0:T(8,128)(2,1)} %bitcast.17), channel_id=1, source_target_pairs={{0,1},{1,0},{2,3},{3,2},{4,5},{5,4},{6,7},{7,6},{8,9},{9,8},{10,11... | collective-permute-start | bytes 1179656 | tf_op jit(solution)/shard_map/ppermute | solution.py:26
  35.2 5.1 %collective-permute-start.14 = (bf16[64,3072]{1,0:T(8,128)(2,1)S(1)}, bf16[64,3072]{1,0:T(8,128)(2,1)S(1)}, u32[]{:S(2)}, u32[]{:S(2)}) collective-permute-start(bf16[64,3072]{1,0:T(8,128)(2,1)S(1)} %collective-permute-done.13.refs_12_), channel_id=1, source_target_pairs={{0,1},{1,0},{2,3},{3,2},{4,5},{5,4},{6,7},{7,6},{8,9},{9,8},{10,11... | collective-permute-start | bytes 1179656 | tf_op jit(solution)/shard_map/ppermute | solution.py:26
  35.2 5.1 %collective-permute-start.6 = (bf16[64,3072]{1,0:T(8,128)(2,1)S(1)}, bf16[64,3072]{1,0:T(8,128)(2,1)S(1)}, u32[]{:S(2)}, u32[]{:S(2)}) collective-permute-start(bf16[64,3072]{1,0:T(8,128)(2,1)S(1)} %collective-permute-done.5.refs_4_), channel_id=1, source_target_pairs={{0,1},{1,0},{2,3},{3,2},{4,5},{5,4},{6,7},{7,6},{8,9},{9,8},{10,11... | collective-permute-start | bytes 1179656 | tf_op jit(solution)/shard_map/ppermute | solution.py:26
  35.7 11.1 %collective-permute-start.17 = (bf16[64,3072]{1,0:T(8,128)(2,1)S(1)}, bf16[64,3072]{1,0:T(8,128)(2,1)S(1)}, u32[]{:S(2)}, u32[]{:S(2)}) collective-permute-start(bf16[64,3072]{1,0:T(8,128)(2,1)S(1)} %collective-permute-done.5.refs_4_), channel_id=1, source_target_pairs={{0,2},{1,3},{2,0},{3,1},{4,6},{5,7},{6,4},{7,5},{8,10},{9,11},{10,... | collective-permute-start | bytes 1179656 | tf_op jit(solution)/shard_map/ppermute | solution.py:26
  37.2 8.6 %collective-permute-start.16 = (bf16[64,1024]{1,0:T(8,128)(2,1)S(1)}, bf16[64,1024]{1,0:T(8,128)(2,1)S(1)}, u32[]{:S(2)}, u32[]{:S(2)}) collective-permute-start(bf16[64,1024]{1,0:T(8,128)(2,1)S(1)} %get-tuple-element.35), channel_id=1, source_target_pairs={{0,8},{1,9},{2,10},{3,11},{4,12},{5,13},{6,14},{7,15},{8,0},{9,1},... | collective-permute-start | bytes 393224 | tf_op jit(solution)/shard_map/ppermute | solution.py:26
  38.6 5.7 %copy-start.2 = (bf16[1,128,1024]{2,1,0:T(8,128)(2,1)S(1)}, bf16[1,128,1024]{2,1,0:T(8,128)(2,1)}, u32[]{:S(2)}) copy-start(bf16[1,128,1024]{2,1,0:T(8,128)(2,1)} %param.6) | copy-start | bytes 786436
  38.6 7.5 %collective-permute-start.15 = (bf16[64,1024]{1,0:T(8,128)(2,1)S(1)}, bf16[64,1024]{1,0:T(8,128)(2,1)S(1)}, u32[]{:S(2)}, u32[]{:S(2)}) collective-permute-start(bf16[64,1024]{1,0:T(8,128)(2,1)S(1)} %get-tuple-element.33), channel_id=1, source_target_pairs={{0,4},{1,5},{2,6},{3,7},{4,0},{5,1},{6,2},{7,3},{8,12},{9,13},{10,... | collective-permute-start | bytes 393224 | tf_op jit(solution)/shard_map/ppermute | solution.py:26
  40.2 1.0 %copy-start.4 = (bf16[1,64,3072]{2,1,0:T(8,128)(2,1)S(1)}, bf16[1,64,3072]{2,1,0:T(8,128)(2,1)}, u32[]{:S(2)}) copy-start(bf16[1,64,3072]{2,1,0:T(8,128)(2,1)} %param.9) | copy-start | bytes 1179652
  41.2 3.0 %copy-start.6 = (f32[1,1024]{1,0:T(1,128)S(1)}, f32[1,1024]{1,0:T(1,128)}, u32[]{:S(2)}) copy-start(f32[1,1024]{1,0:T(1,128)} %refs_4_.5) | copy-start | bytes 12292
  45.3 3.2 %copy-start.3 = (bf16[1,1024,1024]{2,1,0:T(8,128)(2,1)S(1)}, bf16[1,1024,1024]{2,1,0:T(8,128)(2,1)}, u32[]{:S(2)}) copy-start(bf16[1,1024,1024]{2,1,0:T(8,128)(2,1)} %param.10) | copy-start | bytes 6291460
  46.8 1.7 %collective-permute-start.18 = (bf16[64,3072]{1,0:T(8,128)(2,1)S(1)}, bf16[64,3072]{1,0:T(8,128)(2,1)S(1)}, u32[]{:S(2)}, u32[]{:S(2)}) collective-permute-start(bf16[64,3072]{1,0:T(8,128)(2,1)S(1)} %collective-permute-done.17.refs_6_), channel_id=1, source_target_pairs={{0,1},{1,0},{2,3},{3,2},{4,5},{5,4},{6,7},{7,6},{8,9},{9,8},{10,11... | collective-permute-start | bytes 1179656 | tf_op jit(solution)/shard_map/ppermute | solution.py:26
  48.5 11.6 %copy-start.5 = (bf16[128,1024]{1,0:T(8,128)(2,1)S(1)}, bf16[128,1024]{1,0:T(8,128)(2,1)}, u32[]{:S(2)}) copy-start(bf16[128,1024]{1,0:T(8,128)(2,1)} %arriving_ref.1) | copy-start | bytes 786436
  50.8 9.3 %collective-permute-start.19 = (bf16[128,1024]{1,0:T(8,128)(2,1)S(1)}, bf16[128,1024]{1,0:T(8,128)(2,1)S(1)}, u32[]{:S(2)}, u32[]{:S(2)}) collective-permute-start(bf16[128,1024]{1,0:T(8,128)(2,1)S(1)} %shard_map.68.refs_8_), channel_id=1, source_target_pairs={{0,16},{1,17},{2,18},{3,19},{4,20},{5,21},{6,22},{7,23},{8,24},{9,... | collective-permute-start | bytes 786440 | tf_op jit(solution)/shard_map/ppermute | solution.py:32
  60.4 2.4 %collective-permute-start.20 = (bf16[64,1024]{1,0:T(8,128)(2,1)S(1)}, bf16[64,1024]{1,0:T(8,128)(2,1)S(1)}, u32[]{:S(2)}, u32[]{:S(2)}) collective-permute-start(bf16[64,1024]{1,0:T(8,128)(2,1)S(1)} %get-tuple-element.39), channel_id=1, source_target_pairs={{0,1},{1,0},{2,3},{3,2},{4,5},{5,4},{6,7},{7,6},{8,9},{9,8},{10,11... | collective-permute-start | bytes 393224 | tf_op jit(solution)/shard_map/ppermute | solution.py:26
  60.4 9.6 %collective-permute-start.23 = (bf16[64,1024]{1,0:T(8,128)(2,1)S(1)}, bf16[64,1024]{1,0:T(8,128)(2,1)S(1)}, u32[]{:S(2)}, u32[]{:S(2)}) collective-permute-start(bf16[64,1024]{1,0:T(8,128)(2,1)S(1)} %get-tuple-element.44), channel_id=1, source_target_pairs={{0,8},{1,9},{2,10},{3,11},{4,12},{5,13},{6,14},{7,15},{8,0},{9,1},... | collective-permute-start | bytes 393224 | tf_op jit(solution)/shard_map/ppermute | solution.py:26
  62.7 7.3 %collective-permute-start.22 = (bf16[64,1024]{1,0:T(8,128)(2,1)S(1)}, bf16[64,1024]{1,0:T(8,128)(2,1)S(1)}, u32[]{:S(2)}, u32[]{:S(2)}) collective-permute-start(bf16[64,1024]{1,0:T(8,128)(2,1)S(1)} %get-tuple-element.43), channel_id=1, source_target_pairs={{0,4},{1,5},{2,6},{3,7},{4,0},{5,1},{6,2},{7,3},{8,12},{9,13},{10,... | collective-permute-start | bytes 393224 | tf_op jit(solution)/shard_map/ppermute | solution.py:26
  64.4 5.7 %collective-permute-start.21 = (bf16[64,1024]{1,0:T(8,128)(2,1)S(1)}, bf16[64,1024]{1,0:T(8,128)(2,1)S(1)}, u32[]{:S(2)}, u32[]{:S(2)}) collective-permute-start(bf16[64,1024]{1,0:T(8,128)(2,1)S(1)} %get-tuple-element.41), channel_id=1, source_target_pairs={{0,2},{1,3},{2,0},{3,1},{4,6},{5,7},{6,4},{7,5},{8,10},{9,11},{10,... | collective-permute-start | bytes 393224 | tf_op jit(solution)/shard_map/ppermute | solution.py:26
